TPU v7x, 256 devices: a whole 4x4x8 slice. The times are simulated.
256 devices in a mesh: row: 8 (over x, core), col: 32 (over z, y).
Axes of the slice: x: 4, y: 4, z: 8, core: 2. Of those that a mesh axis runs over, the one named last changes fastest.
Arguments:
- start_block: float32 [32, 256, 4096], P(None, 'row', 'col'), may hold values from -6 to 6
- sea_mask: int32 [256, 4096], P('row', 'col'), may hold values 0 or 1
- depth_levels: int32 [256, 4096], P('row', 'col'), may hold values from 1 to 50
Outputs:
- basis: float32 [128, 256, 4096], P(None, 'row', 'col')
- alphas: float32 [3, 32, 32], replicated
- betas: float32 [3, 32, 32], replicated
All inputs are finite; a program needn't handle non-finite values. No bound on the sum of `sea_mask` on one device may be relied on, other than what follows from the above.
Results may differ from a plain program's by a relative error of at most 0.00075.
Values sent between devices are 32-bit elements; how exact they have to be, the bound alone decides.
No kernel may reach another device: no remote copies, remote signals or barrier semaphores. Data moves between devices by JAX's collectives and lax.ppermute only.
A program may use at most 64 MiB of HBM per device.

v0:
```python
import jax
import jax.numpy as jnp
from jax import lax
from jax.sharding import PartitionSpec as P

ITERS = 3
LEVELS = 50


HIGH = lax.Precision.HIGHEST
KAPPA = 1.5


def extended(block, sides, width, periodic):
    for axis, dim in sides:
        count = lax.axis_size(axis)
        forward = [(i, i + 1) for i in range(count - 1)]
        if periodic:
            forward.append((count - 1, 0))
        backward = [(target, source) for source, target in forward]
        low = lax.ppermute(
            lax.slice_in_dim(block, block.shape[dim] - width, None, axis=dim), axis, forward
        )
        high = lax.ppermute(lax.slice_in_dim(block, 0, width, axis=dim), axis, backward)
        block = jnp.concatenate([low, block, high], axis=dim)
    return block


def widen(field):
    rimmed = extended(field, (("row", 1),), 1, False)
    return extended(rimmed, (("col", 2),), 1, True)


def inner(left, right, cells):
    return jnp.dot(left, right.T, precision=HIGH, preferred_element_type=jnp.float32) / cells


def lower_solve(lower, values):
    return jax.scipy.linalg.solve_triangular(lower, values, lower=True)


def finish(flat, gram):
    lower = jnp.linalg.cholesky(gram)
    return (lower_solve(lower, flat), lower.T)


def factorize(flat, cells):
    gram = lax.psum(inner(flat, flat, cells), ("row", "col"))
    return finish(flat, gram)


def body(start_block, sea_mask, depth_levels):
    blocks, lats, lons = start_block.shape
    cells = float(lats * lons * lax.axis_size("row") * lax.axis_size("col"))
    mask = sea_mask.astype(jnp.float32)
    depth = (mask * depth_levels.astype(jnp.float32) / LEVELS)[None]
    depth_wide = widen(depth)
    centre = depth_wide[:, 1:-1, 1:-1]
    weight_north = jnp.minimum(centre, depth_wide[:, :-2, 1:-1])
    weight_south = jnp.minimum(centre, depth_wide[:, 2:, 1:-1])
    weight_west = jnp.minimum(centre, depth_wide[:, 1:-1, :-2])
    weight_east = jnp.minimum(centre, depth_wide[:, 1:-1, 2:])
    flat = (mask[None] * start_block).reshape(blocks, lats * lons)
    alpha_list = []
    beta_list = []
    stacked, unused = factorize(flat, cells)
    for step in range(ITERS):
        current = stacked[step * blocks : (step + 1) * blocks]
        wide = widen(current.reshape(blocks, lats, lons))
        middle = wide[:, 1:-1, 1:-1]
        total = weight_north * (middle - wide[:, :-2, 1:-1]) + weight_south * (
            middle - wide[:, 2:, 1:-1]
        )
        total = (
            total
            + weight_west * (middle - wide[:, 1:-1, :-2])
            + weight_east * (middle - wide[:, 1:-1, 2:])
        )
        image = (mask[None] * middle + KAPPA * total).reshape(blocks, lats * lons)
        coeffs = lax.psum(inner(stacked, image, cells), ("row", "col"))
        image = image - jnp.dot(
            coeffs.T, stacked, precision=HIGH, preferred_element_type=jnp.float32
        )
        fresh, upper = factorize(image, cells)
        alpha_list.append(coeffs[step * blocks : (step + 1) * blocks])
        beta_list.append(upper)
        stacked = jnp.concatenate([stacked, fresh], axis=0)
    return (
        stacked.reshape((ITERS + 1) * blocks, lats, lons),
        jnp.stack(alpha_list),
        jnp.stack(beta_list),
    )


def solution(mesh):
    in_specs = (P(None, "row", "col"), P("row", "col"), P("row", "col"))
    out_specs = (P(None, "row", "col"), P(), P())
    return jax.shard_map(body, mesh=mesh, in_specs=in_specs, out_specs=out_specs, check_vma=False)
```

profile of v0, /device:TPU:8, one launch (start us, length us, event | category | flops | bytes accessed | tf_op | source)
XLA Modules:
  0.0 632.5 jit_solution(8549179668749599186)
XLA Ops:
  1.4 1.7 collective-permute-start
  3.1 1.3 collective-permute-start.2
  5.1 1.1 broadcast_multiply_fusion
  6.2 0.8 fusion
  7.1 80.9 %psum.49 = f32[32,32]{0,1:T(8,128)S(1)} all-reduce(f32[32,32]{0,1:T(8,128)S(1)} %fusion), channel_id=1, replica_groups=mesh['row'=8,'col'=32] {'row','col'}, use_global_device_ids=true, to_apply=%region_0.0 | all-reduce | flops 1024 | bytes 8192 | tf_op jit(solution)/shard_map/psum | solution.py:48
  88.0 2.9 cholesky.74
  92.3 2.4 custom-call.8
  94.7 0.9 fusion.4
  95.8 1.3 collective-permute-start.3
  97.1 3.0 collective-permute-start.1
  100.2 1.1 collective-permute-start.4
  101.3 0.9 collective-permute-start.6
  103.2 5.2 collective-permute-start.7
  108.5 3.6 collective-permute-done.5
  114.3 74.1 %psum.50 = f32[32,32]{0,1:T(8,128)S(1)} all-reduce(f32[32,32]{0,1:T(8,128)S(1)} %convolution_multiply_fusion.5), channel_id=1, replica_groups=mesh['row'=8,'col'=32] {'row','col'}, use_global_device_ids=true, to_apply=%region_3.0 | all-reduce | flops 1024 | bytes 8192 | tf_op jit(solution)/shard_map/psum | solution.py:80
  189.8 74.5 %psum.51 = f32[32,32]{0,1:T(8,128)S(1)} all-reduce(f32[32,32]{0,1:T(8,128)S(1)} %convolution_multiply_fusion.4), channel_id=1, replica_groups=mesh['row'=8,'col'=32] {'row','col'}, use_global_device_ids=true, to_apply=%region_4.0 | all-reduce | flops 1024 | bytes 8192 | tf_op jit(solution)/shard_map/psum | solution.py:48
  264.4 2.9 cholesky.85
  268.0 1.3 fusion.70
  269.3 2.4 custom-call.9
  272.5 1.3 collective-permute-start.9
  273.8 3.0 collective-permute-start.8
  276.9 0.8 collective-permute-done.8
  279.3 1.5 collective-permute-start.11
  280.8 1.4 collective-permute-done.10
  283.2 1.2 copy.338
  284.4 1.7 fusion.24
  286.1 1.1 convolution_multiply_fusion
  287.3 79.9 %psum.52 = f32[64,32]{0,1:T(8,128)S(1)} all-reduce(f32[64,32]{0,1:T(8,128)S(1)} %convolution_multiply_fusion), channel_id=1, replica_groups=mesh['row'=8,'col'=32] {'row','col'}, use_global_device_ids=true, to_apply=%region_5.0 | all-reduce | flops 2048 | bytes 16384 | tf_op jit(solution)/shard_map/psum | solution.py:80
  367.2 0.9 convolution_subtract_fusion.1
  368.6 73.4 %psum.53 = f32[32,32]{0,1:T(8,128)S(1)} all-reduce(f32[32,32]{0,1:T(8,128)S(1)} %convolution_multiply_fusion.3), channel_id=1, replica_groups=mesh['row'=8,'col'=32] {'row','col'}, use_global_device_ids=true, to_apply=%region_6.0 | all-reduce | flops 1024 | bytes 8192 | tf_op jit(solution)/shard_map/psum | solution.py:48
  442.1 2.9 cholesky.96
  445.7 1.2 fusion.71
  447.0 2.4 custom-call.10
  450.2 1.3 collective-permute-start.13
  451.5 3.0 collective-permute-start.12
  455.7 0.9 copy.347
  456.9 1.2 collective-permute-start.15
  458.1 1.1 collective-permute-start.14
  459.3 4.7 collective-permute-done.14
  464.3 1.2 copy.350
  465.5 1.7 fusion.11
  467.2 1.5 convolution_multiply_fusion.2
  468.7 76.6 %psum.54 = f32[96,32]{0,1:T(8,128)S(1)} all-reduce(f32[96,32]{0,1:T(8,128)S(1)} %convolution_multiply_fusion.2), channel_id=1, replica_groups=mesh['row'=8,'col'=32] {'row','col'}, use_global_device_ids=true, to_apply=%region_7.10 | all-reduce | flops 3072 | bytes 24576 | tf_op jit(solution)/shard_map/psum | solution.py:80
  545.3 1.1 convolution_subtract_fusion
  547.8 74.7 %psum.55 = f32[32,32]{0,1:T(8,128)S(1)} all-reduce(f32[32,32]{0,1:T(8,128)S(1)} %convolution_multiply_fusion.1), channel_id=1, replica_groups=mesh['row'=8,'col'=32] {'row','col'}, use_global_device_ids=true, to_apply=%region_8.11 | all-reduce | flops 1024 | bytes 8192 | tf_op jit(solution)/shard_map/psum | solution.py:48
  622.5 2.9 cholesky.107
  627.5 2.4 custom-call.11
  630.8 1.7 copy.368
  (79 shorter events, 20.2 us)
Async XLA Ops:
  1.4 98.7 %collective-permute-start = (f32[1,1,128]{2,1,0:T(1,128)S(1)}, f32[1,1,128]{2,1,0:T(1,128)S(1)}, u32[]{:S(2)}, u32[]{:S(2)}) collective-permute-start(f32[1,1,128]{2,1,0:T(1,128)S(1)} %get-tuple-element.50), channel_id=1, source_target_pairs={{0,32},{32,64},{64,96},{96,128},{128,160},{160,192},{192,224},{1,3... | collective-permute-start | bytes 1544 | tf_op jit(solution)/shard_map/ppermute | solution.py:21
  3.1 97.0 %collective-permute-start.2 = (f32[1,1,128]{2,1,0:T(1,128)S(1)}, f32[1,1,128]{2,1,0:T(1,128)S(1)}, u32[]{:S(2)}, u32[]{:S(2)}) collective-permute-start(f32[1,1,128]{2,1,0:T(1,128)S(1)} %get-tuple-element.51), channel_id=1, source_target_pairs={{32,0},{64,32},{96,64},{128,96},{160,128},{192,160},{224,192},{33,... | collective-permute-start | bytes 1544 | tf_op jit(solution)/shard_map/ppermute | solution.py:24
  95.8 6.5 %collective-permute-start.3 = (f32[32,1,128]{2,0,1:T(8,128)S(1)}, f32[32,1,128]{2,0,1:T(8,128)S(1)}, u32[]{:S(2)}, u32[]{:S(2)}) collective-permute-start(f32[32,1,128]{2,0,1:T(8,128)S(1)} %bitcast.161), channel_id=1, source_target_pairs={{32,0},{64,32},{96,64},{128,96},{160,128},{192,160},{224,192},{33,... | collective-permute-start | bytes 49160 | tf_op jit(solution)/shard_map/ppermute | solution.py:24
  97.1 5.2 collective-permute-start.1
  100.2 8.2 %collective-permute-start.4 = (f32[1,34,1]{2,1,0:T(8,128)S(1)}, f32[1,34,1]{2,1,0:T(8,128)S(1)}, u32[]{:S(2)}, u32[]{:S(2)}) collective-permute-start(f32[1,34,1]{2,1,0:T(8,128)S(1)} %get-tuple-element.38), channel_id=1, source_target_pairs={{0,1},{1,2},{2,3},{3,4},{4,5},{5,6},{6,7},{7,8},{8,9},{9,10},{10,1... | collective-permute-start | bytes 416 | tf_op jit(solution)/shard_map/ppermute | solution.py:21
  101.3 7.1 %collective-permute-start.6 = (f32[1,34,1]{2,1,0:T(8,128)S(1)}, f32[1,34,1]{2,1,0:T(8,128)S(1)}, u32[]{:S(2)}, u32[]{:S(2)}) collective-permute-start(f32[1,34,1]{2,1,0:T(8,128)S(1)} %get-tuple-element.39), channel_id=1, source_target_pairs={{1,0},{2,1},{3,2},{4,3},{5,4},{6,5},{7,6},{8,7},{9,8},{10,9},{11,1... | collective-permute-start | bytes 416 | tf_op jit(solution)/shard_map/ppermute | solution.py:24
  103.2 9.3 %collective-permute-start.7 = (f32[32,34,1]{1,0,2:T(8,128)S(1)}, f32[32,34,1]{1,0,2:T(8,128)S(1)}, u32[]{:S(2)}, u32[]{:S(2)}) collective-permute-start(f32[32,34,1]{1,0,2:T(8,128)S(1)} %copy.324), channel_id=1, source_target_pairs={{1,0},{2,1},{3,2},{4,3},{5,4},{6,5},{7,6},{8,7},{9,8},{10,9},{11,1... | collective-permute-start | bytes 13064 | tf_op jit(solution)/shard_map/ppermute | solution.py:24
  108.4 3.7 collective-permute-start.5
  272.5 4.3 collective-permute-start.9
  273.8 3.9 collective-permute-start.8
  278.3 3.8 collective-permute-start.10
  279.3 4.0 collective-permute-start.11
  450.2 4.3 collective-permute-start.13
  451.5 3.9 collective-permute-start.12
  456.9 7.4 %collective-permute-start.15 = (f32[32,34,1]{1,0,2:T(8,128)S(1)}, f32[32,34,1]{1,0,2:T(8,128)S(1)}, u32[]{:S(2)}, u32[]{:S(2)}) collective-permute-start(f32[32,34,1]{1,0,2:T(8,128)S(1)} %copy.349), channel_id=1, source_target_pairs={{1,0},{2,1},{3,2},{4,3},{5,4},{6,5},{7,6},{8,7},{9,8},{10,9},{11,1... | collective-permute-start | bytes 13064 | tf_op jit(solution)/shard_map/ppermute | solution.py:24
  458.1 5.9 collective-permute-start.14
  545.3 81.4 %copy-start = (f32[1,32,32]{1,2,0:T(8,128)S(1)}, f32[1,32,32]{1,2,0:T(8,128)}, u32[]{:S(2)}) copy-start(f32[1,32,32]{1,2,0:T(8,128)} %get-tuple-element.44) | copy-start | bytes 12292
  545.3 81.4 %copy-start.1 = (f32[1,32,32]{1,2,0:T(8,128)S(1)}, f32[1,32,32]{1,2,0:T(8,128)}, u32[]{:S(2)}) copy-start(f32[1,32,32]{1,2,0:T(8,128)} %get-tuple-element.46) | copy-start | bytes 12292
where the time goes:
time: 636 us; the launch traced here: 632 us
  blocking collectives  534 us (84%)
  other arithmetic  35.2 us (6%)
  starting transfers between devices  27.7 us (4%)
  waiting for transfers between devices  12.1 us (2%)
  matrix products  11.5 us (2%)
  local copies, waits for them, and re-layouts  10.9 us (2%)
    psum x4, blocking collectives, factorize(): gram = lax.psum(inner(flat, flat, cells), ('row', 'col'))  304 us
    psum x3, blocking collectives, body(): coeffs = lax.psum(inner(stacked, image, cells), ('row', 'col'))  231 us
    another operation x12, other arithmetic, finish(): lower = jnp.linalg.cholesky(gram)  14.4 us
    ppermute x8, starting transfers between devices, extended(): lax.ppermute(lax.slice_in_dim(block, 0, width, axis=dim), axis, backward)  14 us
    ppermute x8, starting transfers between devices, extended(): lax.ppermute(lax.slice_in_dim(block, block.shape[dim] - width, None, axis...  13.7 us
  transfers between devices with their start and end apart: 16, of which 6 were waited for; matrix products, arithmetic and copies ran while one was open for 2% of the time, Pallas kernels for 0%

commit v1 on v0

--- a/solution.py
+++ b/solution.py
@@ -1,7 +1,7 @@
 import jax
 import jax.numpy as jnp
 from jax import lax
-from jax.sharding import PartitionSpec as P
+from jax.sharding import Mesh, PartitionSpec as P
 
 ITERS = 3
 LEVELS = 50
@@ -27,8 +27,18 @@
 
 
 def widen(field):
-    rimmed = extended(field, (("row", 1),), 1, False)
-    return extended(rimmed, (("col", 2),), 1, True)
+    rimmed = extended(field, ((("x", "core"), 1),), 1, False)
+    return extended(rimmed, ((("z", "y"), 2),), 1, True)
+
+
+def spread_sum(part, axes):
+    count = lax.axis_size(axes)
+    copies = jnp.broadcast_to(part[None], (count, *part.shape))
+    return jnp.sum(lax.all_to_all(copies, axes, 0, 0), axis=0)
+
+
+def total_sum(part):
+    return spread_sum(spread_sum(part, ("x", "y")), ("core", "z"))
 
 
 def inner(left, right, cells):
@@ -45,13 +55,13 @@
 
 
 def factorize(flat, cells):
-    gram = lax.psum(inner(flat, flat, cells), ("row", "col"))
+    gram = total_sum(inner(flat, flat, cells))
     return finish(flat, gram)
 
 
 def body(start_block, sea_mask, depth_levels):
     blocks, lats, lons = start_block.shape
-    cells = float(lats * lons * lax.axis_size("row") * lax.axis_size("col"))
+    cells = float(lats * lons * lax.axis_size(("x", "core", "z", "y")))
     mask = sea_mask.astype(jnp.float32)
     depth = (mask * depth_levels.astype(jnp.float32) / LEVELS)[None]
     depth_wide = widen(depth)
@@ -77,7 +87,7 @@
             + weight_east * (middle - wide[:, 1:-1, 2:])
         )
         image = (mask[None] * middle + KAPPA * total).reshape(blocks, lats * lons)
-        coeffs = lax.psum(inner(stacked, image, cells), ("row", "col"))
+        coeffs = total_sum(inner(stacked, image, cells))
         image = image - jnp.dot(
             coeffs.T, stacked, precision=HIGH, preferred_element_type=jnp.float32
         )
@@ -93,6 +103,8 @@
 
 
 def solution(mesh):
-    in_specs = (P(None, "row", "col"), P("row", "col"), P("row", "col"))
-    out_specs = (P(None, "row", "col"), P(), P())
-    return jax.shard_map(body, mesh=mesh, in_specs=in_specs, out_specs=out_specs, check_vma=False)
+    torus = Mesh(mesh.devices.reshape(4, 2, 8, 4), ("x", "core", "z", "y"))
+    row, col = ("x", "core"), ("z", "y")
+    in_specs = (P(None, row, col), P(row, col), P(row, col))
+    out_specs = (P(None, row, col), P(), P())
+    return jax.shard_map(body, mesh=torus, in_specs=in_specs, out_specs=out_specs, check_vma=False)

time: 636 us -> 297 us (0.47)
  blocking collectives: 534 us -> 145 us
  starting transfers between devices: 27.7 us -> 47.8 us
  waiting for transfers between devices: 12.1 us -> 27.2 us
  other arithmetic: 35.2 us -> 44.4 us
    psum x7 -> x0, blocking collectives: 534 us -> none  [the longest x4 304 us: factorize(): gram = lax.psum(inner(flat, flat, cells), ('row', 'col'))]
    all_to_all x0 -> x11, blocking collectives: none -> 145 us  [spread_sum(): return jnp.sum(lax.all_to_all(copies, axes, 0, 0), axis=0)]
    all_to_all x0 -> x3, starting transfers between devices: none -> 20.1 us  [spread_sum(): return jnp.sum(lax.all_to_all(copies, axes, 0, 0), axis=0)]
    all_to_all x0 -> x3, waiting for transfers between devices: none -> 15.9 us  [spread_sum(): return jnp.sum(lax.all_to_all(copies, axes, 0, 0), axis=0)]
    all_to_all x0 -> x12, other arithmetic: none -> 8.84 us  [spread_sum(): return jnp.sum(lax.all_to_all(copies, axes, 0, 0), axis=0)]
  transfers between devices with their start and end apart: 16 -> 19, of which waited for: 6 -> 11; matrix products, arithmetic and copies ran while one was open for 2% -> 1% of each run, Pallas kernels for 0% -> 0%
where the time goes in v1:
time: 297 us; the launch traced here: 294 us
  blocking collectives  145 us (49%)
  starting transfers between devices  47.8 us (16%)
  other arithmetic  44.4 us (15%)
  waiting for transfers between devices  27.2 us (9%)
  local copies, waits for them, and re-layouts  16.4 us (6%)
  matrix products  11.5 us (4%)
    all_to_all x11, blocking collectives, spread_sum(): return jnp.sum(lax.all_to_all(copies, axes, 0, 0), axis=0)  145 us
    all_to_all x3, starting transfers between devices, spread_sum(): return jnp.sum(lax.all_to_all(copies, axes, 0, 0), axis=0)  20.1 us
    all_to_all x3, waiting for transfers between devices, spread_sum(): return jnp.sum(lax.all_to_all(copies, axes, 0, 0), axis=0)  15.9 us
    another operation x12, other arithmetic, finish(): lower = jnp.linalg.cholesky(gram)  14.4 us
    ppermute x8, starting transfers between devices, extended(): lax.ppermute(lax.slice_in_dim(block, 0, width, axis=dim), axis, backward)  13.8 us
    ppermute x8, starting transfers between devices, extended(): lax.ppermute(lax.slice_in_dim(block, block.shape[dim] - width, None, axis...  13.8 us
    another operation x5, other arithmetic, lower_solve(): return jax.scipy.linalg.solve_triangular(lower, values, lower=True)  10.4 us
    all_to_all x12, other arithmetic, spread_sum(): return jnp.sum(lax.all_to_all(copies, axes, 0, 0), axis=0)  8.84 us
  transfers between devices with their start and end apart: 19, of which 11 were waited for; matrix products, arithmetic and copies ran while one was open for 1% of the time, Pallas kernels for 0%

profile of v1, /device:TPU:8, one launch (start us, length us, event | category | flops | bytes accessed | tf_op | source)
XLA Modules:
  0.0 293.6 jit_solution(4666917088985142221)
XLA Ops:
  4.2 7.4 %all-to-all-start = ((f32[16,1,1024]{2,1,0:T(1,128)}), f32[16,1,1024]{2,1,0:T(1,128)S(1)}, u32[]{:S(2)}, u32[]{:S(2)}) async-start(f32[16,1,1024]{2,1,0:T(1,128)} %reshape.62), calls=%async_computation | async-start | bytes 131072 | tf_op jit(solution)/shard_map/all_to_all | solution.py:37
  11.6 6.3 %all-to-all-done = f32[16,1,1024]{2,1,0:T(1,128)S(1)} async-done(((f32[16,1,1024]{2,1,0:T(1,128)}), f32[16,1,1024]{2,1,0:T(1,128)S(1)}, u32[]{:S(2)}, u32[]{:S(2)}) %all-to-all-start) | async-done | bytes 65568 | tf_op jit(solution)/shard_map/all_to_all | solution.py:37
  20.1 8.6 %all-to-all-start.1 = ((f32[16,1,1024]{2,1,0:T(1,128)}), f32[16,1,1024]{2,1,0:T(1,128)S(1)}, u32[]{:S(2)}, u32[]{:S(2)}) async-start(f32[16,1,1024]{2,1,0:T(1,128)} %reshape.64), calls=%async_computation.1 | async-start | bytes 131072 | tf_op jit(solution)/shard_map/all_to_all | solution.py:37
  28.7 2.3 collective-permute-start
  31.0 1.3 collective-permute-start.2
  32.3 1.7 collective-permute-done.2
  34.0 2.6 all-to-all-done.1
  37.6 2.9 cholesky.74
  41.8 2.4 custom-call.8
  45.3 1.3 collective-permute-start.3
  46.6 3.0 %collective-permute-start.1 = (f32[32,1,128]{2,0,1:T(8,128)S(1)}, f32[32,1,128]{2,0,1:T(8,128)S(1)}, u32[]{:S(2)}, u32[]{:S(2)}) collective-permute-start(f32[32,1,128]{2,0,1:T(8,128)S(1)} %bitcast.168), channel_id=1, source_target_pairs={{0,32},{32,64},{64,96},{96,128},{128,160},{160,192},{192,224},{1,3... | collective-permute-start | bytes 49160 | tf_op jit(solution)/shard_map/ppermute | solution.py:21
  50.5 1.2 collective-permute-start.6
  52.7 4.8 %collective-permute-start.7 = (f32[32,34,1]{1,0,2:T(8,128)S(1)}, f32[32,34,1]{1,0,2:T(8,128)S(1)}, u32[]{:S(2)}, u32[]{:S(2)}) collective-permute-start(f32[32,34,1]{1,0,2:T(8,128)S(1)} %copy.294), channel_id=1, source_target_pairs={{1,0},{2,1},{3,2},{4,3},{5,4},{6,5},{7,6},{8,7},{9,8},{10,9},{11,1... | collective-permute-start | bytes 13064 | tf_op jit(solution)/shard_map/ppermute | solution.py:24
  57.7 3.6 %collective-permute-done.5 = f32[32,34,1]{1,0,2:T(8,128)S(1)} collective-permute-done((f32[32,34,1]{1,0,2:T(8,128)S(1)}, f32[32,34,1]{1,0,2:T(8,128)S(1)}, u32[]{:S(2)}, u32[]{:S(2)}) %collective-permute-start.5) | collective-permute-done | bytes 4384 | tf_op jit(solution)/shard_map/ppermute | solution.py:21
  63.7 13.5 %all_to_all.70 = f32[16,1,1024]{2,1,0:T(1,128)S(1)} all-to-all(f32[16,1,1024]{2,1,0:T(1,128)S(1)} %reshape.66), channel_id=1, replica_groups=mesh['x'=4,'core'=2,'z'=8,'y'=4] {'x','y'}, dimensions={0} | all-to-all | bytes 131072 | tf_op jit(solution)/shard_map/all_to_all | solution.py:37
  78.3 13.7 %all_to_all.71 = f32[16,1,1024]{2,1,0:T(1,128)S(1)} all-to-all(f32[16,1,1024]{2,1,0:T(1,128)S(1)} %reshape.68), channel_id=1, replica_groups=mesh['x'=4,'core'=2,'z'=8,'y'=4] {'core','z'}, dimensions={0} | all-to-all | bytes 131072 | tf_op jit(solution)/shard_map/all_to_all | solution.py:37
  94.5 10.9 %all_to_all.72 = f32[16,1,1024]{2,1,0:T(1,128)S(1)} all-to-all(f32[16,1,1024]{2,1,0:T(1,128)S(1)} %reshape.70), channel_id=1, replica_groups=mesh['x'=4,'core'=2,'z'=8,'y'=4] {'x','y'}, dimensions={0} | all-to-all | bytes 131072 | tf_op jit(solution)/shard_map/all_to_all | solution.py:37
  106.5 10.5 %all_to_all.73 = f32[16,1,1024]{2,1,0:T(1,128)S(1)} all-to-all(f32[16,1,1024]{2,1,0:T(1,128)S(1)} %reshape.72), channel_id=1, replica_groups=mesh['x'=4,'core'=2,'z'=8,'y'=4] {'core','z'}, dimensions={0} | all-to-all | bytes 131072 | tf_op jit(solution)/shard_map/all_to_all | solution.py:37
  117.9 2.9 cholesky.85
  121.5 1.3 fusion.70
  122.7 2.4 custom-call.9
  126.0 1.3 collective-permute-start.9
  127.3 3.0 %collective-permute-start.8 = (f32[32,1,128]{2,0,1:T(8,128)S(1)}, f32[32,1,128]{2,0,1:T(8,128)S(1)}, u32[]{:S(2)}, u32[]{:S(2)}) collective-permute-start(f32[32,1,128]{2,0,1:T(8,128)S(1)} %bitcast.170), channel_id=1, source_target_pairs={{0,32},{32,64},{64,96},{96,128},{128,160},{160,192},{192,224},{1,3... | collective-permute-start | bytes 49160 | tf_op jit(solution)/shard_map/ppermute | solution.py:21
  132.9 1.3 collective-permute-start.11
  134.2 1.5 collective-permute-done.10
  136.7 1.2 copy.306
  137.9 1.7 fusion.24
  141.0 17.2 %all_to_all.74 = f32[16,1,2048]{2,1,0:T(1,128)S(1)} all-to-all(f32[16,1,2048]{2,1,0:T(1,128)S(1)} %reshape.74), channel_id=1, replica_groups=mesh['x'=4,'core'=2,'z'=8,'y'=4] {'x','y'}, dimensions={0} | all-to-all | bytes 262144 | tf_op jit(solution)/shard_map/all_to_all | solution.py:37
  159.4 13.0 %all_to_all.75 = f32[16,1,2048]{2,1,0:T(1,128)S(1)} all-to-all(f32[16,1,2048]{2,1,0:T(1,128)S(1)} %reshape.76), channel_id=1, replica_groups=mesh['x'=4,'core'=2,'z'=8,'y'=4] {'core','z'}, dimensions={0} | all-to-all | bytes 262144 | tf_op jit(solution)/shard_map/all_to_all | solution.py:37
  175.0 11.2 %all_to_all.76 = f32[16,1,1024]{2,1,0:T(1,128)S(1)} all-to-all(f32[16,1,1024]{2,1,0:T(1,128)S(1)} %reshape.78), channel_id=1, replica_groups=mesh['x'=4,'core'=2,'z'=8,'y'=4] {'x','y'}, dimensions={0} | all-to-all | bytes 131072 | tf_op jit(solution)/shard_map/all_to_all | solution.py:37
  187.2 11.1 %all_to_all.77 = f32[16,1,1024]{2,1,0:T(1,128)S(1)} all-to-all(f32[16,1,1024]{2,1,0:T(1,128)S(1)} %reshape.80), channel_id=1, replica_groups=mesh['x'=4,'core'=2,'z'=8,'y'=4] {'core','z'}, dimensions={0} | all-to-all | bytes 131072 | tf_op jit(solution)/shard_map/all_to_all | solution.py:37
  199.2 2.9 cholesky.96
  202.8 1.2 fusion.71
  204.1 2.4 custom-call.10
  207.3 1.3 collective-permute-start.13
  208.6 3.0 %collective-permute-start.12 = (f32[32,1,128]{2,0,1:T(8,128)S(1)}, f32[32,1,128]{2,0,1:T(8,128)S(1)}, u32[]{:S(2)}, u32[]{:S(2)}) collective-permute-start(f32[32,1,128]{2,0,1:T(8,128)S(1)} %bitcast.171), channel_id=1, source_target_pairs={{0,32},{32,64},{64,96},{96,128},{128,160},{160,192},{192,224},{1,3... | collective-permute-start | bytes 49160 | tf_op jit(solution)/shard_map/ppermute | solution.py:21
  214.8 1.3 collective-permute-start.15
  216.1 1.6 collective-permute-done.14
  219.8 1.7 fusion.11
  221.5 1.5 convolution_multiply_fusion.2
  223.0 17.7 %all_to_all.78 = f32[16,96,32]{1,2,0:T(8,128)S(1)} all-to-all(f32[16,96,32]{1,2,0:T(8,128)S(1)} %broadcast_in_dim.42), channel_id=1, replica_groups=mesh['x'=4,'core'=2,'z'=8,'y'=4] {'x','y'}, dimensions={0} | all-to-all | bytes 393216 | tf_op jit(solution)/shard_map/all_to_all | solution.py:37
  240.8 14.9 %all_to_all.79 = f32[16,96,32]{1,2,0:T(8,128)S(1)} all-to-all(f32[16,96,32]{1,2,0:T(8,128)S(1)} %broadcast_in_dim.43), channel_id=1, replica_groups=mesh['x'=4,'core'=2,'z'=8,'y'=4] {'core','z'}, dimensions={0} | all-to-all | bytes 393216 | tf_op jit(solution)/shard_map/all_to_all | solution.py:37
  257.6 11.3 %all_to_all.80 = f32[16,1,1024]{2,1,0:T(1,128)S(1)} all-to-all(f32[16,1,1024]{2,1,0:T(1,128)S(1)} %reshape.82), channel_id=1, replica_groups=mesh['x'=4,'core'=2,'z'=8,'y'=4] {'x','y'}, dimensions={0} | all-to-all | bytes 131072 | tf_op jit(solution)/shard_map/all_to_all | solution.py:37
  270.6 4.2 %all-to-all-start.13 = ((f32[16,1,1024]{2,1,0:T(1,128)}), f32[16,1,1024]{2,1,0:T(1,128)S(1)}, u32[]{:S(2)}, u32[]{:S(2)}) async-start(f32[16,1,1024]{2,1,0:T(1,128)} %reshape.84), calls=%async_computation.13 | async-start | bytes 131072 | tf_op jit(solution)/shard_map/all_to_all | solution.py:37
  275.7 7.0 %all-to-all-done.13 = f32[16,1,1024]{2,1,0:T(1,128)S(1)} async-done(((f32[16,1,1024]{2,1,0:T(1,128)}), f32[16,1,1024]{2,1,0:T(1,128)S(1)}, u32[]{:S(2)}, u32[]{:S(2)}) %all-to-all-start.13) | async-done | bytes 65568 | tf_op jit(solution)/shard_map/all_to_all | solution.py:37
  283.7 2.9 cholesky.107
  288.7 2.4 custom-call.11
  291.9 1.7 copy.331
  (159 shorter events, 45.9 us)
Async XLA Ops:
  0.6 10.9 %copy-start = (s32[32,128]{1,0:T(8,128)S(1)}, s32[32,128]{1,0:T(8,128)}, u32[]{:S(2)}) copy-start(s32[32,128]{1,0:T(8,128)} %param.7) | copy-start | bytes 49156
  0.6 10.9 %copy-start.3 = (s32[32,128]{1,0:T(8,128)S(1)}, s32[32,128]{1,0:T(8,128)}, u32[]{:S(2)}) copy-start(s32[32,128]{1,0:T(8,128)} %param.8) | copy-start | bytes 49156
  4.2 13.7 %all-to-all-start = ((f32[16,1,1024]{2,1,0:T(1,128)}), f32[16,1,1024]{2,1,0:T(1,128)S(1)}, u32[]{:S(2)}, u32[]{:S(2)}) async-start(f32[16,1,1024]{2,1,0:T(1,128)} %reshape.62), calls=%async_computation | async-start | bytes 131072 | tf_op jit(solution)/shard_map/all_to_all | solution.py:37
  20.1 16.6 %all-to-all-start.1 = ((f32[16,1,1024]{2,1,0:T(1,128)}), f32[16,1,1024]{2,1,0:T(1,128)S(1)}, u32[]{:S(2)}, u32[]{:S(2)}) async-start(f32[16,1,1024]{2,1,0:T(1,128)} %reshape.64), calls=%async_computation.1 | async-start | bytes 131072 | tf_op jit(solution)/shard_map/all_to_all | solution.py:37
  28.7 3.6 %collective-permute-start = (f32[1,1,128]{2,1,0:T(1,128)S(1)}, f32[1,1,128]{2,1,0:T(1,128)S(1)}, u32[]{:S(2)}, u32[]{:S(2)}) collective-permute-start(f32[1,1,128]{2,1,0:T(1,128)S(1)} %get-tuple-element.50), channel_id=1, source_target_pairs={{0,32},{32,64},{64,96},{96,128},{128,160},{160,192},{192,224},{1,3... | collective-permute-start | bytes 1544 | tf_op jit(solution)/shard_map/ppermute | solution.py:21
  31.0 3.0 %collective-permute-start.2 = (f32[1,1,128]{2,1,0:T(1,128)S(1)}, f32[1,1,128]{2,1,0:T(1,128)S(1)}, u32[]{:S(2)}, u32[]{:S(2)}) collective-permute-start(f32[1,1,128]{2,1,0:T(1,128)S(1)} %get-tuple-element.51), channel_id=1, source_target_pairs={{32,0},{64,32},{96,64},{128,96},{160,128},{192,160},{224,192},{33,... | collective-permute-start | bytes 1544 | tf_op jit(solution)/shard_map/ppermute | solution.py:24
  45.3 6.5 %collective-permute-start.3 = (f32[32,1,128]{2,0,1:T(8,128)S(1)}, f32[32,1,128]{2,0,1:T(8,128)S(1)}, u32[]{:S(2)}, u32[]{:S(2)}) collective-permute-start(f32[32,1,128]{2,0,1:T(8,128)S(1)} %bitcast.169), channel_id=1, source_target_pairs={{32,0},{64,32},{96,64},{128,96},{160,128},{192,160},{224,192},{33,... | collective-permute-start | bytes 49160 | tf_op jit(solution)/shard_map/ppermute | solution.py:24
  46.6 5.2 %collective-permute-start.1 = (f32[32,1,128]{2,0,1:T(8,128)S(1)}, f32[32,1,128]{2,0,1:T(8,128)S(1)}, u32[]{:S(2)}, u32[]{:S(2)}) collective-permute-start(f32[32,1,128]{2,0,1:T(8,128)S(1)} %bitcast.168), channel_id=1, source_target_pairs={{0,32},{32,64},{64,96},{96,128},{128,160},{160,192},{192,224},{1,3... | collective-permute-start | bytes 49160 | tf_op jit(solution)/shard_map/ppermute | solution.py:21
  49.7 7.9 %collective-permute-start.4 = (f32[1,34,1]{2,1,0:T(8,128)S(1)}, f32[1,34,1]{2,1,0:T(8,128)S(1)}, u32[]{:S(2)}, u32[]{:S(2)}) collective-permute-start(f32[1,34,1]{2,1,0:T(8,128)S(1)} %get-tuple-element.38), channel_id=1, source_target_pairs={{0,1},{1,2},{2,3},{3,4},{4,5},{5,6},{6,7},{7,8},{8,9},{9,10},{10,1... | collective-permute-start | bytes 416 | tf_op jit(solution)/shard_map/ppermute | solution.py:21
  50.5 7.0 %collective-permute-start.6 = (f32[1,34,1]{2,1,0:T(8,128)S(1)}, f32[1,34,1]{2,1,0:T(8,128)S(1)}, u32[]{:S(2)}, u32[]{:S(2)}) collective-permute-start(f32[1,34,1]{2,1,0:T(8,128)S(1)} %get-tuple-element.39), channel_id=1, source_target_pairs={{1,0},{2,1},{3,2},{4,3},{5,4},{6,5},{7,6},{8,7},{9,8},{10,9},{11,1... | collective-permute-start | bytes 416 | tf_op jit(solution)/shard_map/ppermute | solution.py:24
  52.7 8.9 %collective-permute-start.7 = (f32[32,34,1]{1,0,2:T(8,128)S(1)}, f32[32,34,1]{1,0,2:T(8,128)S(1)}, u32[]{:S(2)}, u32[]{:S(2)}) collective-permute-start(f32[32,34,1]{1,0,2:T(8,128)S(1)} %copy.294), channel_id=1, source_target_pairs={{1,0},{2,1},{3,2},{4,3},{5,4},{6,5},{7,6},{8,7},{9,8},{10,9},{11,1... | collective-permute-start | bytes 13064 | tf_op jit(solution)/shard_map/ppermute | solution.py:24
  57.6 3.7 %collective-permute-start.5 = (f32[32,34,1]{1,0,2:T(8,128)S(1)}, f32[32,34,1]{1,0,2:T(8,128)S(1)}, u32[]{:S(2)}, u32[]{:S(2)}) collective-permute-start(f32[32,34,1]{1,0,2:T(8,128)S(1)} %copy.292), channel_id=1, source_target_pairs={{0,1},{1,2},{2,3},{3,4},{4,5},{5,6},{6,7},{7,8},{8,9},{9,10},{10,1... | collective-permute-start | bytes 13064 | tf_op jit(solution)/shard_map/ppermute | solution.py:21
  126.0 4.3 %collective-permute-start.9 = (f32[32,1,128]{2,0,1:T(8,128)S(1)}, f32[32,1,128]{2,0,1:T(8,128)S(1)}, u32[]{:S(2)}, u32[]{:S(2)}) collective-permute-start(f32[32,1,128]{2,0,1:T(8,128)S(1)} %bitcast.172), channel_id=1, source_target_pairs={{32,0},{64,32},{96,64},{128,96},{160,128},{192,160},{224,192},{33,... | collective-permute-start | bytes 49160 | tf_op jit(solution)/shard_map/ppermute | solution.py:24
  127.3 3.9 %collective-permute-start.8 = (f32[32,1,128]{2,0,1:T(8,128)S(1)}, f32[32,1,128]{2,0,1:T(8,128)S(1)}, u32[]{:S(2)}, u32[]{:S(2)}) collective-permute-start(f32[32,1,128]{2,0,1:T(8,128)S(1)} %bitcast.170), channel_id=1, source_target_pairs={{0,32},{32,64},{64,96},{96,128},{128,160},{160,192},{192,224},{1,3... | collective-permute-start | bytes 49160 | tf_op jit(solution)/shard_map/ppermute | solution.py:21
  131.8 3.9 %collective-permute-start.10 = (f32[32,34,1]{1,0,2:T(8,128)S(1)}, f32[32,34,1]{1,0,2:T(8,128)S(1)}, u32[]{:S(2)}, u32[]{:S(2)}) collective-permute-start(f32[32,34,1]{1,0,2:T(8,128)S(1)} %copy.303), channel_id=1, source_target_pairs={{0,1},{1,2},{2,3},{3,4},{4,5},{5,6},{6,7},{7,8},{8,9},{9,10},{10,1... | collective-permute-start | bytes 13064 | tf_op jit(solution)/shard_map/ppermute | solution.py:21
  132.9 3.8 %collective-permute-start.11 = (f32[32,34,1]{1,0,2:T(8,128)S(1)}, f32[32,34,1]{1,0,2:T(8,128)S(1)}, u32[]{:S(2)}, u32[]{:S(2)}) collective-permute-start(f32[32,34,1]{1,0,2:T(8,128)S(1)} %copy.305), channel_id=1, source_target_pairs={{1,0},{2,1},{3,2},{4,3},{5,4},{6,5},{7,6},{8,7},{9,8},{10,9},{11,1... | collective-permute-start | bytes 13064 | tf_op jit(solution)/shard_map/ppermute | solution.py:24
  207.3 4.3 %collective-permute-start.13 = (f32[32,1,128]{2,0,1:T(8,128)S(1)}, f32[32,1,128]{2,0,1:T(8,128)S(1)}, u32[]{:S(2)}, u32[]{:S(2)}) collective-permute-start(f32[32,1,128]{2,0,1:T(8,128)S(1)} %bitcast.173), channel_id=1, source_target_pairs={{32,0},{64,32},{96,64},{128,96},{160,128},{192,160},{224,192},{33,... | collective-permute-start | bytes 49160 | tf_op jit(solution)/shard_map/ppermute | solution.py:24
  208.6 3.9 %collective-permute-start.12 = (f32[32,1,128]{2,0,1:T(8,128)S(1)}, f32[32,1,128]{2,0,1:T(8,128)S(1)}, u32[]{:S(2)}, u32[]{:S(2)}) collective-permute-start(f32[32,1,128]{2,0,1:T(8,128)S(1)} %bitcast.171), channel_id=1, source_target_pairs={{0,32},{32,64},{64,96},{96,128},{128,160},{160,192},{192,224},{1,3... | collective-permute-start | bytes 49160 | tf_op jit(solution)/shard_map/ppermute | solution.py:21
  213.7 4.0 %collective-permute-start.14 = (f32[32,34,1]{1,0,2:T(8,128)}, f32[32,34,1]{1,0,2:T(8,128)S(1)}, u32[]{:S(2)}, u32[]{:S(2)}) collective-permute-start(f32[32,34,1]{1,0,2:T(8,128)} %copy.314), channel_id=1, source_target_pairs={{0,1},{1,2},{2,3},{3,4},{4,5},{5,6},{6,7},{7,8},{8,9},{9,10},{10,1... | collective-permute-start | bytes 13064 | tf_op jit(solution)/shard_map/ppermute | solution.py:21
  214.8 3.8 %collective-permute-start.15 = (f32[32,34,1]{1,0,2:T(8,128)S(1)}, f32[32,34,1]{1,0,2:T(8,128)S(1)}, u32[]{:S(2)}, u32[]{:S(2)}) collective-permute-start(f32[32,34,1]{1,0,2:T(8,128)S(1)} %copy.316), channel_id=1, source_target_pairs={{1,0},{2,1},{3,2},{4,3},{5,4},{6,5},{7,6},{8,7},{9,8},{10,9},{11,1... | collective-permute-start | bytes 13064 | tf_op jit(solution)/shard_map/ppermute | solution.py:24
  257.4 30.5 %copy-start.1 = (f32[1,32,32]{1,2,0:T(8,128)S(1)}, f32[1,32,32]{1,2,0:T(8,128)}, u32[]{:S(2)}) copy-start(f32[1,32,32]{1,2,0:T(8,128)} %get-tuple-element.44) | copy-start | bytes 12292
  257.4 30.5 %copy-start.2 = (f32[1,32,32]{1,2,0:T(8,128)S(1)}, f32[1,32,32]{1,2,0:T(8,128)}, u32[]{:S(2)}) copy-start(f32[1,32,32]{1,2,0:T(8,128)} %get-tuple-element.46) | copy-start | bytes 12292
  270.6 12.1 %all-to-all-start.13 = ((f32[16,1,1024]{2,1,0:T(1,128)}), f32[16,1,1024]{2,1,0:T(1,128)S(1)}, u32[]{:S(2)}, u32[]{:S(2)}) async-start(f32[16,1,1024]{2,1,0:T(1,128)} %reshape.84), calls=%async_computation.13 | async-start | bytes 131072 | tf_op jit(solution)/shard_map/all_to_all | solution.py:37

commit v2 on v0

v2 whole, which is shorter than its diff:
```python
import jax
import jax.numpy as jnp
from jax import lax
from jax.experimental import pallas as pl
from jax.experimental.pallas import tpu as pltpu
from jax.sharding import Mesh, PartitionSpec as P

ITERS = 3
LEVELS = 50.0
KAPPA = 1.5
SHIFT = 3.0
CELLS = 1048576.0

B = 32
LAT = 32
LON = 128
RIM = 3
ROWS = LAT + 2 * RIM
WIDE = 2 * LON
ALL = (ITERS + 1) * B
HIGH = lax.Precision.HIGHEST
ROW, COL = ("x", "core"), ("z", "y")
NT = (((1,), (1,)), ((), ()))
PARAMS = pltpu.CompilerParams(vmem_limit_bytes=48 * 1024 * 1024)


def lanes_of(rows):
    return lax.broadcasted_iota(jnp.int32, (rows, LON), 1)


def call(kernel, outs, scratch=(), flops=0, moved=0):
    return pl.pallas_call(
        kernel,
        out_shape=tuple(jax.ShapeDtypeStruct(s, jnp.float32) for s in outs),
        scratch_shapes=list(scratch),
        compiler_params=PARAMS,
        cost_estimate=pl.CostEstimate(flops=flops, bytes_accessed=moved, transcendentals=0),
    )


def masked_row(lat, x_ref, mask_ref, depth_ref):
    mask = mask_ref[pl.ds(lat, 1), :].astype(jnp.float32)
    depth = mask * depth_ref[pl.ds(lat, 1), :].astype(jnp.float32) / LEVELS
    row = x_ref[pl.ds(lat, B, stride=LAT), :] * mask
    return jnp.concatenate([row, jnp.broadcast_to(depth, (8, LON))], axis=0)


def edge_rows(x_ref, mask_ref, depth_ref, top_ref, bottom_ref):
    for i in range(RIM):
        top_ref[i] = masked_row(i, x_ref, mask_ref, depth_ref)
        bottom_ref[i] = masked_row(LAT - RIM + i, x_ref, mask_ref, depth_ref)


def pack_sides(row, r, west, east):
    lane = lanes_of(B + 8)
    here = (lane >= RIM * r) & (lane < RIM * r + RIM)
    west = jnp.where(here, pltpu.roll(row, (RIM * r) % LON, 1), west)
    east = jnp.where(here, pltpu.roll(row, (RIM * r + RIM) % LON, 1), east)
    return west, east


def core_rows(x_ref, mask_ref, depth_ref, core_ref, west_ref, east_ref):
    west = east = jnp.zeros((B + 8, LON), jnp.float32)
    for i in range(LAT):
        row = masked_row(i, x_ref, mask_ref, depth_ref)
        core_ref[i] = row
        west, east = pack_sides(row, i + RIM, west, east)
    west_ref[...] = west
    east_ref[...] = east


def side_columns(north_ref, south_ref, part_west_ref, part_east_ref, west_ref, east_ref):
    west, east = part_west_ref[...], part_east_ref[...]
    for i in range(RIM):
        west, east = pack_sides(north_ref[i], i, west, east)
        west, east = pack_sides(south_ref[i], i + RIM + LAT, west, east)
    west_ref[...] = west
    east_ref[...] = east


def four(field):
    return jnp.concatenate([field] * (B // 8), axis=0)


def krylov(core_ref, north_ref, south_ref, west_ref, east_ref, s_ref, gram_ref,
           x_ref, k1_ref, k2_ref, h_ref, down_ref, right_ref):
    lane = lanes_of(B + 8)
    from_west, from_east = west_ref[...], east_ref[...]
    for r in range(ROWS):
        if r < RIM:
            row = north_ref[r]
        elif r < RIM + LAT:
            row = core_ref[r - RIM]
        else:
            row = south_ref[r - RIM - LAT]
        beyond = jnp.where(lane < RIM, pltpu.roll(from_east, (-RIM * r) % LON, 1), 0.0)
        beyond = jnp.where(lane >= LON - RIM, pltpu.roll(from_west, (LON - RIM - RIM * r) % LON, 1), beyond)
        full = jnp.concatenate([row, beyond], axis=1)
        x_ref[r] = full[:B]
        h_ref[r] = full[B:]
    for r in range(ROWS):
        h = h_ref[r]
        if r + 1 < ROWS:
            down_ref[r] = KAPPA * jnp.minimum(h, h_ref[r + 1])
        right_ref[r] = KAPPA * jnp.minimum(h, pltpu.roll(h, WIDE - 1, 1))
    for i in range(LAT):
        s_ref[i, :B, :] = x_ref[i + RIM][:, :LON]
    levels = ((x_ref, k1_ref, 1.0), (k1_ref, k2_ref, 1.0 + SHIFT), (k2_ref, None, 1.0 + SHIFT))
    for step, (source, target, shift) in enumerate(levels):
        first, last = step + 1, ROWS - 2 - step
        flux = four(down_ref[first - 1]) * (source[first - 1] - source[first])
        for r in range(first, last + 1):
            v = source[r]
            centre = jnp.where(h_ref[r] > 0.0, 1.0 - shift, -shift)
            down = four(down_ref[r]) * (v - source[r + 1])
            right = four(right_ref[r]) * (v - pltpu.roll(v, WIDE - 1, 1))
            new = four(centre) * v + ((down - flux) + (right - pltpu.roll(right, 1, 1)))
            flux = down
            if target is not None:
                target[r] = new
            if RIM <= r < RIM + LAT:
                s_ref[r - RIM, (step + 1) * B:(step + 2) * B, :] = new[:, :LON]
    total = jnp.zeros((ALL, ALL), jnp.float32)
    for i in range(0, LAT, 2):
        pair = jnp.concatenate([s_ref[i], s_ref[i + 1]], axis=1)
        total += lax.dot_general(pair, pair, NT, precision=HIGH, preferred_element_type=jnp.float32)
    gram_ref[...] = total


def spread(parts_ref, out_ref):
    total = parts_ref[0]
    for i in range(1, parts_ref.shape[0]):
        total += parts_ref[i]
    for i in range(out_ref.shape[0]):
        out_ref[i] = total


def basis(parts_ref, s_ref, q_ref, alpha_ref, beta_ref):
    total = parts_ref[0]
    for i in range(1, parts_ref.shape[0]):
        total += parts_ref[i]
    work = total * (1.0 / CELLS)
    lane = lax.broadcasted_iota(jnp.int32, (ALL, ALL), 1)
    sub = lax.broadcasted_iota(jnp.int32, (ALL, ALL), 0)
    for j in range(ALL):
        base = (j // 8) * 8
        low = work[base:]
        pivot = work[j:j + 1, j:j + 1]
        row = jnp.where(lane[:1] == j, 1.0, work[j:j + 1])
        ratio = jnp.where(sub[base:, :1] > j, low[:, j:j + 1] * (1.0 / pivot), 0.0)
        kept = jnp.where((lane[base:] == j) & (sub[base:] > j), 0.0, low)
        low = kept - ratio * row
        work = low if base == 0 else jnp.concatenate([work[:base], low], axis=0)
    pivots = jnp.sum(jnp.where(lane == sub, work, 0.0), axis=1, keepdims=True)
    scale = lax.rsqrt(pivots)
    inverse = scale * jnp.where(lane < sub, work, jnp.where(lane == sub, 1.0, 0.0))
    upper = scale * jnp.where(lane >= sub, work, 0.0)
    own = jnp.where(lane < B, 1.0, jnp.where(lane < ITERS * B, 1.0 + SHIFT, 0.0))
    image = inverse * own + jnp.where(lane >= B, pltpu.roll(inverse, B, 1), 0.0)
    coeffs = lax.dot_general(upper, image, NT, precision=HIGH, preferred_element_type=jnp.float32)
    for k in range(ITERS):
        here, after = slice(k * B, (k + 1) * B), slice((k + 1) * B, (k + 2) * B)
        alpha_ref[k] = coeffs[here, here]
        beta_ref[k] = coeffs[after, here]
    for i in range(0, LAT, 2):
        pair = jnp.concatenate([s_ref[i], s_ref[i + 1]], axis=1)
        new = jnp.dot(inverse, pair, precision=HIGH, preferred_element_type=jnp.float32)
        q_ref[pl.ds(i, ALL, stride=LAT), :] = new[:, :LON]
        q_ref[pl.ds(i + 1, ALL, stride=LAT), :] = new[:, LON:]


def body(start_block, sea_mask, depth_levels):
    x = start_block.reshape(B * LAT, LON)
    edge = (RIM, B + 8, LON)
    side = (B + 8, LON)
    top, bottom = call(edge_rows, (edge, edge))(x, sea_mask, depth_levels)
    down = [(i, i + 1) for i in range(7)]
    up = [(i + 1, i) for i in range(7)]
    north = lax.ppermute(bottom, ROW, down)
    south = lax.ppermute(top, ROW, up)
    core, part_west, part_east = call(core_rows, ((LAT, B + 8, LON), side, side), flops=1 << 22, moved=1 << 20)(
        x, sea_mask, depth_levels
    )
    west, east = call(side_columns, (side, side))(north, south, part_west, part_east)
    from_east = lax.ppermute(west, COL, [((i + 1) % 32, i) for i in range(32)])
    from_west = lax.ppermute(east, COL, [(i, (i + 1) % 32) for i in range(32)])
    wide = (ROWS, B, WIDE)
    thin = (ROWS, 8, WIDE)
    s, gram = call(
        krylov,
        ((LAT, ALL, LON), (ALL, ALL)),
        [pltpu.VMEM(wide, jnp.float32)] * 3 + [pltpu.VMEM(thin, jnp.float32)] * 3,
    )(core, north, south, from_west, from_east)
    pair = lax.all_gather(gram, "core")
    copies = call(spread, ((16, ALL, ALL),))(pair)[0]
    parts = lax.all_to_all(copies, ("x", "y"), 0, 0)
    copies = call(spread, ((8, ALL, ALL),))(parts)[0]
    parts = lax.all_to_all(copies, "z", 0, 0)
    q, alphas, betas = call(basis, ((ALL * LAT, LON), (ITERS, B, B), (ITERS, B, B)))(parts, s)
    return q.reshape(ALL, LAT, LON), alphas, betas


def solution(mesh):
    torus = Mesh(mesh.devices.reshape(4, 2, 8, 4), ("x", "core", "z", "y"))
    in_specs = (P(None, ROW, COL), P(ROW, COL), P(ROW, COL))
    out_specs = (P(None, ROW, COL), P(), P())
    return jax.shard_map(body, mesh=torus, in_specs=in_specs, out_specs=out_specs, check_vma=False)
```

time: 636 us -> 87.2 us (0.14)
  blocking collectives: 534 us -> 52.8 us
  other arithmetic: 35.2 us -> 0 us
  starting transfers between devices: 27.7 us -> 5.14 us
  Pallas kernels: 0 us -> 19.8 us
  matrix products: 11.5 us -> 0 us
  local copies, waits for them, and re-layouts: 10.9 us -> 2.47 us
    psum x7 -> x0, blocking collectives: 534 us -> none  [the longest x4 304 us: factorize(): gram = lax.psum(inner(flat, flat, cells), ('row', 'col'))]
    all_to_all x0 -> x2, blocking collectives: none -> 49.8 us  [the longest x1 25.8 us: body(): parts = lax.all_to_all(copies, ('x', 'y'), 0, 0)]
    another operation x22 -> x0, other arithmetic: 27.9 us -> none  [the longest x12 14.4 us: finish(): lower = jnp.linalg.cholesky(gram)]
    ppermute x16 -> x4, starting transfers between devices: 27.7 us -> 5.14 us  [the longest x1 1.74 us: body(): north = lax.ppermute(bottom, ROW, down)]
    pallas_call x0 -> x7, Pallas kernels: none -> 19.8 us  [the longest x1 15.1 us: body(): call(basis, ((ALL * LAT, LON), (ITERS, B, B), (ITERS, B, B)))(parts, s)]
    dot_general x10 -> x0, matrix products: 8.61 us -> none  [the longest x7 5.89 us: inner(): jnp.dot(left, right.T, precision=HIGH, preferred_element_type=jnp.float32)]
  transfers between devices with their start and end apart: 16 -> 4, of which waited for: 6 -> 3; matrix products, arithmetic and copies ran while one was open for 2% -> 0% of each run, Pallas kernels for 0% -> 1%
where the time goes in v2:
time: 87.2 us; the launch traced here: 86.8 us
  blocking collectives  52.8 us (61%)
  Pallas kernels  19.8 us (23%)
  waiting for transfers between devices  5.94 us (7%)
  starting transfers between devices  5.14 us (6%)
  local copies, waits for them, and re-layouts  2.47 us (3%)
    all_to_all x1, blocking collectives, body(): parts = lax.all_to_all(copies, ('x', 'y'), 0, 0)  25.8 us
    all_to_all x1, blocking collectives, body(): parts = lax.all_to_all(copies, 'z', 0, 0)  24 us
    pallas_call x1, Pallas kernels, body(): call(basis, ((ALL * LAT, LON), (ITERS, B, B), (ITERS, B, B)))(parts, s)  15.1 us
    pallas_call x1, Pallas kernels, body(): call(krylov, ((LAT, ALL, LON), (ALL, ALL)), [pltpu.VMEM(wide, jnp.float32...  3.86 us
    all_gather x1, blocking collectives, body(): pair = lax.all_gather(gram, 'core')  3.01 us
    ppermute x1, waiting for transfers between devices, body(): south = lax.ppermute(top, ROW, up)  2.6 us
    unnamed x6, local copies, waits for them, and re-layouts  2.47 us
    ppermute x1, waiting for transfers between devices, body(): from_west = lax.ppermute(east, COL, [(i, (i + 1) % 32) for i in range(32)])  1.76 us
  transfers between devices with their start and end apart: 4, of which 3 were waited for; matrix products, arithmetic and copies ran while one was open for 0% of the time, Pallas kernels for 1%

profile of v2, /device:TPU:8, one launch (start us, length us, event | category | flops | bytes accessed | tf_op | source)
XLA Modules:
  0.0 86.8 jit_solution(5999298969413198101)
XLA Ops:
  0.6 0.0 copy-start
  0.6 1.0 %copy-done = f32[32,32,128]{2,1,0:T(8,128)S(1)} copy-done((f32[32,32,128]{2,1,0:T(8,128)S(1)}, f32[32,32,128]{2,1,0:T(8,128)}, u32[]{:S(2)}) %copy-start) | copy-done | bytes 524312
  1.7 0.0 copy-start.1
  1.7 0.7 copy-done.1
  2.4 0.0 copy-start.2
  2.4 0.7 copy-done.2
  3.1 0.1 shard_map.59
  3.2 1.7 %collective-permute-start = (f32[3,40,128]{2,1,0:T(8,128)S(1)}, f32[3,40,128]{2,1,0:T(8,128)S(1)}, u32[]{:S(2)}, u32[]{:S(2)}) collective-permute-start(f32[3,40,128]{2,1,0:T(8,128)S(1)} %get-tuple-element.16), channel_id=1, source_target_pairs={{0,32},{32,64},{64,96},{96,128},{128,160},{160,192},{192,224},{1,3... | collective-permute-start | bytes 184328 | tf_op jit(solution)/shard_map/ppermute | solution.py:179
  4.9 1.3 %collective-permute-start.1 = (f32[3,40,128]{2,1,0:T(8,128)S(1)}, f32[3,40,128]{2,1,0:T(8,128)S(1)}, u32[]{:S(2)}, u32[]{:S(2)}) collective-permute-start(f32[3,40,128]{2,1,0:T(8,128)S(1)} %get-tuple-element.17), channel_id=1, source_target_pairs={{32,0},{64,32},{96,64},{128,96},{160,128},{192,160},{224,192},{33,... | collective-permute-start | bytes 184328 | tf_op jit(solution)/shard_map/ppermute | solution.py:180
  6.2 0.5 shard_map.58
  6.7 0.0 collective-permute-done.north_ref
  6.7 2.6 %collective-permute-done.1.south_ref = f32[3,40,128]{2,1,0:T(8,128)S(1)} collective-permute-done((f32[3,40,128]{2,1,0:T(8,128)S(1)}, f32[3,40,128]{2,1,0:T(8,128)S(1)}, u32[]{:S(2)}, u32[]{:S(2)}) %collective-permute-start.1) | collective-permute-done | bytes 61472 | tf_op jit(solution)/shard_map/ppermute | solution.py:180
  9.3 0.1 shard_map.60
  9.5 1.7 %collective-permute-start.2 = (f32[40,128]{1,0:T(8,128)S(1)}, f32[40,128]{1,0:T(8,128)S(1)}, u32[]{:S(2)}, u32[]{:S(2)}) collective-permute-start(f32[40,128]{1,0:T(8,128)S(1)} %get-tuple-element.20), channel_id=1, source_target_pairs={{0,1},{1,2},{2,3},{3,4},{4,5},{5,6},{6,7},{7,8},{8,9},{9,10},{10,1... | collective-permute-start | bytes 61448 | tf_op jit(solution)/shard_map/ppermute | solution.py:186
  11.1 0.4 collective-permute-start.3
  11.6 1.8 %collective-permute-done.2.west_ref = f32[40,128]{1,0:T(8,128)S(1)} collective-permute-done((f32[40,128]{1,0:T(8,128)S(1)}, f32[40,128]{1,0:T(8,128)S(1)}, u32[]{:S(2)}, u32[]{:S(2)}) %collective-permute-start.2) | collective-permute-done | bytes 20512 | tf_op jit(solution)/shard_map/ppermute | solution.py:186
  13.3 1.6 %collective-permute-done.3.east_ref = f32[40,128]{1,0:T(8,128)S(1)} collective-permute-done((f32[40,128]{1,0:T(8,128)S(1)}, f32[40,128]{1,0:T(8,128)S(1)}, u32[]{:S(2)}, u32[]{:S(2)}) %collective-permute-start.3) | collective-permute-done | bytes 20512 | tf_op jit(solution)/shard_map/ppermute | solution.py:185
  14.9 3.9 %shard_map.61 = (f32[32,128,128]{2,1,0:T(8,128)S(1)}, f32[128,128]{1,0:T(8,128)S(1)}) custom-call(f32[32,40,128]{2,1,0:T(8,128)S(1)} %get-tuple-element.15.core_ref, f32[3,40,128]{2,1,0:T(8,128)S(1)} %collective-permute-done.north_ref, f32[3,40,128]{2,1,0:T(8,128)S(1)} %collective-permute-done.1.south_ref, f32[40,128]{1,0:T(8,128)S(1)} %collective-permute-done.2.west_ref, ...), custom_call_target="tpu_custom_call" | custom-call | tf_op jit(solution)/shard_map/pallas_call | solution.py:189
  18.8 3.0 %all-gather = f32[256,128]{1,0:T(8,128)S(1)} all-gather(f32[128,128]{1,0:T(8,128)S(1)} %get-tuple-element.22), channel_id=2, replica_groups=mesh['x'=4,'core'=2,'z'=8,'y'=4] {'core'}, dimensions={0}, use_global_device_ids=true | all-gather | bytes 196608 | tf_op jit(solution)/shard_map/all_gather | solution.py:194
  21.8 0.1 shard_map.62
  21.9 25.8 %all_to_all.10.parts_ref = f32[16,128,128]{2,1,0:T(8,128)S(1)} all-to-all(f32[16,128,128]{2,1,0:T(8,128)S(1)} %shard_map.62), channel_id=1, replica_groups=mesh['x'=4,'core'=2,'z'=8,'y'=4] {'x','y'}, dimensions={0} | all-to-all | bytes 2097152 | tf_op jit(solution)/shard_map/all_to_all | solution.py:196
  47.7 0.1 shard_map.63
  47.8 24.0 %all_to_all.11.parts_ref = f32[8,128,128]{2,1,0:T(8,128)S(1)} all-to-all(f32[8,128,128]{2,1,0:T(8,128)S(1)} %shard_map.63), channel_id=1, replica_groups=mesh['x'=4,'core'=2,'z'=8,'y'=4] {'z'}, dimensions={0} | all-to-all | bytes 1048576 | tf_op jit(solution)/shard_map/all_to_all | solution.py:198
  71.7 15.1 %shard_map.64 = (f32[4096,128]{1,0:T(8,128)}, f32[3,32,32]{2,1,0:T(8,128)}, f32[3,32,32]{2,1,0:T(8,128)}) custom-call(f32[8,128,128]{2,1,0:T(8,128)S(1)} %all_to_all.11.parts_ref, f32[32,128,128]{2,1,0:T(8,128)S(1)} %get-tuple-element.23.s_ref), custom_call_target="tpu_custom_call" | custom-call | tf_op jit(solution)/shard_map/pallas_call | solution.py:199
Async XLA Ops:
  0.6 1.0 %copy-start = (f32[32,32,128]{2,1,0:T(8,128)S(1)}, f32[32,32,128]{2,1,0:T(8,128)}, u32[]{:S(2)}) copy-start(f32[32,32,128]{2,1,0:T(8,128)} %param.3) | copy-start | bytes 1572868
  1.7 0.7 copy-start.1
  2.4 0.7 copy-start.2
  3.2 3.6 %collective-permute-start = (f32[3,40,128]{2,1,0:T(8,128)S(1)}, f32[3,40,128]{2,1,0:T(8,128)S(1)}, u32[]{:S(2)}, u32[]{:S(2)}) collective-permute-start(f32[3,40,128]{2,1,0:T(8,128)S(1)} %get-tuple-element.16), channel_id=1, source_target_pairs={{0,32},{32,64},{64,96},{96,128},{128,160},{160,192},{192,224},{1,3... | collective-permute-start | bytes 184328 | tf_op jit(solution)/shard_map/ppermute | solution.py:179
  4.9 4.4 %collective-permute-start.1 = (f32[3,40,128]{2,1,0:T(8,128)S(1)}, f32[3,40,128]{2,1,0:T(8,128)S(1)}, u32[]{:S(2)}, u32[]{:S(2)}) collective-permute-start(f32[3,40,128]{2,1,0:T(8,128)S(1)} %get-tuple-element.17), channel_id=1, source_target_pairs={{32,0},{64,32},{96,64},{128,96},{160,128},{192,160},{224,192},{33,... | collective-permute-start | bytes 184328 | tf_op jit(solution)/shard_map/ppermute | solution.py:180
  9.5 3.9 %collective-permute-start.2 = (f32[40,128]{1,0:T(8,128)S(1)}, f32[40,128]{1,0:T(8,128)S(1)}, u32[]{:S(2)}, u32[]{:S(2)}) collective-permute-start(f32[40,128]{1,0:T(8,128)S(1)} %get-tuple-element.20), channel_id=1, source_target_pairs={{0,1},{1,2},{2,3},{3,4},{4,5},{5,6},{6,7},{7,8},{8,9},{9,10},{10,1... | collective-permute-start | bytes 61448 | tf_op jit(solution)/shard_map/ppermute | solution.py:186
  11.1 3.8 %collective-permute-start.3 = (f32[40,128]{1,0:T(8,128)S(1)}, f32[40,128]{1,0:T(8,128)S(1)}, u32[]{:S(2)}, u32[]{:S(2)}) collective-permute-start(f32[40,128]{1,0:T(8,128)S(1)} %get-tuple-element.21), channel_id=1, source_target_pairs={{1,0},{2,1},{3,2},{4,3},{5,4},{6,5},{7,6},{8,7},{9,8},{10,9},{11,1... | collective-permute-start | bytes 61448 | tf_op jit(solution)/shard_map/ppermute | solution.py:185

commit v3 on v2

--- a/solution.py
+++ b/solution.py
@@ -28,9 +28,10 @@
     return lax.broadcasted_iota(jnp.int32, (rows, LON), 1)
 
 
-def call(kernel, outs, scratch=(), flops=0, moved=0):
+def call(kernel, outs, scratch=(), flops=0, moved=0, **specs):
     return pl.pallas_call(
         kernel,
+        **specs,
         out_shape=tuple(jax.ShapeDtypeStruct(s, jnp.float32) for s in outs),
         scratch_shapes=list(scratch),
         compiler_params=PARAMS,
@@ -45,7 +46,13 @@
     return jnp.concatenate([row, jnp.broadcast_to(depth, (8, LON))], axis=0)
 
 
-def edge_rows(x_ref, mask_ref, depth_ref, top_ref, bottom_ref):
+def edge_rows(x_hbm, mask_hbm, depth_hbm, top_ref, bottom_ref, x_ref, mask_ref, depth_ref, sems):
+    pairs = ((x_hbm, x_ref), (mask_hbm, mask_ref), (depth_hbm, depth_ref))
+    copies = [pltpu.make_async_copy(source, target, sems.at[i]) for i, (source, target) in enumerate(pairs)]
+    for copy in copies:
+        copy.start()
+    for copy in copies:
+        copy.wait()
     for i in range(RIM):
         top_ref[i] = masked_row(i, x_ref, mask_ref, depth_ref)
         bottom_ref[i] = masked_row(LAT - RIM + i, x_ref, mask_ref, depth_ref)
@@ -76,6 +83,14 @@
         west, east = pack_sides(south_ref[i], i + RIM + LAT, west, east)
     west_ref[...] = west
     east_ref[...] = east
+
+
+def split(value):
+    high = value.astype(jnp.bfloat16)
+    rest = value - high.astype(jnp.float32)
+    middle = rest.astype(jnp.bfloat16)
+    low = (rest - middle.astype(jnp.float32)).astype(jnp.bfloat16)
+    return high, middle, low
 
 
 def four(field):
@@ -120,11 +135,25 @@
                 target[r] = new
             if RIM <= r < RIM + LAT:
                 s_ref[r - RIM, (step + 1) * B:(step + 2) * B, :] = new[:, :LON]
-    total = jnp.zeros((ALL, ALL), jnp.float32)
+    outer = lambda left, right: lax.dot_general(left, right, NT, preferred_element_type=jnp.float32)
+    large = small = jnp.zeros((ALL, 2 * ALL), jnp.float32)
     for i in range(0, LAT, 2):
-        pair = jnp.concatenate([s_ref[i], s_ref[i + 1]], axis=1)
-        total += lax.dot_general(pair, pair, NT, precision=HIGH, preferred_element_type=jnp.float32)
-    gram_ref[...] = total
+        high, middle, low = split(jnp.concatenate([s_ref[i], s_ref[i + 1]], axis=1))
+        large += outer(high, jnp.concatenate([high, middle], axis=0))
+        small += jnp.concatenate([outer(high, low), outer(middle, middle)], axis=1)
+    half = large[:, ALL:] + small[:, :ALL]
+    gram = large[:, :ALL] + small[:, ALL:] + half + half.T
+    row = lax.broadcasted_iota(jnp.int32, (B, LON), 0)
+    lane = lax.broadcasted_iota(jnp.int32, (B, LON), 1)
+    packed = diagonal = jnp.zeros((B, LON), jnp.float32)
+    for k in range(ITERS + 1):
+        own = gram[k * B:(k + 1) * B]
+        after = pltpu.roll(own, LON - B, 1)
+        here = (lane >= k * B) & (lane < (k + 1) * B)
+        packed = jnp.where(here, jnp.where(lane - k * B >= row, own, after), packed)
+        diagonal = jnp.where(here & (lane - k * B == row), after, diagonal)
+    gram_ref[:B] = packed
+    gram_ref[B:] = (diagonal[:8] + diagonal[8:16]) + (diagonal[16:24] + diagonal[24:])
 
 
 def spread(parts_ref, out_ref):
@@ -135,26 +164,94 @@
         out_ref[i] = total
 
 
-def basis(parts_ref, s_ref, q_ref, alpha_ref, beta_ref):
+def unpack(total):
+    row = lax.broadcasted_iota(jnp.int32, (B, LON), 0)
+    lane = lax.broadcasted_iota(jnp.int32, (B, LON), 1)
+    block, place = lane // B, lane % B
+    turned = jnp.concatenate([total[:B], jnp.zeros((LON - B, LON), jnp.float32)], axis=0).T
+    mirror = jnp.zeros((B, LON), jnp.float32)
+    for k in range(ITERS + 1):
+        part = turned[k * B:(k + 1) * B]
+        mirror = jnp.where(block == k, pltpu.roll(part, k * B, 1) if k else part, mirror)
+    even = jnp.where(place >= row, total[:B], mirror)
+    odd = jnp.where(place < row, total[:B], mirror)
+    odd = jnp.where(place == row, jnp.sum(total[B:], axis=0, keepdims=True), odd)
+    move = lambda field, k: pltpu.roll(field, (k * B) % LON, 1)
+    even1, even2, odd1, odd2, odd3 = move(even, 1), move(even, -1), move(odd, 1), move(odd, 2), move(odd, 3)
+    pick = lambda a, b, c, d: jnp.where(block == 0, a, jnp.where(block == 1, b, jnp.where(block == 2, c, d)))
+    corner = move(odd, -1)
+    return jnp.concatenate(
+        [
+            pick(even, odd1, even1 - SHIFT * odd2, odd2 - SHIFT * (move(even, 2) - SHIFT * odd3)),
+            pick(odd, even, odd1, even1),
+            pick(even2 - SHIFT * odd, odd, even, odd1),
+            pick(corner - SHIFT * (even2 - SHIFT * odd), even2, odd, even),
+        ],
+        axis=0,
+    )
+
+
+def factor(gram):
+    groups = ALL // 8
+    lane = lax.broadcasted_iota(jnp.int32, (8, ALL), 1)
+    sub = lax.broadcasted_iota(jnp.int32, (8, ALL), 0)
+    full = lambda value: jnp.broadcast_to(value, (8, ALL))
+    tree = lambda p: ((p[0] + p[1]) + (p[2] + p[3])) + ((p[4] + p[5]) + (p[6] + p[7]))
+    left = [gram[8 * g:8 * g + 8] for g in range(groups)]
+    right = [jnp.where(lane == sub + 8 * g, 1.0, 0.0) for g in range(groups)]
+    uppers, inverses = [], []
+    for g in range(groups):
+        columns = [full(left[g][:, 8 * g + t:8 * g + t + 1]) for t in range(8)]
+        d = {(s, t): full(columns[t][s:s + 1]) for t in range(8) for s in range(t, 8)}
+        a = [full(left[g][t:t + 1]) for t in range(8)]
+        b = [full(right[g][t:t + 1]) for t in range(8)]
+        ratio, recip = {}, []
+        for t in range(8):
+            recip.append(1.0 / d[t, t])
+            for s in range(t + 1, 8):
+                ratio[s, t] = d[s, t] * recip[t]
+            for s in range(t + 1, 8):
+                for u in range(t + 1, s + 1):
+                    d[s, u] = d[s, u] - ratio[s, t] * d[u, t]
+                a[s] = a[s] - ratio[s, t] * a[t]
+                b[s] = b[s] - ratio[s, t] * b[t]
+        upper = inverse = jnp.zeros((8, ALL), jnp.float32)
+        for t in range(8):
+            scale = lax.rsqrt(d[t, t])
+            upper = jnp.where(sub == t, a[t] * scale, upper)
+            inverse = jnp.where(sub == t, b[t] * scale, inverse)
+        uppers.append(jnp.where(lane >= sub + 8 * g, upper, 0.0))
+        inverses.append(inverse)
+        a = [a[t] * recip[t] for t in range(8)]
+        b = [b[t] * recip[t] for t in range(8)]
+        for t in range(7, 0, -1):
+            for s in range(t):
+                a[s] = a[s] - ratio[t, s] * a[t]
+                b[s] = b[s] - ratio[t, s] * b[t]
+        for k in range(g + 1, groups):
+            below = [full(left[k][:, 8 * g + t:8 * g + t + 1]) for t in range(8)]
+            left[k] = left[k] - tree([below[t] * a[t] for t in range(8)])
+            right[k] = right[k] - tree([below[t] * b[t] for t in range(8)])
+    return jnp.concatenate(inverses, axis=0), jnp.concatenate(uppers, axis=0)
+
+
+def swap(rows, sub):
+    for k in (4, 2, 1):
+        low, new = (sub & k) == 0, list(rows)
+        for i in range(8):
+            if not i & k:
+                new[i] = jnp.where(low, rows[i], pltpu.roll(rows[i | k], k, 0))
+                new[i | k] = jnp.where(low, pltpu.roll(rows[i], 8 - k, 0), rows[i | k])
+        rows = new
+    return rows
+
+
+def basis(parts_ref, s_ref, q_hbm, alpha_ref, beta_ref, q_ref, sems):
     total = parts_ref[0]
     for i in range(1, parts_ref.shape[0]):
         total += parts_ref[i]
-    work = total * (1.0 / CELLS)
+    inverse, upper = factor(unpack(total * (1.0 / CELLS)))
     lane = lax.broadcasted_iota(jnp.int32, (ALL, ALL), 1)
-    sub = lax.broadcasted_iota(jnp.int32, (ALL, ALL), 0)
-    for j in range(ALL):
-        base = (j // 8) * 8
-        low = work[base:]
-        pivot = work[j:j + 1, j:j + 1]
-        row = jnp.where(lane[:1] == j, 1.0, work[j:j + 1])
-        ratio = jnp.where(sub[base:, :1] > j, low[:, j:j + 1] * (1.0 / pivot), 0.0)
-        kept = jnp.where((lane[base:] == j) & (sub[base:] > j), 0.0, low)
-        low = kept - ratio * row
-        work = low if base == 0 else jnp.concatenate([work[:base], low], axis=0)
-    pivots = jnp.sum(jnp.where(lane == sub, work, 0.0), axis=1, keepdims=True)
-    scale = lax.rsqrt(pivots)
-    inverse = scale * jnp.where(lane < sub, work, jnp.where(lane == sub, 1.0, 0.0))
-    upper = scale * jnp.where(lane >= sub, work, 0.0)
     own = jnp.where(lane < B, 1.0, jnp.where(lane < ITERS * B, 1.0 + SHIFT, 0.0))
     image = inverse * own + jnp.where(lane >= B, pltpu.roll(inverse, B, 1), 0.0)
     coeffs = lax.dot_general(upper, image, NT, precision=HIGH, preferred_element_type=jnp.float32)
@@ -162,18 +259,40 @@
         here, after = slice(k * B, (k + 1) * B), slice((k + 1) * B, (k + 2) * B)
         alpha_ref[k] = coeffs[here, here]
         beta_ref[k] = coeffs[after, here]
-    for i in range(0, LAT, 2):
-        pair = jnp.concatenate([s_ref[i], s_ref[i + 1]], axis=1)
-        new = jnp.dot(inverse, pair, precision=HIGH, preferred_element_type=jnp.float32)
-        q_ref[pl.ds(i, ALL, stride=LAT), :] = new[:, :LON]
-        q_ref[pl.ds(i + 1, ALL, stride=LAT), :] = new[:, LON:]
+    high, middle, low = split(inverse)
+    two = jnp.concatenate([high, middle], axis=1)
+    three = jnp.concatenate([high, middle, low], axis=1)
+    dot = lambda a, b: jnp.dot(a, b, preferred_element_type=jnp.float32)
+    sub = lax.broadcasted_iota(jnp.int32, (8, LON), 0)
+    copies = []
+    for g in range(LAT // 8):
+        rows = []
+        for i in range(8 * g, 8 * g + 8, 2):
+            a, b, c = split(jnp.concatenate([s_ref[i], s_ref[i + 1]], axis=1))
+            new = dot(three, jnp.concatenate([a, a, a], axis=0)) + dot(two, jnp.concatenate([b, b], axis=0)) + dot(high, c)
+            rows += [new[:, :LON], new[:, LON:]]
+        for v in range(0, ALL, 8):
+            for t, tile in enumerate(swap([row[v:v + 8] for row in rows], sub)):
+                q_ref[v + t, 8 * g:8 * g + 8, :] = tile
+        chunk = pl.ds(8 * g, 8)
+        copies.append(pltpu.make_async_copy(q_ref.at[:, chunk, :], q_hbm.at[:, chunk, :], sems.at[g]))
+        copies[-1].start()
+    for copy in copies:
+        copy.wait()
 
 
 def body(start_block, sea_mask, depth_levels):
     x = start_block.reshape(B * LAT, LON)
     edge = (RIM, B + 8, LON)
     side = (B + 8, LON)
-    top, bottom = call(edge_rows, (edge, edge))(x, sea_mask, depth_levels)
+    anywhere = pl.BlockSpec(memory_space=pl.ANY)
+    small = pltpu.VMEM((LAT, LON), jnp.int32)
+    top, bottom = call(
+        edge_rows,
+        (edge, edge),
+        [pltpu.VMEM((B * LAT, LON), jnp.float32), small, small, pltpu.SemaphoreType.DMA((3,))],
+        in_specs=[anywhere] * 3,
+    )(x, sea_mask, depth_levels)
     down = [(i, i + 1) for i in range(7)]
     up = [(i + 1, i) for i in range(7)]
     north = lax.ppermute(bottom, ROW, down)
@@ -188,16 +307,21 @@
     thin = (ROWS, 8, WIDE)
     s, gram = call(
         krylov,
-        ((LAT, ALL, LON), (ALL, ALL)),
+        ((LAT, ALL, LON), (B + 8, LON)),
         [pltpu.VMEM(wide, jnp.float32)] * 3 + [pltpu.VMEM(thin, jnp.float32)] * 3,
     )(core, north, south, from_west, from_east)
     pair = lax.all_gather(gram, "core")
-    copies = call(spread, ((16, ALL, ALL),))(pair)[0]
+    copies = call(spread, ((16, B + 8, LON),))(pair)[0]
     parts = lax.all_to_all(copies, ("x", "y"), 0, 0)
-    copies = call(spread, ((8, ALL, ALL),))(parts)[0]
+    copies = call(spread, ((8, B + 8, LON),))(parts)[0]
     parts = lax.all_to_all(copies, "z", 0, 0)
-    q, alphas, betas = call(basis, ((ALL * LAT, LON), (ITERS, B, B), (ITERS, B, B)))(parts, s)
-    return q.reshape(ALL, LAT, LON), alphas, betas
+    vmem = pl.BlockSpec(memory_space=pltpu.VMEM)
+    return call(
+        basis,
+        ((ALL, LAT, LON), (ITERS, B, B), (ITERS, B, B)),
+        [pltpu.VMEM((ALL, LAT, LON), jnp.float32), pltpu.SemaphoreType.DMA((LAT // 8,))],
+        out_specs=(anywhere, vmem, vmem),
+    )(parts, s)
 
 
 def solution(mesh):

time: 87.2 us -> 67.2 us (0.77)
  blocking collectives: 52.8 us -> 37.8 us
  Pallas kernels: 19.8 us -> 14.8 us
    all_to_all x1, blocking collectives: 25.8 us -> 17.6 us  [body(): parts = lax.all_to_all(copies, ('x', 'y'), 0, 0)]
    all_to_all x1, blocking collectives: 24 us -> 17.2 us  [body(): parts = lax.all_to_all(copies, 'z', 0, 0)]
    pallas_call x5, Pallas kernels: 19.1 us -> 14.1 us  [the longest x1 8.92 us: body(): call(basis, ((ALL, LAT, LON), (ITERS, B, B), (ITERS, B, B)), [pltpu.VMEM(...]
where the time goes in v3:
time: 67.2 us; the launch traced here: 66.8 us
  blocking collectives  37.8 us (56%)
  Pallas kernels  14.8 us (22%)
  waiting for transfers between devices  5.94 us (9%)
  starting transfers between devices  5.14 us (8%)
  local copies, waits for them, and re-layouts  2.47 us (4%)
  between operations  0.7 us (1%)
    all_to_all x1, blocking collectives, body(): parts = lax.all_to_all(copies, ('x', 'y'), 0, 0)  17.6 us
    all_to_all x1, blocking collectives, body(): parts = lax.all_to_all(copies, 'z', 0, 0)  17.2 us
    pallas_call x1, Pallas kernels, body(): call(basis, ((ALL, LAT, LON), (ITERS, B, B), (ITERS, B, B)), [pltpu.VMEM(...  8.92 us
    pallas_call x1, Pallas kernels, body(): call(krylov, ((LAT, ALL, LON), (B + 8, LON)), [pltpu.VMEM(wide, jnp.float...  5.01 us
    all_gather x1, blocking collectives, body(): pair = lax.all_gather(gram, 'core')  2.96 us
    ppermute x1, waiting for transfers between devices, body(): south = lax.ppermute(top, ROW, up)  2.6 us
    unnamed x6, local copies, waits for them, and re-layouts  2.47 us
    ppermute x1, waiting for transfers between devices, body(): from_west = lax.ppermute(east, COL, [(i, (i + 1) % 32) for i in range(32)])  1.76 us
  transfers between devices with their start and end apart: 4, of which 3 were waited for; matrix products, arithmetic and copies ran while one was open for 0% of the time, Pallas kernels for 1%

profile of v3, /device:TPU:8, one launch (start us, length us, event | category | flops | bytes accessed | tf_op | source)
XLA Modules:
  0.0 66.8 jit_solution(11620509896677887133)
XLA Ops:
  0.6 0.0 copy-start
  0.6 1.0 %copy-done = f32[32,32,128]{2,1,0:T(8,128)S(1)} copy-done((f32[32,32,128]{2,1,0:T(8,128)S(1)}, f32[32,32,128]{2,1,0:T(8,128)}, u32[]{:S(2)}) %copy-start) | copy-done | bytes 524312
  1.7 0.0 copy-start.1
  1.7 0.7 %copy-done.1 = s32[32,128]{1,0:T(8,128)S(1)} copy-done((s32[32,128]{1,0:T(8,128)S(1)}, s32[32,128]{1,0:T(8,128)}, u32[]{:S(2)}) %copy-start.1) | copy-done | bytes 16408
  2.4 0.0 copy-start.2
  2.4 0.7 %copy-done.2 = s32[32,128]{1,0:T(8,128)S(1)} copy-done((s32[32,128]{1,0:T(8,128)S(1)}, s32[32,128]{1,0:T(8,128)}, u32[]{:S(2)}) %copy-start.2) | copy-done | bytes 16408
  3.1 0.2 shard_map.59
  3.3 1.7 %collective-permute-start = (f32[3,40,128]{2,1,0:T(8,128)S(1)}, f32[3,40,128]{2,1,0:T(8,128)S(1)}, u32[]{:S(2)}, u32[]{:S(2)}) collective-permute-start(f32[3,40,128]{2,1,0:T(8,128)S(1)} %get-tuple-element.13), channel_id=1, source_target_pairs={{0,32},{32,64},{64,96},{96,128},{128,160},{160,192},{192,224},{1,3... | collective-permute-start | bytes 184328 | tf_op jit(solution)/shard_map/ppermute | solution.py:298
  5.0 1.3 %collective-permute-start.1 = (f32[3,40,128]{2,1,0:T(8,128)S(1)}, f32[3,40,128]{2,1,0:T(8,128)S(1)}, u32[]{:S(2)}, u32[]{:S(2)}) collective-permute-start(f32[3,40,128]{2,1,0:T(8,128)S(1)} %get-tuple-element.14), channel_id=1, source_target_pairs={{32,0},{64,32},{96,64},{128,96},{160,128},{192,160},{224,192},{33,... | collective-permute-start | bytes 184328 | tf_op jit(solution)/shard_map/ppermute | solution.py:299
  6.3 0.5 shard_map.58
  6.8 0.0 collective-permute-done.north_ref
  6.8 2.6 %collective-permute-done.1.south_ref = f32[3,40,128]{2,1,0:T(8,128)S(1)} collective-permute-done((f32[3,40,128]{2,1,0:T(8,128)S(1)}, f32[3,40,128]{2,1,0:T(8,128)S(1)}, u32[]{:S(2)}, u32[]{:S(2)}) %collective-permute-start.1) | collective-permute-done | bytes 61472 | tf_op jit(solution)/shard_map/ppermute | solution.py:299
  9.5 0.1 shard_map.60
  9.6 1.7 %collective-permute-start.2 = (f32[40,128]{1,0:T(8,128)S(1)}, f32[40,128]{1,0:T(8,128)S(1)}, u32[]{:S(2)}, u32[]{:S(2)}) collective-permute-start(f32[40,128]{1,0:T(8,128)S(1)} %get-tuple-element.17), channel_id=1, source_target_pairs={{0,1},{1,2},{2,3},{3,4},{4,5},{5,6},{6,7},{7,8},{8,9},{9,10},{10,1... | collective-permute-start | bytes 61448 | tf_op jit(solution)/shard_map/ppermute | solution.py:305
  11.2 0.4 collective-permute-start.3
  11.7 1.8 %collective-permute-done.2.west_ref = f32[40,128]{1,0:T(8,128)S(1)} collective-permute-done((f32[40,128]{1,0:T(8,128)S(1)}, f32[40,128]{1,0:T(8,128)S(1)}, u32[]{:S(2)}, u32[]{:S(2)}) %collective-permute-start.2) | collective-permute-done | bytes 20512 | tf_op jit(solution)/shard_map/ppermute | solution.py:305
  13.4 1.6 %collective-permute-done.3.east_ref = f32[40,128]{1,0:T(8,128)S(1)} collective-permute-done((f32[40,128]{1,0:T(8,128)S(1)}, f32[40,128]{1,0:T(8,128)S(1)}, u32[]{:S(2)}, u32[]{:S(2)}) %collective-permute-start.3) | collective-permute-done | bytes 20512 | tf_op jit(solution)/shard_map/ppermute | solution.py:304
  15.0 5.0 %shard_map.61 = (f32[32,128,128]{2,1,0:T(8,128)S(1)}, f32[40,128]{1,0:T(8,128)S(1)}) custom-call(f32[32,40,128]{2,1,0:T(8,128)S(1)} %get-tuple-element.12.core_ref, f32[3,40,128]{2,1,0:T(8,128)S(1)} %collective-permute-done.north_ref, f32[3,40,128]{2,1,0:T(8,128)S(1)} %collective-permute-done.1.south_ref, f32[40,128]{1,0:T(8,128)S(1)} %collective-permute-done.2.west_ref, ...), custom_call_target="tpu_custom_call" | custom-call | tf_op jit(solution)/shard_map/pallas_call | solution.py:308
  20.0 3.0 %all-gather = f32[80,128]{1,0:T(8,128)S(1)} all-gather(f32[40,128]{1,0:T(8,128)S(1)} %get-tuple-element.19), channel_id=2, replica_groups=mesh['x'=4,'core'=2,'z'=8,'y'=4] {'core'}, dimensions={0}, use_global_device_ids=true | all-gather | bytes 61440 | tf_op jit(solution)/shard_map/all_gather | solution.py:313
  23.0 17.6 %all_to_all.10.parts_ref = f32[16,40,128]{2,1,0:T(8,128)S(1)} all-to-all(f32[16,40,128]{2,1,0:T(8,128)S(1)} %shard_map.62), channel_id=1, replica_groups=mesh['x'=4,'core'=2,'z'=8,'y'=4] {'x','y'}, dimensions={0} | all-to-all | bytes 655360 | tf_op jit(solution)/shard_map/all_to_all | solution.py:315
  40.7 17.2 %all_to_all.11.parts_ref = f32[8,40,128]{2,1,0:T(8,128)S(1)} all-to-all(f32[8,40,128]{2,1,0:T(8,128)S(1)} %shard_map.63), channel_id=1, replica_groups=mesh['x'=4,'core'=2,'z'=8,'y'=4] {'z'}, dimensions={0} | all-to-all | bytes 327680 | tf_op jit(solution)/shard_map/all_to_all | solution.py:317
  57.9 8.9 %shard_map.64 = (f32[128,32,128]{2,1,0:T(8,128)}, f32[3,32,32]{2,1,0:T(8,128)}, f32[3,32,32]{2,1,0:T(8,128)}) custom-call(f32[8,40,128]{2,1,0:T(8,128)S(1)} %all_to_all.11.parts_ref, f32[32,128,128]{2,1,0:T(8,128)S(1)} %get-tuple-element.20.s_ref), custom_call_target="tpu_custom_call" | custom-call | tf_op jit(solution)/shard_map/pallas_call | solution.py:319
  (2 shorter events, 0.1 us)
Async XLA Ops:
  0.6 1.0 %copy-start = (f32[32,32,128]{2,1,0:T(8,128)S(1)}, f32[32,32,128]{2,1,0:T(8,128)}, u32[]{:S(2)}) copy-start(f32[32,32,128]{2,1,0:T(8,128)} %param.3) | copy-start | bytes 1572868
  1.7 0.7 %copy-start.1 = (s32[32,128]{1,0:T(8,128)S(1)}, s32[32,128]{1,0:T(8,128)}, u32[]{:S(2)}) copy-start(s32[32,128]{1,0:T(8,128)} %mask_hbm.1) | copy-start | bytes 49156
  2.4 0.7 %copy-start.2 = (s32[32,128]{1,0:T(8,128)S(1)}, s32[32,128]{1,0:T(8,128)}, u32[]{:S(2)}) copy-start(s32[32,128]{1,0:T(8,128)} %depth_hbm.1) | copy-start | bytes 49156
  3.3 3.6 %collective-permute-start = (f32[3,40,128]{2,1,0:T(8,128)S(1)}, f32[3,40,128]{2,1,0:T(8,128)S(1)}, u32[]{:S(2)}, u32[]{:S(2)}) collective-permute-start(f32[3,40,128]{2,1,0:T(8,128)S(1)} %get-tuple-element.13), channel_id=1, source_target_pairs={{0,32},{32,64},{64,96},{96,128},{128,160},{160,192},{192,224},{1,3... | collective-permute-start | bytes 184328 | tf_op jit(solution)/shard_map/ppermute | solution.py:298
  5.0 4.4 %collective-permute-start.1 = (f32[3,40,128]{2,1,0:T(8,128)S(1)}, f32[3,40,128]{2,1,0:T(8,128)S(1)}, u32[]{:S(2)}, u32[]{:S(2)}) collective-permute-start(f32[3,40,128]{2,1,0:T(8,128)S(1)} %get-tuple-element.14), channel_id=1, source_target_pairs={{32,0},{64,32},{96,64},{128,96},{160,128},{192,160},{224,192},{33,... | collective-permute-start | bytes 184328 | tf_op jit(solution)/shard_map/ppermute | solution.py:299
  9.6 3.9 %collective-permute-start.2 = (f32[40,128]{1,0:T(8,128)S(1)}, f32[40,128]{1,0:T(8,128)S(1)}, u32[]{:S(2)}, u32[]{:S(2)}) collective-permute-start(f32[40,128]{1,0:T(8,128)S(1)} %get-tuple-element.17), channel_id=1, source_target_pairs={{0,1},{1,2},{2,3},{3,4},{4,5},{5,6},{6,7},{7,8},{8,9},{9,10},{10,1... | collective-permute-start | bytes 61448 | tf_op jit(solution)/shard_map/ppermute | solution.py:305
  11.2 3.8 %collective-permute-start.3 = (f32[40,128]{1,0:T(8,128)S(1)}, f32[40,128]{1,0:T(8,128)S(1)}, u32[]{:S(2)}, u32[]{:S(2)}) collective-permute-start(f32[40,128]{1,0:T(8,128)S(1)} %get-tuple-element.18), channel_id=1, source_target_pairs={{1,0},{2,1},{3,2},{4,3},{5,4},{6,5},{7,6},{8,7},{9,8},{10,9},{11,1... | collective-permute-start | bytes 61448 | tf_op jit(solution)/shard_map/ppermute | solution.py:304

commit v4 on v3

--- a/solution.py
+++ b/solution.py
@@ -46,16 +46,22 @@
     return jnp.concatenate([row, jnp.broadcast_to(depth, (8, LON))], axis=0)
 
 
-def edge_rows(x_hbm, mask_hbm, depth_hbm, top_ref, bottom_ref, x_ref, mask_ref, depth_ref, sems):
-    pairs = ((x_hbm, x_ref), (mask_hbm, mask_ref), (depth_hbm, depth_ref))
-    copies = [pltpu.make_async_copy(source, target, sems.at[i]) for i, (source, target) in enumerate(pairs)]
+def load(sources, targets, sems):
+    copies = [pltpu.make_async_copy(a, b, sems.at[i]) for i, (a, b) in enumerate(zip(sources, targets))]
     for copy in copies:
         copy.start()
     for copy in copies:
         copy.wait()
+
+
+def edge_rows(x_hbm, mask_hbm, depth_hbm, near_ref, far_ref, x_ref, mask_ref, depth_ref, sems):
+    load((x_hbm, mask_hbm, depth_hbm), (x_ref, mask_ref, depth_ref), sems)
+    odd = lax.axis_index("core") == 1
     for i in range(RIM):
-        top_ref[i] = masked_row(i, x_ref, mask_ref, depth_ref)
-        bottom_ref[i] = masked_row(LAT - RIM + i, x_ref, mask_ref, depth_ref)
+        top = masked_row(i, x_ref, mask_ref, depth_ref)
+        bottom = masked_row(LAT - RIM + i, x_ref, mask_ref, depth_ref)
+        near_ref[i] = jnp.where(odd, top, bottom)
+        far_ref[i] = jnp.where(odd, bottom, top)
 
 
 def pack_sides(row, r, west, east):
@@ -66,7 +72,8 @@
     return west, east
 
 
-def core_rows(x_ref, mask_ref, depth_ref, core_ref, west_ref, east_ref):
+def core_rows(x_hbm, mask_hbm, depth_hbm, core_ref, west_ref, east_ref, x_ref, mask_ref, depth_ref, sems):
+    load((x_hbm, mask_hbm, depth_hbm), (x_ref, mask_ref, depth_ref), sems)
     west = east = jnp.zeros((B + 8, LON), jnp.float32)
     for i in range(LAT):
         row = masked_row(i, x_ref, mask_ref, depth_ref)
@@ -76,13 +83,19 @@
     east_ref[...] = east
 
 
-def side_columns(north_ref, south_ref, part_west_ref, part_east_ref, west_ref, east_ref):
+def side_columns(near_ref, far_ref, part_west_ref, part_east_ref, near_out, far_out, north_ref, south_ref):
+    odd = lax.axis_index("core") == 1
     west, east = part_west_ref[...], part_east_ref[...]
     for i in range(RIM):
-        west, east = pack_sides(north_ref[i], i, west, east)
-        west, east = pack_sides(south_ref[i], i + RIM + LAT, west, east)
-    west_ref[...] = west
-    east_ref[...] = east
+        north = jnp.where(odd, near_ref[i], far_ref[i])
+        south = jnp.where(odd, far_ref[i], near_ref[i])
+        north_ref[i] = north
+        south_ref[i] = south
+        west, east = pack_sides(north, i, west, east)
+        west, east = pack_sides(south, i + RIM + LAT, west, east)
+    odd = lax.axis_index("y") % 2 == 1
+    near_out[...] = jnp.where(odd, west, east)
+    far_out[...] = jnp.where(odd, east, west)
 
 
 def split(value):
@@ -97,10 +110,12 @@
     return jnp.concatenate([field] * (B // 8), axis=0)
 
 
-def krylov(core_ref, north_ref, south_ref, west_ref, east_ref, s_ref, gram_ref,
+def krylov(core_ref, north_ref, south_ref, near_ref, far_ref, s_ref, gram_ref,
            x_ref, k1_ref, k2_ref, h_ref, down_ref, right_ref):
     lane = lanes_of(B + 8)
-    from_west, from_east = west_ref[...], east_ref[...]
+    odd = lax.axis_index("y") % 2 == 1
+    near, far = near_ref[...], far_ref[...]
+    from_west, from_east = jnp.where(odd, near, far), jnp.where(odd, far, near)
     for r in range(ROWS):
         if r < RIM:
             row = north_ref[r]
@@ -113,13 +128,13 @@
         full = jnp.concatenate([row, beyond], axis=1)
         x_ref[r] = full[:B]
         h_ref[r] = full[B:]
-    for r in range(ROWS):
+        if RIM <= r < RIM + LAT:
+            s_ref[r - RIM, :B, :] = row[:B]
+
+    for r in range(ROWS - 1):
         h = h_ref[r]
-        if r + 1 < ROWS:
-            down_ref[r] = KAPPA * jnp.minimum(h, h_ref[r + 1])
+        down_ref[r] = KAPPA * jnp.minimum(h, h_ref[r + 1])
         right_ref[r] = KAPPA * jnp.minimum(h, pltpu.roll(h, WIDE - 1, 1))
-    for i in range(LAT):
-        s_ref[i, :B, :] = x_ref[i + RIM][:, :LON]
     levels = ((x_ref, k1_ref, 1.0), (k1_ref, k2_ref, 1.0 + SHIFT), (k2_ref, None, 1.0 + SHIFT))
     for step, (source, target, shift) in enumerate(levels):
         first, last = step + 1, ROWS - 2 - step
@@ -287,29 +302,24 @@
     side = (B + 8, LON)
     anywhere = pl.BlockSpec(memory_space=pl.ANY)
     small = pltpu.VMEM((LAT, LON), jnp.int32)
-    top, bottom = call(
-        edge_rows,
-        (edge, edge),
-        [pltpu.VMEM((B * LAT, LON), jnp.float32), small, small, pltpu.SemaphoreType.DMA((3,))],
-        in_specs=[anywhere] * 3,
+    inputs = dict(in_specs=[pl.BlockSpec(memory_space=pltpu.HBM)] * 3)
+    room = [pltpu.VMEM((B * LAT, LON), jnp.float32), small, small, pltpu.SemaphoreType.DMA((3,))]
+    near, far = call(edge_rows, (edge, edge), room, **inputs)(x, sea_mask, depth_levels)
+    near = lax.ppermute(near, ROW, [(i, i ^ 1) for i in range(8)])
+    far = lax.ppermute(far, ROW, [(i, ((i + 1) ^ 1) - 1) for i in range(1, 7)])
+    core, part_west, part_east = call(
+        core_rows, ((LAT, B + 8, LON), side, side), room, flops=1 << 22, moved=1 << 20, **inputs
     )(x, sea_mask, depth_levels)
-    down = [(i, i + 1) for i in range(7)]
-    up = [(i + 1, i) for i in range(7)]
-    north = lax.ppermute(bottom, ROW, down)
-    south = lax.ppermute(top, ROW, up)
-    core, part_west, part_east = call(core_rows, ((LAT, B + 8, LON), side, side), flops=1 << 22, moved=1 << 20)(
-        x, sea_mask, depth_levels
-    )
-    west, east = call(side_columns, (side, side))(north, south, part_west, part_east)
-    from_east = lax.ppermute(west, COL, [((i + 1) % 32, i) for i in range(32)])
-    from_west = lax.ppermute(east, COL, [(i, (i + 1) % 32) for i in range(32)])
+    near, far, north, south = call(side_columns, (side, side, edge, edge))(near, far, part_west, part_east)
+    near = lax.ppermute(near, COL, [(i, i ^ 1) for i in range(32)])
+    far = lax.ppermute(far, COL, [(i, (((i + 1) ^ 1) - 1) % 32) for i in range(32)])
     wide = (ROWS, B, WIDE)
     thin = (ROWS, 8, WIDE)
     s, gram = call(
         krylov,
         ((LAT, ALL, LON), (B + 8, LON)),
         [pltpu.VMEM(wide, jnp.float32)] * 3 + [pltpu.VMEM(thin, jnp.float32)] * 3,
-    )(core, north, south, from_west, from_east)
+    )(core, north, south, near, far)
     pair = lax.all_gather(gram, "core")
     copies = call(spread, ((16, B + 8, LON),))(pair)[0]
     parts = lax.all_to_all(copies, ("x", "y"), 0, 0)

time: 67.2 us -> 64.6 us (0.961)
  waiting for transfers between devices: 5.94 us -> 3.11 us
  blocking collectives: 37.8 us -> 39.3 us
  starting transfers between devices: 5.14 us -> 3.7 us
    ppermute x4, waiting for transfers between devices: 5.94 us -> 3.11 us  [the longest x1 2.02 us: body(): lax.ppermute(far, COL, [(i, ((i + 1 ^ 1) - 1) % 32) for i in range(32)])]
    all_gather x1, blocking collectives: 2.96 us -> 4.76 us  [body(): pair = lax.all_gather(gram, 'core')]
    ppermute x4, starting transfers between devices: 5.14 us -> 3.7 us  [the longest x1 2.27 us: body(): near = lax.ppermute(near, COL, [(i, i ^ 1) for i in range(32)])]
    all_to_all x1, blocking collectives: 17.2 us -> 16 us  [body(): parts = lax.all_to_all(copies, 'z', 0, 0)]
    all_to_all x1, blocking collectives: 17.6 us -> 18.6 us  [body(): parts = lax.all_to_all(copies, ('x', 'y'), 0, 0)]
  transfers between devices with their start and end apart: 4 -> 4, of which waited for: 3 -> 2; matrix products, arithmetic and copies ran while one was open for 0% -> 0% of each run, Pallas kernels for 1% -> 1%
where the time goes in v4:
time: 64.6 us; the launch traced here: 64.2 us
  blocking collectives  39.3 us (61%)
  Pallas kernels  14.9 us (23%)
  starting transfers between devices  3.7 us (6%)
  waiting for transfers between devices  3.11 us (5%)
  local copies, waits for them, and re-layouts  2.47 us (4%)
  between operations  0.71 us (1%)
    all_to_all x1, blocking collectives, body(): parts = lax.all_to_all(copies, ('x', 'y'), 0, 0)  18.6 us
    all_to_all x1, blocking collectives, body(): parts = lax.all_to_all(copies, 'z', 0, 0)  16 us
    pallas_call x1, Pallas kernels, body(): call(basis, ((ALL, LAT, LON), (ITERS, B, B), (ITERS, B, B)), [pltpu.VMEM(...  8.92 us
    pallas_call x1, Pallas kernels, body(): call(krylov, ((LAT, ALL, LON), (B + 8, LON)), [pltpu.VMEM(wide, jnp.float...  5.01 us
    all_gather x1, blocking collectives, body(): pair = lax.all_gather(gram, 'core')  4.76 us
    unnamed x6, local copies, waits for them, and re-layouts  2.47 us
    ppermute x1, starting transfers between devices, body(): near = lax.ppermute(near, COL, [(i, i ^ 1) for i in range(32)])  2.27 us
    ppermute x1, waiting for transfers between devices, body(): lax.ppermute(far, COL, [(i, ((i + 1 ^ 1) - 1) % 32) for i in range(32)])  2.02 us
  transfers between devices with their start and end apart: 4, of which 2 were waited for; matrix products, arithmetic and copies ran while one was open for 0% of the time, Pallas kernels for 1%

profile of v4, /device:TPU:8, one launch (start us, length us, event | category | flops | bytes accessed | tf_op | source)
XLA Modules:
  0.0 64.2 jit_solution(10236328026349101037)
XLA Ops:
  0.6 0.0 copy-start
  0.6 1.0 %copy-done = f32[32,32,128]{2,1,0:T(8,128)S(1)} copy-done((f32[32,32,128]{2,1,0:T(8,128)S(1)}, f32[32,32,128]{2,1,0:T(8,128)}, u32[]{:S(2)}) %copy-start) | copy-done | bytes 524312
  1.7 0.0 copy-start.1
  1.7 0.7 %copy-done.1 = s32[32,128]{1,0:T(8,128)S(1)} copy-done((s32[32,128]{1,0:T(8,128)S(1)}, s32[32,128]{1,0:T(8,128)}, u32[]{:S(2)}) %copy-start.1) | copy-done | bytes 16408
  2.4 0.0 copy-start.2
  2.4 0.7 %copy-done.2 = s32[32,128]{1,0:T(8,128)S(1)} copy-done((s32[32,128]{1,0:T(8,128)S(1)}, s32[32,128]{1,0:T(8,128)}, u32[]{:S(2)}) %copy-start.2) | copy-done | bytes 16408
  3.1 0.2 shard_map.59
  3.3 0.1 collective-permute-start
  3.4 0.7 %collective-permute-start.1 = (f32[3,40,128]{2,1,0:T(8,128)S(1)}, f32[3,40,128]{2,1,0:T(8,128)S(1)}, u32[]{:S(2)}, u32[]{:S(2)}) collective-permute-start(f32[3,40,128]{2,1,0:T(8,128)S(1)} %get-tuple-element.16), channel_id=1, source_target_pairs={{32,64},{64,32},{96,128},{128,96},{160,192},{192,160},{33,65},{65,... | collective-permute-start | bytes 184328 | tf_op jit(solution)/shard_map/ppermute | solution.py:309
  4.1 0.6 shard_map.58
  4.7 0.0 collective-permute-done.near_ref
  4.7 0.0 collective-permute-done.1.far_ref
  4.7 0.1 shard_map.60
  4.8 2.3 %collective-permute-start.2 = (f32[40,128]{1,0:T(8,128)S(1)}, f32[40,128]{1,0:T(8,128)S(1)}, u32[]{:S(2)}, u32[]{:S(2)}) collective-permute-start(f32[40,128]{1,0:T(8,128)S(1)} %get-tuple-element.21), channel_id=1, source_target_pairs={{0,1},{1,0},{2,3},{3,2},{4,5},{5,4},{6,7},{7,6},{8,9},{9,8},{10,11... | collective-permute-start | bytes 61448 | tf_op jit(solution)/shard_map/ppermute | solution.py:314
  7.1 0.7 %collective-permute-start.3 = (f32[40,128]{1,0:T(8,128)S(1)}, f32[40,128]{1,0:T(8,128)S(1)}, u32[]{:S(2)}, u32[]{:S(2)}) collective-permute-start(f32[40,128]{1,0:T(8,128)S(1)} %get-tuple-element.22), channel_id=1, source_target_pairs={{0,31},{1,2},{2,1},{3,4},{4,3},{5,6},{6,5},{7,8},{8,7},{9,10},{10,... | collective-permute-start | bytes 61448 | tf_op jit(solution)/shard_map/ppermute | solution.py:315
  7.8 1.1 %collective-permute-done.2.near_ref = f32[40,128]{1,0:T(8,128)S(1)} collective-permute-done((f32[40,128]{1,0:T(8,128)S(1)}, f32[40,128]{1,0:T(8,128)S(1)}, u32[]{:S(2)}, u32[]{:S(2)}) %collective-permute-start.2) | collective-permute-done | bytes 20512 | tf_op jit(solution)/shard_map/ppermute | solution.py:314
  8.9 2.0 %collective-permute-done.3.far_ref = f32[40,128]{1,0:T(8,128)S(1)} collective-permute-done((f32[40,128]{1,0:T(8,128)S(1)}, f32[40,128]{1,0:T(8,128)S(1)}, u32[]{:S(2)}, u32[]{:S(2)}) %collective-permute-start.3) | collective-permute-done | bytes 20512 | tf_op jit(solution)/shard_map/ppermute | solution.py:315
  10.9 5.0 %shard_map.61 = (f32[32,128,128]{2,1,0:T(8,128)S(1)}, f32[40,128]{1,0:T(8,128)S(1)}) custom-call(f32[32,40,128]{2,1,0:T(8,128)S(1)} %get-tuple-element.14.core_ref, f32[3,40,128]{2,1,0:T(8,128)S(1)} %get-tuple-element.19.north_ref, f32[3,40,128]{2,1,0:T(8,128)S(1)} %get-tuple-element.20.south_ref, f32[40,128]{1,0:T(8,128)S(1)} %collective-permute-done.2.near_ref, ...), custom_call_target="tpu_custom_call" | custom-call | tf_op jit(solution)/shard_map/pallas_call | solution.py:318
  15.9 4.8 %all-gather = f32[80,128]{1,0:T(8,128)S(1)} all-gather(f32[40,128]{1,0:T(8,128)S(1)} %get-tuple-element.23), channel_id=2, replica_groups=mesh['x'=4,'core'=2,'z'=8,'y'=4] {'core'}, dimensions={0}, use_global_device_ids=true | all-gather | bytes 61440 | tf_op jit(solution)/shard_map/all_gather | solution.py:323
  20.7 18.6 %all_to_all.10.parts_ref = f32[16,40,128]{2,1,0:T(8,128)S(1)} all-to-all(f32[16,40,128]{2,1,0:T(8,128)S(1)} %shard_map.62), channel_id=1, replica_groups=mesh['x'=4,'core'=2,'z'=8,'y'=4] {'x','y'}, dimensions={0} | all-to-all | bytes 655360 | tf_op jit(solution)/shard_map/all_to_all | solution.py:325
  39.3 16.0 %all_to_all.11.parts_ref = f32[8,40,128]{2,1,0:T(8,128)S(1)} all-to-all(f32[8,40,128]{2,1,0:T(8,128)S(1)} %shard_map.63), channel_id=1, replica_groups=mesh['x'=4,'core'=2,'z'=8,'y'=4] {'z'}, dimensions={0} | all-to-all | bytes 327680 | tf_op jit(solution)/shard_map/all_to_all | solution.py:327
  55.3 8.9 %shard_map.64 = (f32[128,32,128]{2,1,0:T(8,128)}, f32[3,32,32]{2,1,0:T(8,128)}, f32[3,32,32]{2,1,0:T(8,128)}) custom-call(f32[8,40,128]{2,1,0:T(8,128)S(1)} %all_to_all.11.parts_ref, f32[32,128,128]{2,1,0:T(8,128)S(1)} %get-tuple-element.24.s_ref), custom_call_target="tpu_custom_call" | custom-call | tf_op jit(solution)/shard_map/pallas_call | solution.py:329
  (2 shorter events, 0.1 us)
Async XLA Ops:
  0.6 1.0 %copy-start = (f32[32,32,128]{2,1,0:T(8,128)S(1)}, f32[32,32,128]{2,1,0:T(8,128)}, u32[]{:S(2)}) copy-start(f32[32,32,128]{2,1,0:T(8,128)} %param.3) | copy-start | bytes 1572868
  1.7 0.7 %copy-start.1 = (s32[32,128]{1,0:T(8,128)S(1)}, s32[32,128]{1,0:T(8,128)}, u32[]{:S(2)}) copy-start(s32[32,128]{1,0:T(8,128)} %mask_hbm.3) | copy-start | bytes 49156
  2.4 0.7 %copy-start.2 = (s32[32,128]{1,0:T(8,128)S(1)}, s32[32,128]{1,0:T(8,128)}, u32[]{:S(2)}) copy-start(s32[32,128]{1,0:T(8,128)} %depth_hbm.3) | copy-start | bytes 49156
  3.3 1.4 %collective-permute-start = (f32[3,40,128]{2,1,0:T(8,128)S(1)}, f32[3,40,128]{2,1,0:T(8,128)S(1)}, u32[]{:S(2)}, u32[]{:S(2)}) collective-permute-start(f32[3,40,128]{2,1,0:T(8,128)S(1)} %get-tuple-element.15), channel_id=1, source_target_pairs={{0,32},{32,0},{64,96},{96,64},{128,160},{160,128},{192,224},{224,1... | collective-permute-start | bytes 184328 | tf_op jit(solution)/shard_map/ppermute | solution.py:308
  3.4 1.3 %collective-permute-start.1 = (f32[3,40,128]{2,1,0:T(8,128)S(1)}, f32[3,40,128]{2,1,0:T(8,128)S(1)}, u32[]{:S(2)}, u32[]{:S(2)}) collective-permute-start(f32[3,40,128]{2,1,0:T(8,128)S(1)} %get-tuple-element.16), channel_id=1, source_target_pairs={{32,64},{64,32},{96,128},{128,96},{160,192},{192,160},{33,65},{65,... | collective-permute-start | bytes 184328 | tf_op jit(solution)/shard_map/ppermute | solution.py:309
  4.8 4.0 %collective-permute-start.2 = (f32[40,128]{1,0:T(8,128)S(1)}, f32[40,128]{1,0:T(8,128)S(1)}, u32[]{:S(2)}, u32[]{:S(2)}) collective-permute-start(f32[40,128]{1,0:T(8,128)S(1)} %get-tuple-element.21), channel_id=1, source_target_pairs={{0,1},{1,0},{2,3},{3,2},{4,5},{5,4},{6,7},{7,6},{8,9},{9,8},{10,11... | collective-permute-start | bytes 61448 | tf_op jit(solution)/shard_map/ppermute | solution.py:314
  7.1 3.8 %collective-permute-start.3 = (f32[40,128]{1,0:T(8,128)S(1)}, f32[40,128]{1,0:T(8,128)S(1)}, u32[]{:S(2)}, u32[]{:S(2)}) collective-permute-start(f32[40,128]{1,0:T(8,128)S(1)} %get-tuple-element.22), channel_id=1, source_target_pairs={{0,31},{1,2},{2,1},{3,4},{4,3},{5,6},{6,5},{7,8},{8,7},{9,10},{10,... | collective-permute-start | bytes 61448 | tf_op jit(solution)/shard_map/ppermute | solution.py:315

commit v5 on v4

--- a/solution.py
+++ b/solution.py
@@ -16,7 +16,8 @@
 LON = 128
 RIM = 3
 ROWS = LAT + 2 * RIM
-WIDE = 2 * LON
+SPAN = 3 * RIM
+FLAT = 3 * LON
 ALL = (ITERS + 1) * B
 HIGH = lax.Precision.HIGHEST
 ROW, COL = ("x", "core"), ("z", "y")
@@ -66,36 +67,46 @@
 
 def pack_sides(row, r, west, east):
     lane = lanes_of(B + 8)
-    here = (lane >= RIM * r) & (lane < RIM * r + RIM)
-    west = jnp.where(here, pltpu.roll(row, (RIM * r) % LON, 1), west)
-    east = jnp.where(here, pltpu.roll(row, (RIM * r + RIM) % LON, 1), east)
-    return west, east
+    for sides, source, target in ((west, 0, SPAN * r + RIM), (east, LON - 2 * RIM, SPAN * r)):
+        moved = pltpu.roll(row, (target - source) % LON, 1)
+        for k in range(target // LON, (target + 2 * RIM - 1) // LON + 1):
+            place = lane + k * LON
+            sides[k] = jnp.where((place >= target) & (place < target + 2 * RIM), moved, sides[k])
+
+
+def chunks(flat):
+    return [flat[:, k * LON:(k + 1) * LON] for k in range(FLAT // LON)]
 
 
 def core_rows(x_hbm, mask_hbm, depth_hbm, core_ref, west_ref, east_ref, x_ref, mask_ref, depth_ref, sems):
     load((x_hbm, mask_hbm, depth_hbm), (x_ref, mask_ref, depth_ref), sems)
-    west = east = jnp.zeros((B + 8, LON), jnp.float32)
+    west, east = chunks(jnp.zeros((B + 8, FLAT), jnp.float32)), chunks(jnp.zeros((B + 8, FLAT), jnp.float32))
     for i in range(LAT):
         row = masked_row(i, x_ref, mask_ref, depth_ref)
         core_ref[i] = row
-        west, east = pack_sides(row, i + RIM, west, east)
-    west_ref[...] = west
-    east_ref[...] = east
-
-
-def side_columns(near_ref, far_ref, part_west_ref, part_east_ref, near_out, far_out, north_ref, south_ref):
+        pack_sides(row, i + RIM, west, east)
+    west_ref[...] = jnp.concatenate(west, axis=1)
+    east_ref[...] = jnp.concatenate(east, axis=1)
+
+
+def side_columns(near_ref, far_ref, part_west_ref, part_east_ref,
+                 near_out, far_out, north_ref, south_ref, west_ref, east_ref):
     odd = lax.axis_index("core") == 1
-    west, east = part_west_ref[...], part_east_ref[...]
+    west, east = chunks(part_west_ref[...]), chunks(part_east_ref[...])
     for i in range(RIM):
         north = jnp.where(odd, near_ref[i], far_ref[i])
         south = jnp.where(odd, far_ref[i], near_ref[i])
         north_ref[i] = north
         south_ref[i] = south
-        west, east = pack_sides(north, i, west, east)
-        west, east = pack_sides(south, i + RIM + LAT, west, east)
+        pack_sides(north, i, west, east)
+        pack_sides(south, i + RIM + LAT, west, east)
+    west, east = jnp.concatenate(west, axis=1), jnp.concatenate(east, axis=1)
+    west_ref[...] = west
+    east_ref[...] = east
+    to_west, to_east = pltpu.roll(west, RIM, 1), pltpu.roll(east, FLAT - RIM, 1)
     odd = lax.axis_index("y") % 2 == 1
-    near_out[...] = jnp.where(odd, west, east)
-    far_out[...] = jnp.where(odd, east, west)
+    near_out[...] = jnp.where(odd, to_west, to_east)
+    far_out[...] = jnp.where(odd, to_east, to_west)
 
 
 def split(value):
@@ -110,54 +121,92 @@
     return jnp.concatenate([field] * (B // 8), axis=0)
 
 
-def krylov(core_ref, north_ref, south_ref, near_ref, far_ref, s_ref, gram_ref,
-           x_ref, k1_ref, k2_ref, h_ref, down_ref, right_ref):
-    lane = lanes_of(B + 8)
-    odd = lax.axis_index("y") % 2 == 1
-    near, far = near_ref[...], far_ref[...]
-    from_west, from_east = jnp.where(odd, near, far), jnp.where(odd, far, near)
-    for r in range(ROWS):
+def outer(left, right):
+    return lax.dot_general(left, right, NT, preferred_element_type=jnp.float32)
+
+
+def products(value):
+    high, middle, low = split(value)
+    both = outer(high, jnp.concatenate([high, middle], axis=0))
+    return both[:, :ALL] + outer(middle, middle), both[:, ALL:] + outer(high, low)
+
+
+def inside(core_ref, north_ref, south_ref, s_ref, even_ref, half_ref, k1_ref, k2_ref, down_ref, right_ref, centre_ref):
+    def base(r):
         if r < RIM:
-            row = north_ref[r]
-        elif r < RIM + LAT:
-            row = core_ref[r - RIM]
-        else:
-            row = south_ref[r - RIM - LAT]
-        beyond = jnp.where(lane < RIM, pltpu.roll(from_east, (-RIM * r) % LON, 1), 0.0)
-        beyond = jnp.where(lane >= LON - RIM, pltpu.roll(from_west, (LON - RIM - RIM * r) % LON, 1), beyond)
-        full = jnp.concatenate([row, beyond], axis=1)
-        x_ref[r] = full[:B]
-        h_ref[r] = full[B:]
-        if RIM <= r < RIM + LAT:
-            s_ref[r - RIM, :B, :] = row[:B]
+            return north_ref[r]
+        return core_ref[r - RIM] if r < RIM + LAT else south_ref[r - RIM - LAT]
 
     for r in range(ROWS - 1):
-        h = h_ref[r]
-        down_ref[r] = KAPPA * jnp.minimum(h, h_ref[r + 1])
-        right_ref[r] = KAPPA * jnp.minimum(h, pltpu.roll(h, WIDE - 1, 1))
-    levels = ((x_ref, k1_ref, 1.0), (k1_ref, k2_ref, 1.0 + SHIFT), (k2_ref, None, 1.0 + SHIFT))
+        h = base(r)[B:]
+        down_ref[r] = KAPPA * jnp.minimum(h, base(r + 1)[B:])
+        right_ref[r] = KAPPA * jnp.minimum(h, pltpu.roll(h, LON - 1, 1))
+        centre_ref[r] = jnp.where(h > 0.0, 0.0, -1.0)
+    levels = (
+        (lambda r: base(r)[:B], k1_ref, 0.0),
+        (lambda r: k1_ref[r], k2_ref, SHIFT),
+        (lambda r: k2_ref[r], None, SHIFT),
+    )
     for step, (source, target, shift) in enumerate(levels):
         first, last = step + 1, ROWS - 2 - step
-        flux = four(down_ref[first - 1]) * (source[first - 1] - source[first])
+        v, after = source(first - 1), source(first)
+        flux = four(down_ref[first - 1]) * (v - after)
         for r in range(first, last + 1):
-            v = source[r]
-            centre = jnp.where(h_ref[r] > 0.0, 1.0 - shift, -shift)
-            down = four(down_ref[r]) * (v - source[r + 1])
-            right = four(right_ref[r]) * (v - pltpu.roll(v, WIDE - 1, 1))
-            new = four(centre) * v + ((down - flux) + (right - pltpu.roll(right, 1, 1)))
+            v, after = after, source(r + 1)
+            down = four(down_ref[r]) * (v - after)
+            right = four(right_ref[r]) * (v - pltpu.roll(v, LON - 1, 1))
+            new = four(centre_ref[r] - shift) * v + ((down - flux) + (right - pltpu.roll(right, 1, 1)))
             flux = down
             if target is not None:
                 target[r] = new
             if RIM <= r < RIM + LAT:
-                s_ref[r - RIM, (step + 1) * B:(step + 2) * B, :] = new[:, :LON]
-    outer = lambda left, right: lax.dot_general(left, right, NT, preferred_element_type=jnp.float32)
-    large = small = jnp.zeros((ALL, 2 * ALL), jnp.float32)
+                s_ref[r - RIM, (step + 1) * B:(step + 2) * B, :] = new
+    lane = lanes_of(ALL)
+    clean = (lane >= RIM) & (lane < LON - RIM)
+    even = half = jnp.zeros((ALL, ALL), jnp.float32)
     for i in range(0, LAT, 2):
-        high, middle, low = split(jnp.concatenate([s_ref[i], s_ref[i + 1]], axis=1))
-        large += outer(high, jnp.concatenate([high, middle], axis=0))
-        small += jnp.concatenate([outer(high, low), outer(middle, middle)], axis=1)
-    half = large[:, ALL:] + small[:, :ALL]
-    gram = large[:, :ALL] + small[:, ALL:] + half + half.T
+        rows = []
+        for j in (i, i + 1):
+            s_ref[j, :B, :] = core_ref[j, :B]
+            rows.append(jnp.where(clean, s_ref[j], 0.0))
+        one, two = products(jnp.concatenate(rows, axis=1))
+        even += one
+        half += two
+    even_ref[...] = even
+    half_ref[...] = half
+
+
+def border(near_ref, far_ref, own_west_ref, own_east_ref, even_ref, half_ref, gram_ref, west_ref, east_ref):
+    odd = lax.axis_index("y") % 2 == 1
+    near, far = near_ref[...], far_ref[...]
+    lane = lax.broadcasted_iota(jnp.int32, (B + 8, FLAT), 1)
+    line = (lane * 7282) >> 16
+    place = lane - line * SPAN
+    west = jnp.where(place < RIM, jnp.where(odd, near, far), own_west_ref[...])
+    east = jnp.where(place >= 2 * RIM, jnp.where(odd, far, near), own_east_ref[...])
+    joint = place[:8] < SPAN - 1
+    kept = (place[:1] >= RIM) & (place[:1] < 2 * RIM) & (line[:1] >= RIM) & (line[:1] < RIM + LAT)
+    fields = []
+    for start, out_ref in ((west, west_ref), (east, east_ref)):
+        h = start[B:]
+        down = four(KAPPA * jnp.minimum(h, pltpu.roll(h, FLAT - SPAN, 1)))
+        right = four(jnp.where(joint, KAPPA * jnp.minimum(h, pltpu.roll(h, FLAT - 1, 1)), 0.0))
+        centre = jnp.where(h > 0.0, 0.0, -1.0)
+        v = start[:B]
+        found = [v]
+        for shift in (0.0, SHIFT, SHIFT):
+            flow = down * (v - pltpu.roll(v, FLAT - SPAN, 1))
+            side = right * (v - pltpu.roll(v, FLAT - 1, 1))
+            v = four(centre - shift) * v + (
+                (flow - pltpu.roll(flow, SPAN, 1)) + (side - pltpu.roll(side, 1, 1))
+            )
+            found.append(v)
+        out_ref[...] = jnp.concatenate(found[1:], axis=0)
+        fields.append(jnp.where(kept, jnp.concatenate(found, axis=0), 0.0))
+    even, half = products(jnp.concatenate(fields, axis=1))
+    even += even_ref[...]
+    half += half_ref[...]
+    gram = even + half + half.T
     row = lax.broadcasted_iota(jnp.int32, (B, LON), 0)
     lane = lax.broadcasted_iota(jnp.int32, (B, LON), 1)
     packed = diagonal = jnp.zeros((B, LON), jnp.float32)
@@ -206,6 +255,10 @@
     )
 
 
+def reciprocal(value):
+    return 1.0 / value
+
+
 def factor(gram):
     groups = ALL // 8
     lane = lax.broadcasted_iota(jnp.int32, (8, ALL), 1)
@@ -214,15 +267,23 @@
     tree = lambda p: ((p[0] + p[1]) + (p[2] + p[3])) + ((p[4] + p[5]) + (p[6] + p[7]))
     left = [gram[8 * g:8 * g + 8] for g in range(groups)]
     right = [jnp.where(lane == sub + 8 * g, 1.0, 0.0) for g in range(groups)]
+    diagonal = sum(jnp.where(lane == sub + 8 * g, left[g], 0.0) for g in range(groups))
+    guess = full(reciprocal(jnp.sum(diagonal, axis=0, keepdims=True)))
     uppers, inverses = [], []
     for g in range(groups):
         columns = [full(left[g][:, 8 * g + t:8 * g + t + 1]) for t in range(8)]
         d = {(s, t): full(columns[t][s:s + 1]) for t in range(8) for s in range(t, 8)}
         a = [full(left[g][t:t + 1]) for t in range(8)]
         b = [full(right[g][t:t + 1]) for t in range(8)]
-        ratio, recip = {}, []
+        following = [full(left[g + 1][:, 8 * g + t:8 * g + t + 1]) for t in range(8)] if g + 1 < groups else None
+        ratio, recip = {}, [None] * 8
         for t in range(8):
-            recip.append(1.0 / d[t, t])
+            if recip[t] is None:
+                recip[t] = reciprocal(d[t, t])
+            if t % 2 == 0:
+                unit = full(guess[:, 8 * g + t:8 * g + t + 1])
+                near = d[t, t] * unit
+                recip[t + 1] = near * reciprocal(near * d[t + 1, t + 1] - d[t + 1, t] * (d[t + 1, t] * unit))
             for s in range(t + 1, 8):
                 ratio[s, t] = d[s, t] * recip[t]
             for s in range(t + 1, 8):
@@ -230,6 +291,8 @@
                     d[s, u] = d[s, u] - ratio[s, t] * d[u, t]
                 a[s] = a[s] - ratio[s, t] * a[t]
                 b[s] = b[s] - ratio[s, t] * b[t]
+                if following:
+                    following[s] = following[s] - ratio[s, t] * following[t]
         upper = inverse = jnp.zeros((8, ALL), jnp.float32)
         for t in range(8):
             scale = lax.rsqrt(d[t, t])
@@ -239,11 +302,14 @@
         inverses.append(inverse)
         a = [a[t] * recip[t] for t in range(8)]
         b = [b[t] * recip[t] for t in range(8)]
+        if following:
+            left[g + 1] = left[g + 1] - tree([following[t] * a[t] for t in range(8)])
+            right[g + 1] = right[g + 1] - tree([following[t] * b[t] for t in range(8)])
         for t in range(7, 0, -1):
             for s in range(t):
                 a[s] = a[s] - ratio[t, s] * a[t]
                 b[s] = b[s] - ratio[t, s] * b[t]
-        for k in range(g + 1, groups):
+        for k in range(g + (2 if following else 1), groups):
             below = [full(left[k][:, 8 * g + t:8 * g + t + 1]) for t in range(8)]
             left[k] = left[k] - tree([below[t] * a[t] for t in range(8)])
             right[k] = right[k] - tree([below[t] * b[t] for t in range(8)])
@@ -261,7 +327,27 @@
     return rows
 
 
-def basis(parts_ref, s_ref, q_hbm, alpha_ref, beta_ref, q_ref, sems):
+def whole_row(i, s_ref, west_ref, east_ref):
+    lane = lanes_of(ALL - B)
+    row = s_ref[i, B:, :]
+    start = SPAN * (i + RIM) + RIM
+    for ref, target in ((west_ref, 0), (east_ref, LON - RIM)):
+        k = start // LON
+        side = ref[:, k * LON:(k + 1) * LON]
+        if (start + RIM - 1) // LON > k:
+            side = jnp.where(lane < start - k * LON, ref[:, (k + 1) * LON:(k + 2) * LON], side)
+        side = pltpu.roll(side, (target - start) % LON, 1)
+        row = jnp.where((lane >= target) & (lane < target + RIM), side, row)
+    return jnp.concatenate([s_ref[i, :B, :], row], axis=0)
+
+
+def basis(parts_ref, s_ref, west_ref, east_ref, q_hbm, alpha_ref, beta_ref, q_ref, high_ref, middle_ref, low_ref, sems):
+    for i in range(0, LAT, 2):
+        pair = [whole_row(j, s_ref, west_ref, east_ref) for j in (i, i + 1)]
+        a, b, c = split(jnp.concatenate(pair, axis=1))
+        high_ref[i // 2] = a
+        middle_ref[i // 2] = b
+        low_ref[i // 2] = c
     total = parts_ref[0]
     for i in range(1, parts_ref.shape[0]):
         total += parts_ref[i]
@@ -283,7 +369,7 @@
     for g in range(LAT // 8):
         rows = []
         for i in range(8 * g, 8 * g + 8, 2):
-            a, b, c = split(jnp.concatenate([s_ref[i], s_ref[i + 1]], axis=1))
+            a, b, c = high_ref[i // 2], middle_ref[i // 2], low_ref[i // 2]
             new = dot(three, jnp.concatenate([a, a, a], axis=0)) + dot(two, jnp.concatenate([b, b], axis=0)) + dot(high, c)
             rows += [new[:, :LON], new[:, LON:]]
         for v in range(0, ALL, 8):
@@ -298,28 +384,32 @@
 
 def body(start_block, sea_mask, depth_levels):
     x = start_block.reshape(B * LAT, LON)
+    x, sea_mask, depth_levels = [pltpu.with_memory_space_constraint(v, pltpu.HBM) for v in (x, sea_mask, depth_levels)]
     edge = (RIM, B + 8, LON)
-    side = (B + 8, LON)
     anywhere = pl.BlockSpec(memory_space=pl.ANY)
     small = pltpu.VMEM((LAT, LON), jnp.int32)
     inputs = dict(in_specs=[pl.BlockSpec(memory_space=pltpu.HBM)] * 3)
     room = [pltpu.VMEM((B * LAT, LON), jnp.float32), small, small, pltpu.SemaphoreType.DMA((3,))]
     near, far = call(edge_rows, (edge, edge), room, **inputs)(x, sea_mask, depth_levels)
+    far = lax.ppermute(far, ROW, [(i, ((i + 1) ^ 1) - 1) for i in range(1, 7)])
     near = lax.ppermute(near, ROW, [(i, i ^ 1) for i in range(8)])
-    far = lax.ppermute(far, ROW, [(i, ((i + 1) ^ 1) - 1) for i in range(1, 7)])
+    flat = (B + 8, FLAT)
     core, part_west, part_east = call(
-        core_rows, ((LAT, B + 8, LON), side, side), room, flops=1 << 22, moved=1 << 20, **inputs
+        core_rows, ((LAT, B + 8, LON), flat, flat), room, flops=1 << 22, moved=1 << 20, **inputs
     )(x, sea_mask, depth_levels)
-    near, far, north, south = call(side_columns, (side, side, edge, edge))(near, far, part_west, part_east)
+    near, far, north, south, own_west, own_east = call(side_columns, (flat, flat, edge, edge, flat, flat))(
+        near, far, part_west, part_east
+    )
+    far = lax.ppermute(far, COL, [(i, (((i + 1) ^ 1) - 1) % 32) for i in range(32)])
     near = lax.ppermute(near, COL, [(i, i ^ 1) for i in range(32)])
-    far = lax.ppermute(far, COL, [(i, (((i + 1) ^ 1) - 1) % 32) for i in range(32)])
-    wide = (ROWS, B, WIDE)
-    thin = (ROWS, 8, WIDE)
-    s, gram = call(
-        krylov,
-        ((LAT, ALL, LON), (B + 8, LON)),
-        [pltpu.VMEM(wide, jnp.float32)] * 3 + [pltpu.VMEM(thin, jnp.float32)] * 3,
-    )(core, north, south, near, far)
+    wide = pltpu.VMEM((ROWS, B, LON), jnp.float32)
+    thin = pltpu.VMEM((ROWS, 8, LON), jnp.float32)
+    square = (ALL, ALL)
+    s, even, half = call(
+        inside, ((LAT, ALL, LON), square, square), [wide, wide, thin, thin, thin], flops=1 << 28, moved=1 << 23
+    )(core, north, south)
+    rim = (ALL - B, FLAT)
+    gram, west, east = call(border, ((B + 8, LON), rim, rim))(near, far, own_west, own_east, even, half)
     pair = lax.all_gather(gram, "core")
     copies = call(spread, ((16, B + 8, LON),))(pair)[0]
     parts = lax.all_to_all(copies, ("x", "y"), 0, 0)
@@ -329,9 +419,10 @@
     return call(
         basis,
         ((ALL, LAT, LON), (ITERS, B, B), (ITERS, B, B)),
-        [pltpu.VMEM((ALL, LAT, LON), jnp.float32), pltpu.SemaphoreType.DMA((LAT // 8,))],
+        [pltpu.VMEM((ALL, LAT, LON), jnp.float32)] + [pltpu.VMEM((LAT // 2, ALL, 2 * LON), jnp.bfloat16)] * 3
+        + [pltpu.SemaphoreType.DMA((LAT // 8,))],
         out_specs=(anywhere, vmem, vmem),
-    )(parts, s)
+    )(parts, s, west, east)
 
 
 def solution(mesh):

time: 64.6 us -> 58.2 us (0.901)
  local copies, waits for them, and re-layouts: 2.47 us -> 0 us
  waiting for transfers between devices: 3.11 us -> 0.89 us
  blocking collectives: 39.3 us -> 38.4 us
  Pallas kernels: 14.9 us -> 14.2 us
    unnamed x6 -> x0, local copies, waits for them, and re-layouts: 2.47 us -> none
    pallas_call x1, Pallas kernels: 8.92 us -> 7.62 us  [body(): call(basis, ((ALL, LAT, LON), (ITERS, B, B), (ITERS, B, B)), [pltpu.VMEM(...]
    ppermute x1, waiting for transfers between devices: 2.02 us -> 0.88 us  [body(): lax.ppermute(far, COL, [(i, ((i + 1 ^ 1) - 1) % 32) for i in range(32)])]
    ppermute x1, waiting for transfers between devices: 1.09 us -> 0.01 us  [body(): near = lax.ppermute(near, COL, [(i, i ^ 1) for i in range(32)])]
    pallas_call x1, Pallas kernels: 0.17 us -> 1.14 us  [body(): call(edge_rows, (edge, edge), room, **inputs)(x, sea_mask, depth_levels)]
    pallas_call x3 -> x4, Pallas kernels: 5.76 us -> 5.43 us  [the longest x1 2.65 us: body(): call(inside, ((LAT, ALL, LON), square, square), [wide, wide, thin, thin,...]
  transfers between devices with their start and end apart: 4 -> 4, of which waited for: 2 -> 1; matrix products, arithmetic and copies ran while one was open for 0% -> 0% of each run, Pallas kernels for 1% -> 7%
where the time goes in v5:
time: 58.2 us; the launch traced here: 57.9 us
  blocking collectives  38.4 us (66%)
  Pallas kernels  14.2 us (24%)
  starting transfers between devices  3.7 us (6%)
  waiting for transfers between devices  0.89 us (2%)
  between operations  0.72 us (1%)
    all_to_all x1, blocking collectives, body(): parts = lax.all_to_all(copies, ('x', 'y'), 0, 0)  18.8 us
    all_to_all x1, blocking collectives, body(): parts = lax.all_to_all(copies, 'z', 0, 0)  15.5 us
    pallas_call x1, Pallas kernels, body(): call(basis, ((ALL, LAT, LON), (ITERS, B, B), (ITERS, B, B)), [pltpu.VMEM(...  7.62 us
    all_gather x1, blocking collectives, body(): pair = lax.all_gather(gram, 'core')  4.12 us
    pallas_call x1, Pallas kernels, body(): call(inside, ((LAT, ALL, LON), square, square), [wide, wide, thin, thin,...  2.65 us
    ppermute x1, starting transfers between devices, body(): near = lax.ppermute(near, COL, [(i, i ^ 1) for i in range(32)])  2.27 us
    pallas_call x1, Pallas kernels, body(): call(core_rows, ((LAT, B + 8, LON), flat, flat), room, flops=1 << 22, mov...  1.55 us
  transfers between devices with their start and end apart: 4, of which 1 were waited for; matrix products, arithmetic and copies ran while one was open for 0% of the time, Pallas kernels for 7%

profile of v5, /device:TPU:8, one launch (start us, length us, event | category | flops | bytes accessed | tf_op | source)
XLA Modules:
  0.0 57.9 jit_solution(6150879045988720852)
XLA Ops:
  0.6 1.1 %shard_map.58 = (f32[3,40,128]{2,1,0:T(8,128)S(1)}, f32[3,40,128]{2,1,0:T(8,128)S(1)}) custom-call(f32[1024,128]{1,0:T(8,128)} %bitcast.3, s32[32,128]{1,0:T(8,128)} %mask_hbm.3, s32[32,128]{1,0:T(8,128)} %depth_hbm.3), custom_call_target="tpu_custom_call" | custom-call | tf_op jit(solution)/shard_map/pallas_call | solution.py:393
  1.8 0.1 collective-permute-start
  1.9 0.7 %collective-permute-start.1 = (f32[3,40,128]{2,1,0:T(8,128)S(1)}, f32[3,40,128]{2,1,0:T(8,128)S(1)}, u32[]{:S(2)}, u32[]{:S(2)}) collective-permute-start(f32[3,40,128]{2,1,0:T(8,128)S(1)} %get-tuple-element.21), channel_id=1, source_target_pairs={{32,64},{64,32},{96,128},{128,96},{160,192},{192,160},{33,65},{65,... | collective-permute-start | bytes 184328 | tf_op jit(solution)/shard_map/ppermute | solution.py:394
  2.6 1.6 %shard_map.59 = (f32[32,40,128]{2,1,0:T(8,128)S(1)}, f32[40,384]{1,0:T(8,128)S(1)}, f32[40,384]{1,0:T(8,128)S(1)}) custom-call(f32[1024,128]{1,0:T(8,128)} %bitcast.4, s32[32,128]{1,0:T(8,128)} %mask_hbm.3, s32[32,128]{1,0:T(8,128)} %depth_hbm.3), custom_call_target="tpu_custom_call" | custom-call | flops 4194304 | bytes 1048576 | tf_op jit(solution)/shard_map/pallas_call | solution.py:397
  4.1 0.0 collective-permute-done.near_ref
  4.1 0.0 collective-permute-done.1.far_ref
  4.1 0.2 shard_map.60
  4.4 2.3 %collective-permute-start.2 = (f32[40,384]{1,0:T(8,128)S(1)}, f32[40,384]{1,0:T(8,128)S(1)}, u32[]{:S(2)}, u32[]{:S(2)}) collective-permute-start(f32[40,384]{1,0:T(8,128)S(1)} %get-tuple-element.24), channel_id=1, source_target_pairs={{0,1},{1,0},{2,3},{3,2},{4,5},{5,4},{6,7},{7,6},{8,9},{9,8},{10,11... | collective-permute-start | bytes 184328 | tf_op jit(solution)/shard_map/ppermute | solution.py:404
  6.6 0.7 %collective-permute-start.3 = (f32[40,384]{1,0:T(8,128)S(1)}, f32[40,384]{1,0:T(8,128)S(1)}, u32[]{:S(2)}, u32[]{:S(2)}) collective-permute-start(f32[40,384]{1,0:T(8,128)S(1)} %get-tuple-element.25), channel_id=1, source_target_pairs={{0,31},{1,2},{2,1},{3,4},{4,3},{5,6},{6,5},{7,8},{8,7},{9,10},{10,... | collective-permute-start | bytes 184328 | tf_op jit(solution)/shard_map/ppermute | solution.py:403
  7.3 2.7 %shard_map.61 = (f32[32,128,128]{2,1,0:T(8,128)S(1)}, f32[128,128]{1,0:T(8,128)S(1)}, f32[128,128]{1,0:T(8,128)S(1)}) custom-call(f32[32,40,128]{2,1,0:T(8,128)S(1)} %get-tuple-element.28.core_ref, f32[3,40,128]{2,1,0:T(8,128)S(1)} %get-tuple-element.29.north_ref, f32[3,40,128]{2,1,0:T(8,128)S(1)} %get-tuple-element.30.south_ref), custom_call_target="tpu_custom_call" | custom-call | flops 268435456 | bytes 8388608 | tf_op jit(solution)/shard_map/pallas_call | solution.py:408
  10.0 0.0 collective-permute-done.2.near_ref
  10.0 0.9 %collective-permute-done.3.far_ref = f32[40,384]{1,0:T(8,128)S(1)} collective-permute-done((f32[40,384]{1,0:T(8,128)S(1)}, f32[40,384]{1,0:T(8,128)S(1)}, u32[]{:S(2)}, u32[]{:S(2)}) %collective-permute-start.3) | collective-permute-done | bytes 61472 | tf_op jit(solution)/shard_map/ppermute | solution.py:403
  10.9 1.0 %shard_map.62 = (f32[40,128]{1,0:T(8,128)S(1)}, f32[96,384]{1,0:T(8,128)S(1)}, f32[96,384]{1,0:T(8,128)S(1)}) custom-call(f32[40,384]{1,0:T(8,128)S(1)} %collective-permute-done.2.near_ref, f32[40,384]{1,0:T(8,128)S(1)} %collective-permute-done.3.far_ref, f32[40,384]{1,0:T(8,128)S(1)} %get-tuple-element.26.own_west_ref, ...), custom_call_target="tpu_custom_call" | custom-call | tf_op jit(solution)/shard_map/pallas_call | solution.py:412
  11.9 4.1 %all-gather = f32[80,128]{1,0:T(8,128)S(1)} all-gather(f32[40,128]{1,0:T(8,128)S(1)} %get-tuple-element.33), channel_id=2, replica_groups=mesh['x'=4,'core'=2,'z'=8,'y'=4] {'core'}, dimensions={0}, use_global_device_ids=true | all-gather | bytes 61440 | tf_op jit(solution)/shard_map/all_gather | solution.py:413
  16.0 18.8 %all_to_all.10.parts_ref = f32[16,40,128]{2,1,0:T(8,128)S(1)} all-to-all(f32[16,40,128]{2,1,0:T(8,128)S(1)} %shard_map.63), channel_id=1, replica_groups=mesh['x'=4,'core'=2,'z'=8,'y'=4] {'x','y'}, dimensions={0} | all-to-all | bytes 655360 | tf_op jit(solution)/shard_map/all_to_all | solution.py:415
  34.8 15.5 %all_to_all.11.parts_ref = f32[8,40,128]{2,1,0:T(8,128)S(1)} all-to-all(f32[8,40,128]{2,1,0:T(8,128)S(1)} %shard_map.64), channel_id=1, replica_groups=mesh['x'=4,'core'=2,'z'=8,'y'=4] {'z'}, dimensions={0} | all-to-all | bytes 327680 | tf_op jit(solution)/shard_map/all_to_all | solution.py:417
  50.3 7.6 %shard_map.65 = (f32[128,32,128]{2,1,0:T(8,128)}, f32[3,32,32]{2,1,0:T(8,128)}, f32[3,32,32]{2,1,0:T(8,128)}) custom-call(f32[8,40,128]{2,1,0:T(8,128)S(1)} %all_to_all.11.parts_ref, f32[32,128,128]{2,1,0:T(8,128)S(1)} %get-tuple-element.34.s_ref, f32[96,384]{1,0:T(8,128)S(1)} %get-tuple-element.35.west_ref, f32[96,384]{1,0:T(8,128)S(1)} %get-tuple-element.36.east_ref), custom_call_target="tpu_custom_call" | custom-call | tf_op jit(solution)/shard_map/pallas_call | solution.py:419
  (2 shorter events, 0.1 us)
Async XLA Ops:
  1.8 2.3 %collective-permute-start = (f32[3,40,128]{2,1,0:T(8,128)S(1)}, f32[3,40,128]{2,1,0:T(8,128)S(1)}, u32[]{:S(2)}, u32[]{:S(2)}) collective-permute-start(f32[3,40,128]{2,1,0:T(8,128)S(1)} %get-tuple-element.20), channel_id=1, source_target_pairs={{0,32},{32,0},{64,96},{96,64},{128,160},{160,128},{192,224},{224,1... | collective-permute-start | bytes 184328 | tf_op jit(solution)/shard_map/ppermute | solution.py:395
  1.9 2.2 %collective-permute-start.1 = (f32[3,40,128]{2,1,0:T(8,128)S(1)}, f32[3,40,128]{2,1,0:T(8,128)S(1)}, u32[]{:S(2)}, u32[]{:S(2)}) collective-permute-start(f32[3,40,128]{2,1,0:T(8,128)S(1)} %get-tuple-element.21), channel_id=1, source_target_pairs={{32,64},{64,32},{96,128},{128,96},{160,192},{192,160},{33,65},{65,... | collective-permute-start | bytes 184328 | tf_op jit(solution)/shard_map/ppermute | solution.py:394
  4.4 5.6 %collective-permute-start.2 = (f32[40,384]{1,0:T(8,128)S(1)}, f32[40,384]{1,0:T(8,128)S(1)}, u32[]{:S(2)}, u32[]{:S(2)}) collective-permute-start(f32[40,384]{1,0:T(8,128)S(1)} %get-tuple-element.24), channel_id=1, source_target_pairs={{0,1},{1,0},{2,3},{3,2},{4,5},{5,4},{6,7},{7,6},{8,9},{9,8},{10,11... | collective-permute-start | bytes 184328 | tf_op jit(solution)/shard_map/ppermute | solution.py:404
  6.6 4.2 %collective-permute-start.3 = (f32[40,384]{1,0:T(8,128)S(1)}, f32[40,384]{1,0:T(8,128)S(1)}, u32[]{:S(2)}, u32[]{:S(2)}) collective-permute-start(f32[40,384]{1,0:T(8,128)S(1)} %get-tuple-element.25), channel_id=1, source_target_pairs={{0,31},{1,2},{2,1},{3,4},{4,3},{5,6},{6,5},{7,8},{8,7},{9,10},{10,... | collective-permute-start | bytes 184328 | tf_op jit(solution)/shard_map/ppermute | solution.py:403

commit v6 on v5

--- a/solution.py
+++ b/solution.py
@@ -19,6 +19,9 @@
 SPAN = 3 * RIM
 FLAT = 3 * LON
 ALL = (ITERS + 1) * B
+HALF = B // 2
+PIECE = 64
+HALVES = [(k, part) for k in range(ITERS) for part in range(2)]
 HIGH = lax.Precision.HIGHEST
 ROW, COL = ("x", "core"), ("z", "y")
 NT = (((1,), (1,)), ((), ()))
@@ -40,29 +43,27 @@
     )
 
 
-def masked_row(lat, x_ref, mask_ref, depth_ref):
-    mask = mask_ref[pl.ds(lat, 1), :].astype(jnp.float32)
-    depth = mask * depth_ref[pl.ds(lat, 1), :].astype(jnp.float32) / LEVELS
-    row = x_ref[pl.ds(lat, B, stride=LAT), :] * mask
-    return jnp.concatenate([row, jnp.broadcast_to(depth, (8, LON))], axis=0)
-
-
-def load(sources, targets, sems):
-    copies = [pltpu.make_async_copy(a, b, sems.at[i]) for i, (a, b) in enumerate(zip(sources, targets))]
+def edge_rows(x_hbm, mask_hbm, depth_hbm, far_ref, near_ref, x_ref, h_ref, mask_ref, depth_ref, sems):
+    pairs = ((x_hbm, x_ref), (mask_hbm, mask_ref), (depth_hbm, depth_ref))
+    copies = [pltpu.make_async_copy(a, b, sems.at[i]) for i, (a, b) in enumerate(pairs)]
     for copy in copies:
         copy.start()
-    for copy in copies:
+    for copy in copies[1:]:
         copy.wait()
-
-
-def edge_rows(x_hbm, mask_hbm, depth_hbm, near_ref, far_ref, x_ref, mask_ref, depth_ref, sems):
-    load((x_hbm, mask_hbm, depth_hbm), (x_ref, mask_ref, depth_ref), sems)
+    h_ref[...] = mask_ref[...].astype(jnp.float32) * depth_ref[...].astype(jnp.float32) / LEVELS
+    copies[0].wait()
     odd = lax.axis_index("core") == 1
     for i in range(RIM):
-        top = masked_row(i, x_ref, mask_ref, depth_ref)
-        bottom = masked_row(LAT - RIM + i, x_ref, mask_ref, depth_ref)
+        top = masked_row(i, x_ref, h_ref)
+        bottom = masked_row(LAT - RIM + i, x_ref, h_ref)
         near_ref[i] = jnp.where(odd, top, bottom)
         far_ref[i] = jnp.where(odd, bottom, top)
+
+
+def masked_row(lat, x_ref, h_ref):
+    depth = h_ref[pl.ds(lat, 1), :]
+    row = jnp.where(depth > 0.0, x_ref[pl.ds(lat, B, stride=LAT), :], 0.0)
+    return jnp.concatenate([row, jnp.broadcast_to(depth, (8, LON))], axis=0)
 
 
 def pack_sides(row, r, west, east):
@@ -78,11 +79,10 @@
     return [flat[:, k * LON:(k + 1) * LON] for k in range(FLAT // LON)]
 
 
-def core_rows(x_hbm, mask_hbm, depth_hbm, core_ref, west_ref, east_ref, x_ref, mask_ref, depth_ref, sems):
-    load((x_hbm, mask_hbm, depth_hbm), (x_ref, mask_ref, depth_ref), sems)
+def core_rows(x_ref, h_ref, core_ref, west_ref, east_ref):
     west, east = chunks(jnp.zeros((B + 8, FLAT), jnp.float32)), chunks(jnp.zeros((B + 8, FLAT), jnp.float32))
     for i in range(LAT):
-        row = masked_row(i, x_ref, mask_ref, depth_ref)
+        row = masked_row(i, x_ref, h_ref)
         core_ref[i] = row
         pack_sides(row, i + RIM, west, east)
     west_ref[...] = jnp.concatenate(west, axis=1)
@@ -90,7 +90,7 @@
 
 
 def side_columns(near_ref, far_ref, part_west_ref, part_east_ref,
-                 near_out, far_out, north_ref, south_ref, west_ref, east_ref):
+                 far_out, near_out, north_ref, south_ref, west_ref, east_ref):
     odd = lax.axis_index("core") == 1
     west, east = chunks(part_west_ref[...]), chunks(part_east_ref[...])
     for i in range(RIM):
@@ -216,8 +216,11 @@
         here = (lane >= k * B) & (lane < (k + 1) * B)
         packed = jnp.where(here, jnp.where(lane - k * B >= row, own, after), packed)
         diagonal = jnp.where(here & (lane - k * B == row), after, diagonal)
-    gram_ref[:B] = packed
-    gram_ref[B:] = (diagonal[:8] + diagonal[8:16]) + (diagonal[16:24] + diagonal[24:])
+    line = jnp.sum(diagonal, axis=0, keepdims=True)
+    for n, (k, part) in enumerate(HALVES):
+        there = (row == B - 1 - n) & (lane >= ITERS * B) & (lane < ITERS * B + HALF)
+        packed = jnp.where(there, pltpu.roll(line, (ITERS * B - k * B - part * HALF) % LON, 1), packed)
+    gram_ref[...] = packed
 
 
 def spread(parts_ref, out_ref):
@@ -231,15 +234,20 @@
 def unpack(total):
     row = lax.broadcasted_iota(jnp.int32, (B, LON), 0)
     lane = lax.broadcasted_iota(jnp.int32, (B, LON), 1)
-    block, place = lane // B, lane % B
-    turned = jnp.concatenate([total[:B], jnp.zeros((LON - B, LON), jnp.float32)], axis=0).T
+    block, place = lane >> 5, lane & (B - 1)
+    turned = jnp.concatenate([total, jnp.zeros((LON - B, LON), jnp.float32)], axis=0).T
     mirror = jnp.zeros((B, LON), jnp.float32)
     for k in range(ITERS + 1):
         part = turned[k * B:(k + 1) * B]
         mirror = jnp.where(block == k, pltpu.roll(part, k * B, 1) if k else part, mirror)
-    even = jnp.where(place >= row, total[:B], mirror)
-    odd = jnp.where(place < row, total[:B], mirror)
-    odd = jnp.where(place == row, jnp.sum(total[B:], axis=0, keepdims=True), odd)
+    even = jnp.where(place >= row, total, mirror)
+    odd = jnp.where(place < row, total, mirror)
+    line = jnp.zeros((1, LON), jnp.float32)
+    for n, (k, part) in enumerate(HALVES):
+        target = k * B + part * HALF
+        moved = pltpu.roll(total[B - 1 - n:B - n], (target - ITERS * B) % LON, 1)
+        line = jnp.where((lane[:1] >= target) & (lane[:1] < target + HALF), moved, line)
+    odd = jnp.where(place == row, line, odd)
     move = lambda field, k: pltpu.roll(field, (k * B) % LON, 1)
     even1, even2, odd1, odd2, odd3 = move(even, 1), move(even, -1), move(odd, 1), move(odd, 2), move(odd, 3)
     pick = lambda a, b, c, d: jnp.where(block == 0, a, jnp.where(block == 1, b, jnp.where(block == 2, c, d)))
@@ -264,55 +272,61 @@
     lane = lax.broadcasted_iota(jnp.int32, (8, ALL), 1)
     sub = lax.broadcasted_iota(jnp.int32, (8, ALL), 0)
     full = lambda value: jnp.broadcast_to(value, (8, ALL))
+    line = lambda value, t: full(value[t:t + 1])
     tree = lambda p: ((p[0] + p[1]) + (p[2] + p[3])) + ((p[4] + p[5]) + (p[6] + p[7]))
-    left = [gram[8 * g:8 * g + 8] for g in range(groups)]
-    right = [jnp.where(lane == sub + 8 * g, 1.0, 0.0) for g in range(groups)]
-    diagonal = sum(jnp.where(lane == sub + 8 * g, left[g], 0.0) for g in range(groups))
+    weigh = lambda p, q: tree([p[t] * q[t] for t in range(8)])
+    work = [gram[8 * g:8 * g + 8] for g in range(groups)]
+    columns = lambda k, g: [full(work[k][:, 8 * g + t:8 * g + t + 1]) for t in range(8)] if k < groups else None
+    diagonal = sum(jnp.where(lane == sub + 8 * g, work[g], 0.0) for g in range(groups))
     guess = full(reciprocal(jnp.sum(diagonal, axis=0, keepdims=True)))
     uppers, inverses = [], []
+    own, after = columns(0, 0), columns(1, 0)
     for g in range(groups):
-        columns = [full(left[g][:, 8 * g + t:8 * g + t + 1]) for t in range(8)]
-        d = {(s, t): full(columns[t][s:s + 1]) for t in range(8) for s in range(t, 8)}
-        a = [full(left[g][t:t + 1]) for t in range(8)]
-        b = [full(right[g][t:t + 1]) for t in range(8)]
-        following = [full(left[g + 1][:, 8 * g + t:8 * g + t + 1]) for t in range(8)] if g + 1 < groups else None
-        ratio, recip = {}, [None] * 8
+        later, coming = columns(g + 2, g), columns(g + 1, g + 1)
+        a = work[g]
+        b = jnp.where(lane == sub + 8 * g, 1.0, jnp.where(lane < 8 * g, work[g], 0.0))
+        recip, ratio, pivot = [None] * 8, {}, []
         for t in range(8):
+            pivot.append(line(own[t], t))
             if recip[t] is None:
-                recip[t] = reciprocal(d[t, t])
-            if t % 2 == 0:
+                recip[t] = reciprocal(pivot[t])
+            if t % 2 == 0 and g > 0:
                 unit = full(guess[:, 8 * g + t:8 * g + t + 1])
-                near = d[t, t] * unit
-                recip[t + 1] = near * reciprocal(near * d[t + 1, t + 1] - d[t + 1, t] * (d[t + 1, t] * unit))
+                near, cross = pivot[t] * unit, line(own[t], t + 1)
+                recip[t + 1] = near * reciprocal(near * line(own[t + 1], t + 1) - cross * (cross * unit))
+            column = jnp.where(sub > t, own[t] * recip[t], 0.0)
             for s in range(t + 1, 8):
-                ratio[s, t] = d[s, t] * recip[t]
-            for s in range(t + 1, 8):
-                for u in range(t + 1, s + 1):
-                    d[s, u] = d[s, u] - ratio[s, t] * d[u, t]
-                a[s] = a[s] - ratio[s, t] * a[t]
-                b[s] = b[s] - ratio[s, t] * b[t]
-                if following:
-                    following[s] = following[s] - ratio[s, t] * following[t]
-        upper = inverse = jnp.zeros((8, ALL), jnp.float32)
+                ratio[s, t] = line(column, s)
+                own[s] = own[s] - column * line(own[t], s)
+            if t < 7:
+                a = a - column * line(a, t)
+                b = b - column * line(b, t)
+                for ahead in (after, later):
+                    for s in range(t + 1, 8) if ahead else ():
+                        ahead[s] = ahead[s] - ratio[s, t] * ahead[t]
+        pivots = inverted = jnp.zeros((8, ALL), jnp.float32)
         for t in range(8):
-            scale = lax.rsqrt(d[t, t])
-            upper = jnp.where(sub == t, a[t] * scale, upper)
-            inverse = jnp.where(sub == t, b[t] * scale, inverse)
-        uppers.append(jnp.where(lane >= sub + 8 * g, upper, 0.0))
-        inverses.append(inverse)
-        a = [a[t] * recip[t] for t in range(8)]
-        b = [b[t] * recip[t] for t in range(8)]
-        if following:
-            left[g + 1] = left[g + 1] - tree([following[t] * a[t] for t in range(8)])
-            right[g + 1] = right[g + 1] - tree([following[t] * b[t] for t in range(8)])
+            pivots = jnp.where(sub == t, pivot[t], pivots)
+            inverted = jnp.where(sub == t, recip[t], inverted)
+        scale = lax.rsqrt(pivots)
+        uppers.append(jnp.where(lane >= sub + 8 * g, a * scale, 0.0))
+        inverses.append(b * scale)
+        if g + 1 == groups:
+            break
+        c = jnp.where(lane < 8 * g + 8, b, a) * inverted
+        c = [line(c, t) for t in range(8)]
+        scaled = [after[t] * recip[t] for t in range(8)]
+        own = [coming[u] - weigh(after, [line(scaled[t], u) for t in range(8)]) for u in range(8)]
+        block = (lane >= 8 * g) & (lane < 8 * g + 8)
+        for k, ahead in ((g + 1, after), (g + 2, later)):
+            if ahead:
+                work[k] = jnp.where(block, 0.0, work[k]) - weigh(ahead, c)
+        after = columns(g + 2, g + 1)
         for t in range(7, 0, -1):
             for s in range(t):
-                a[s] = a[s] - ratio[t, s] * a[t]
-                b[s] = b[s] - ratio[t, s] * b[t]
-        for k in range(g + (2 if following else 1), groups):
-            below = [full(left[k][:, 8 * g + t:8 * g + t + 1]) for t in range(8)]
-            left[k] = left[k] - tree([below[t] * a[t] for t in range(8)])
-            right[k] = right[k] - tree([below[t] * b[t] for t in range(8)])
+                c[s] = c[s] - ratio[t, s] * c[t]
+        for k in range(g + 3, groups):
+            work[k] = jnp.where(block, 0.0, work[k]) - weigh(columns(k, g), c)
     return jnp.concatenate(inverses, axis=0), jnp.concatenate(uppers, axis=0)
 
 
@@ -341,7 +355,8 @@
     return jnp.concatenate([s_ref[i, :B, :], row], axis=0)
 
 
-def basis(parts_ref, s_ref, west_ref, east_ref, q_hbm, alpha_ref, beta_ref, q_ref, high_ref, middle_ref, low_ref, sems):
+def basis(parts_ref, s_ref, west_ref, east_ref, q_hbm, alpha_hbm, beta_hbm,
+          q_ref, alpha_ref, beta_ref, high_ref, middle_ref, low_ref, sems):
     for i in range(0, LAT, 2):
         pair = [whole_row(j, s_ref, west_ref, east_ref) for j in (i, i + 1)]
         a, b, c = split(jnp.concatenate(pair, axis=1))
@@ -360,24 +375,32 @@
         here, after = slice(k * B, (k + 1) * B), slice((k + 1) * B, (k + 2) * B)
         alpha_ref[k] = coeffs[here, here]
         beta_ref[k] = coeffs[after, here]
+    copies = [
+        pltpu.make_async_copy(alpha_ref, alpha_hbm, sems.at[0]),
+        pltpu.make_async_copy(beta_ref, beta_hbm, sems.at[1]),
+    ]
+    for copy in copies:
+        copy.start()
     high, middle, low = split(inverse)
     two = jnp.concatenate([high, middle], axis=1)
     three = jnp.concatenate([high, middle, low], axis=1)
     dot = lambda a, b: jnp.dot(a, b, preferred_element_type=jnp.float32)
     sub = lax.broadcasted_iota(jnp.int32, (8, LON), 0)
-    copies = []
     for g in range(LAT // 8):
         rows = []
         for i in range(8 * g, 8 * g + 8, 2):
             a, b, c = high_ref[i // 2], middle_ref[i // 2], low_ref[i // 2]
             new = dot(three, jnp.concatenate([a, a, a], axis=0)) + dot(two, jnp.concatenate([b, b], axis=0)) + dot(high, c)
             rows += [new[:, :LON], new[:, LON:]]
+        chunk = pl.ds(8 * g, 8)
         for v in range(0, ALL, 8):
             for t, tile in enumerate(swap([row[v:v + 8] for row in rows], sub)):
                 q_ref[v + t, 8 * g:8 * g + 8, :] = tile
-        chunk = pl.ds(8 * g, 8)
-        copies.append(pltpu.make_async_copy(q_ref.at[:, chunk, :], q_hbm.at[:, chunk, :], sems.at[g]))
-        copies[-1].start()
+            if v % PIECE == PIECE - 8:
+                block = pl.ds(v + 8 - PIECE, PIECE)
+                sem = sems.at[len(copies)]
+                copies.append(pltpu.make_async_copy(q_ref.at[block, chunk, :], q_hbm.at[block, chunk, :], sem))
+                copies[-1].start()
     for copy in copies:
         copy.wait()
 
@@ -388,16 +411,19 @@
     edge = (RIM, B + 8, LON)
     anywhere = pl.BlockSpec(memory_space=pl.ANY)
     small = pltpu.VMEM((LAT, LON), jnp.int32)
-    inputs = dict(in_specs=[pl.BlockSpec(memory_space=pltpu.HBM)] * 3)
-    room = [pltpu.VMEM((B * LAT, LON), jnp.float32), small, small, pltpu.SemaphoreType.DMA((3,))]
-    near, far = call(edge_rows, (edge, edge), room, **inputs)(x, sea_mask, depth_levels)
+    far, near, x, h = call(
+        edge_rows,
+        (edge, edge, (B * LAT, LON), (LAT, LON)),
+        [small, small, pltpu.SemaphoreType.DMA((3,))],
+        in_specs=[pl.BlockSpec(memory_space=pltpu.HBM)] * 3,
+    )(x, sea_mask, depth_levels)
     far = lax.ppermute(far, ROW, [(i, ((i + 1) ^ 1) - 1) for i in range(1, 7)])
     near = lax.ppermute(near, ROW, [(i, i ^ 1) for i in range(8)])
     flat = (B + 8, FLAT)
     core, part_west, part_east = call(
-        core_rows, ((LAT, B + 8, LON), flat, flat), room, flops=1 << 22, moved=1 << 20, **inputs
-    )(x, sea_mask, depth_levels)
-    near, far, north, south, own_west, own_east = call(side_columns, (flat, flat, edge, edge, flat, flat))(
+        core_rows, ((LAT, B + 8, LON), flat, flat), flops=1 << 22, moved=1 << 20
+    )(x, h)
+    far, near, north, south, own_west, own_east = call(side_columns, (flat, flat, edge, edge, flat, flat))(
         near, far, part_west, part_east
     )
     far = lax.ppermute(far, COL, [(i, (((i + 1) ^ 1) - 1) % 32) for i in range(32)])
@@ -409,19 +435,21 @@
         inside, ((LAT, ALL, LON), square, square), [wide, wide, thin, thin, thin], flops=1 << 28, moved=1 << 23
     )(core, north, south)
     rim = (ALL - B, FLAT)
-    gram, west, east = call(border, ((B + 8, LON), rim, rim))(near, far, own_west, own_east, even, half)
+    gram, west, east = call(border, ((B, LON), rim, rim))(near, far, own_west, own_east, even, half)
     pair = lax.all_gather(gram, "core")
-    copies = call(spread, ((16, B + 8, LON),))(pair)[0]
+    copies = call(spread, ((16, B, LON),))(pair)[0]
     parts = lax.all_to_all(copies, ("x", "y"), 0, 0)
-    copies = call(spread, ((8, B + 8, LON),))(parts)[0]
+    copies = call(spread, ((8, B, LON),))(parts)[0]
     parts = lax.all_to_all(copies, "z", 0, 0)
-    vmem = pl.BlockSpec(memory_space=pltpu.VMEM)
+    table = (ITERS, B, B)
+    results = ((ALL, LAT, LON), table, table)
     return call(
         basis,
-        ((ALL, LAT, LON), (ITERS, B, B), (ITERS, B, B)),
-        [pltpu.VMEM((ALL, LAT, LON), jnp.float32)] + [pltpu.VMEM((LAT // 2, ALL, 2 * LON), jnp.bfloat16)] * 3
-        + [pltpu.SemaphoreType.DMA((LAT // 8,))],
-        out_specs=(anywhere, vmem, vmem),
+        results,
+        [pltpu.VMEM(shape, jnp.float32) for shape in results]
+        + [pltpu.VMEM((LAT // 2, ALL, 2 * LON), jnp.bfloat16)] * 3
+        + [pltpu.SemaphoreType.DMA((2 + (LAT // 8) * (ALL // PIECE),))],
+        out_specs=(anywhere,) * 3,
     )(parts, s, west, east)
 
 

time: 58.2 us -> 56.2 us (0.966)
  Pallas kernels: 14.2 us -> 12.1 us
    pallas_call x6, Pallas kernels: 11.4 us -> 9.19 us  [the longest x1 6.43 us: body(): call(basis, results, [pltpu.VMEM(shape, jnp.float32) for shape in results...]
    all_gather x1, blocking collectives: 4.12 us -> 4.88 us  [body(): pair = lax.all_gather(gram, 'core')]
  transfers between devices with their start and end apart: 4 -> 4, of which waited for: 1 -> 2; matrix products, arithmetic and copies ran while one was open for 0% -> 0% of each run, Pallas kernels for 7% -> 6%
where the time goes in v6:
time: 56.2 us; the launch traced here: 55.9 us
  blocking collectives  38.5 us (69%)
  Pallas kernels  12.1 us (22%)
  starting transfers between devices  3.7 us (7%)
  waiting for transfers between devices  0.92 us (2%)
  between operations  0.71 us (1%)
    all_to_all x1, blocking collectives, body(): parts = lax.all_to_all(copies, ('x', 'y'), 0, 0)  18.5 us
    all_to_all x1, blocking collectives, body(): parts = lax.all_to_all(copies, 'z', 0, 0)  15.1 us
    pallas_call x1, Pallas kernels, body(): call(basis, results, [pltpu.VMEM(shape, jnp.float32) for shape in results...  6.43 us
    all_gather x1, blocking collectives, body(): pair = lax.all_gather(gram, 'core')  4.88 us
    pallas_call x1, Pallas kernels, body(): call(inside, ((LAT, ALL, LON), square, square), [wide, wide, thin, thin,...  2.68 us
    ppermute x1, starting transfers between devices, body(): near = lax.ppermute(near, COL, [(i, i ^ 1) for i in range(32)])  2.27 us
    pallas_call x1, Pallas kernels, body(): call(edge_rows, (edge, edge, (B * LAT, LON), (LAT, LON)), [small, small,...  1.14 us
  transfers between devices with their start and end apart: 4, of which 2 were waited for; matrix products, arithmetic and copies ran while one was open for 0% of the time, Pallas kernels for 6%

profile of v6, /device:TPU:8, one launch (start us, length us, event | category | flops | bytes accessed | tf_op | source)
XLA Modules:
  0.0 55.9 jit_solution(14249728649734546814)
XLA Ops:
  0.6 1.1 %shard_map.58 = (f32[3,40,128]{2,1,0:T(8,128)S(1)}, f32[3,40,128]{2,1,0:T(8,128)S(1)}, f32[1024,128]{1,0:T(8,128)S(1)}, f32[32,128]{1,0:T(8,128)S(1)}) custom-call(f32[1024,128]{1,0:T(8,128)} %bitcast.3, s32[32,128]{1,0:T(8,128)} %mask_hbm.1, s32[32,128]{1,0:T(8,128)} %depth_hbm.1), custom_call_target="tpu_custom_call" | custom-call | tf_op jit(solution)/shard_map/pallas_call | solution.py:414
  1.8 0.1 collective-permute-start
  1.9 0.7 %collective-permute-start.1 = (f32[3,40,128]{2,1,0:T(8,128)S(1)}, f32[3,40,128]{2,1,0:T(8,128)S(1)}, u32[]{:S(2)}, u32[]{:S(2)}) collective-permute-start(f32[3,40,128]{2,1,0:T(8,128)S(1)} %get-tuple-element.23), channel_id=1, source_target_pairs={{32,64},{64,32},{96,128},{128,96},{160,192},{192,160},{33,65},{65,... | collective-permute-start | bytes 184328 | tf_op jit(solution)/shard_map/ppermute | solution.py:420
  2.5 0.5 shard_map.59
  3.0 0.1 collective-permute-done.near_ref
  3.1 0.0 collective-permute-done.1.far_ref
  3.1 0.2 shard_map.60
  3.3 2.3 %collective-permute-start.2 = (f32[40,384]{1,0:T(8,128)S(1)}, f32[40,384]{1,0:T(8,128)S(1)}, u32[]{:S(2)}, u32[]{:S(2)}) collective-permute-start(f32[40,384]{1,0:T(8,128)S(1)} %get-tuple-element.28), channel_id=1, source_target_pairs={{0,1},{1,0},{2,3},{3,2},{4,5},{5,4},{6,7},{7,6},{8,9},{9,8},{10,11... | collective-permute-start | bytes 184328 | tf_op jit(solution)/shard_map/ppermute | solution.py:430
  5.6 0.7 %collective-permute-start.3 = (f32[40,384]{1,0:T(8,128)S(1)}, f32[40,384]{1,0:T(8,128)S(1)}, u32[]{:S(2)}, u32[]{:S(2)}) collective-permute-start(f32[40,384]{1,0:T(8,128)S(1)} %get-tuple-element.29), channel_id=1, source_target_pairs={{0,31},{1,2},{2,1},{3,4},{4,3},{5,6},{6,5},{7,8},{8,7},{9,10},{10,... | collective-permute-start | bytes 184328 | tf_op jit(solution)/shard_map/ppermute | solution.py:429
  6.3 2.7 %shard_map.61 = (f32[32,128,128]{2,1,0:T(8,128)S(1)}, f32[128,128]{1,0:T(8,128)S(1)}, f32[128,128]{1,0:T(8,128)S(1)}) custom-call(f32[32,40,128]{2,1,0:T(8,128)S(1)} %get-tuple-element.32.core_ref, f32[3,40,128]{2,1,0:T(8,128)S(1)} %get-tuple-element.33.north_ref, f32[3,40,128]{2,1,0:T(8,128)S(1)} %get-tuple-element.34.south_ref), custom_call_target="tpu_custom_call" | custom-call | flops 268435456 | bytes 8388608 | tf_op jit(solution)/shard_map/pallas_call | solution.py:434
  9.0 0.0 collective-permute-done.2.near_ref
  9.0 0.8 %collective-permute-done.3.far_ref = f32[40,384]{1,0:T(8,128)S(1)} collective-permute-done((f32[40,384]{1,0:T(8,128)S(1)}, f32[40,384]{1,0:T(8,128)S(1)}, u32[]{:S(2)}, u32[]{:S(2)}) %collective-permute-start.3) | collective-permute-done | bytes 61472 | tf_op jit(solution)/shard_map/ppermute | solution.py:429
  9.8 1.1 %shard_map.62 = (f32[32,128]{1,0:T(8,128)S(1)}, f32[96,384]{1,0:T(8,128)S(1)}, f32[96,384]{1,0:T(8,128)S(1)}) custom-call(f32[40,384]{1,0:T(8,128)S(1)} %collective-permute-done.2.near_ref, f32[40,384]{1,0:T(8,128)S(1)} %collective-permute-done.3.far_ref, f32[40,384]{1,0:T(8,128)S(1)} %get-tuple-element.30.own_west_ref, ...), custom_call_target="tpu_custom_call" | custom-call | tf_op jit(solution)/shard_map/pallas_call | solution.py:438
  10.9 4.9 %all-gather = f32[64,128]{1,0:T(8,128)S(1)} all-gather(f32[32,128]{1,0:T(8,128)S(1)} %get-tuple-element.37), channel_id=2, replica_groups=mesh['x'=4,'core'=2,'z'=8,'y'=4] {'core'}, dimensions={0}, use_global_device_ids=true | all-gather | bytes 49152 | tf_op jit(solution)/shard_map/all_gather | solution.py:439
  15.8 18.5 %all_to_all.10.parts_ref = f32[16,32,128]{2,1,0:T(8,128)S(1)} all-to-all(f32[16,32,128]{2,1,0:T(8,128)S(1)} %shard_map.63), channel_id=1, replica_groups=mesh['x'=4,'core'=2,'z'=8,'y'=4] {'x','y'}, dimensions={0} | all-to-all | bytes 524288 | tf_op jit(solution)/shard_map/all_to_all | solution.py:441
  34.4 15.1 %all_to_all.11.parts_ref = f32[8,32,128]{2,1,0:T(8,128)S(1)} all-to-all(f32[8,32,128]{2,1,0:T(8,128)S(1)} %shard_map.64), channel_id=1, replica_groups=mesh['x'=4,'core'=2,'z'=8,'y'=4] {'z'}, dimensions={0} | all-to-all | bytes 262144 | tf_op jit(solution)/shard_map/all_to_all | solution.py:443
  49.5 6.4 %shard_map.65 = (f32[128,32,128]{2,1,0:T(8,128)}, f32[3,32,32]{2,1,0:T(8,128)}, f32[3,32,32]{2,1,0:T(8,128)}) custom-call(f32[8,32,128]{2,1,0:T(8,128)S(1)} %all_to_all.11.parts_ref, f32[32,128,128]{2,1,0:T(8,128)S(1)} %get-tuple-element.38.s_ref, f32[96,384]{1,0:T(8,128)S(1)} %get-tuple-element.39.west_ref, f32[96,384]{1,0:T(8,128)S(1)} %get-tuple-element.40.east_ref), custom_call_target="tpu_custom_call" | custom-call | tf_op jit(solution)/shard_map/pallas_call | solution.py:446
  (2 shorter events, 0.0 us)
Async XLA Ops:
  1.8 1.3 %collective-permute-start = (f32[3,40,128]{2,1,0:T(8,128)S(1)}, f32[3,40,128]{2,1,0:T(8,128)S(1)}, u32[]{:S(2)}, u32[]{:S(2)}) collective-permute-start(f32[3,40,128]{2,1,0:T(8,128)S(1)} %get-tuple-element.22), channel_id=1, source_target_pairs={{0,32},{32,0},{64,96},{96,64},{128,160},{160,128},{192,224},{224,1... | collective-permute-start | bytes 184328 | tf_op jit(solution)/shard_map/ppermute | solution.py:421
  1.9 1.2 %collective-permute-start.1 = (f32[3,40,128]{2,1,0:T(8,128)S(1)}, f32[3,40,128]{2,1,0:T(8,128)S(1)}, u32[]{:S(2)}, u32[]{:S(2)}) collective-permute-start(f32[3,40,128]{2,1,0:T(8,128)S(1)} %get-tuple-element.23), channel_id=1, source_target_pairs={{32,64},{64,32},{96,128},{128,96},{160,192},{192,160},{33,65},{65,... | collective-permute-start | bytes 184328 | tf_op jit(solution)/shard_map/ppermute | solution.py:420
  3.3 5.6 %collective-permute-start.2 = (f32[40,384]{1,0:T(8,128)S(1)}, f32[40,384]{1,0:T(8,128)S(1)}, u32[]{:S(2)}, u32[]{:S(2)}) collective-permute-start(f32[40,384]{1,0:T(8,128)S(1)} %get-tuple-element.28), channel_id=1, source_target_pairs={{0,1},{1,0},{2,3},{3,2},{4,5},{5,4},{6,7},{7,6},{8,9},{9,8},{10,11... | collective-permute-start | bytes 184328 | tf_op jit(solution)/shard_map/ppermute | solution.py:430
  5.6 4.2 %collective-permute-start.3 = (f32[40,384]{1,0:T(8,128)S(1)}, f32[40,384]{1,0:T(8,128)S(1)}, u32[]{:S(2)}, u32[]{:S(2)}) collective-permute-start(f32[40,384]{1,0:T(8,128)S(1)} %get-tuple-element.29), channel_id=1, source_target_pairs={{0,31},{1,2},{2,1},{3,4},{4,3},{5,6},{6,5},{7,8},{8,7},{9,10},{10,... | collective-permute-start | bytes 184328 | tf_op jit(solution)/shard_map/ppermute | solution.py:429

commit v7 on v6

--- a/solution.py
+++ b/solution.py
@@ -8,7 +8,6 @@
 ITERS = 3
 LEVELS = 50.0
 KAPPA = 1.5
-SHIFT = 3.0
 CELLS = 1048576.0
 
 B = 32
@@ -89,7 +88,7 @@
     east_ref[...] = jnp.concatenate(east, axis=1)
 
 
-def side_columns(near_ref, far_ref, part_west_ref, part_east_ref,
+def side_columns(far_ref, near_ref, part_west_ref, part_east_ref,
                  far_out, near_out, north_ref, south_ref, west_ref, east_ref):
     odd = lax.axis_index("core") == 1
     west, east = chunks(part_west_ref[...]), chunks(part_east_ref[...])
@@ -131,7 +130,7 @@
     return both[:, :ALL] + outer(middle, middle), both[:, ALL:] + outer(high, low)
 
 
-def inside(core_ref, north_ref, south_ref, s_ref, even_ref, half_ref, k1_ref, k2_ref, down_ref, right_ref, centre_ref):
+def inside(core_ref, north_ref, south_ref, s_ref, own_ref, k1_ref, k2_ref, down_ref, right_ref, centre_ref):
     def base(r):
         if r < RIM:
             return north_ref[r]
@@ -143,11 +142,11 @@
         right_ref[r] = KAPPA * jnp.minimum(h, pltpu.roll(h, LON - 1, 1))
         centre_ref[r] = jnp.where(h > 0.0, 0.0, -1.0)
     levels = (
-        (lambda r: base(r)[:B], k1_ref, 0.0),
-        (lambda r: k1_ref[r], k2_ref, SHIFT),
-        (lambda r: k2_ref[r], None, SHIFT),
+        (lambda r: base(r)[:B], k1_ref),
+        (lambda r: k1_ref[r], k2_ref),
+        (lambda r: k2_ref[r], None),
     )
-    for step, (source, target, shift) in enumerate(levels):
+    for step, (source, target) in enumerate(levels):
         first, last = step + 1, ROWS - 2 - step
         v, after = source(first - 1), source(first)
         flux = four(down_ref[first - 1]) * (v - after)
@@ -155,7 +154,7 @@
             v, after = after, source(r + 1)
             down = four(down_ref[r]) * (v - after)
             right = four(right_ref[r]) * (v - pltpu.roll(v, LON - 1, 1))
-            new = four(centre_ref[r] - shift) * v + ((down - flux) + (right - pltpu.roll(right, 1, 1)))
+            new = four(centre_ref[r]) * v + ((down - flux) + (right - pltpu.roll(right, 1, 1)))
             flux = down
             if target is not None:
                 target[r] = new
@@ -172,11 +171,10 @@
         one, two = products(jnp.concatenate(rows, axis=1))
         even += one
         half += two
-    even_ref[...] = even
-    half_ref[...] = half
-
-
-def border(near_ref, far_ref, own_west_ref, own_east_ref, even_ref, half_ref, gram_ref, west_ref, east_ref):
+    own_ref[...] = even + half + half.T
+
+
+def border(far_ref, near_ref, own_west_ref, own_east_ref, own_ref, gram_ref, west_ref, east_ref):
     odd = lax.axis_index("y") % 2 == 1
     near, far = near_ref[...], far_ref[...]
     lane = lax.broadcasted_iota(jnp.int32, (B + 8, FLAT), 1)
@@ -189,24 +187,22 @@
     fields = []
     for start, out_ref in ((west, west_ref), (east, east_ref)):
         h = start[B:]
-        down = four(KAPPA * jnp.minimum(h, pltpu.roll(h, FLAT - SPAN, 1)))
-        right = four(jnp.where(joint, KAPPA * jnp.minimum(h, pltpu.roll(h, FLAT - 1, 1)), 0.0))
-        centre = jnp.where(h > 0.0, 0.0, -1.0)
+        south = KAPPA * jnp.minimum(h, pltpu.roll(h, FLAT - SPAN, 1))
+        right = jnp.where(joint, KAPPA * jnp.minimum(h, pltpu.roll(h, FLAT - 1, 1)), 0.0)
+        north, left = four(pltpu.roll(south, SPAN, 1)), four(pltpu.roll(right, 1, 1))
+        south, right = four(south), four(right)
+        centre = four(jnp.where(h > 0.0, 0.0, -1.0))
         v = start[:B]
         found = [v]
-        for shift in (0.0, SHIFT, SHIFT):
-            flow = down * (v - pltpu.roll(v, FLAT - SPAN, 1))
-            side = right * (v - pltpu.roll(v, FLAT - 1, 1))
-            v = four(centre - shift) * v + (
-                (flow - pltpu.roll(flow, SPAN, 1)) + (side - pltpu.roll(side, 1, 1))
-            )
+        for step in range(ITERS):
+            down = south * (v - pltpu.roll(v, FLAT - SPAN, 1)) + north * (v - pltpu.roll(v, SPAN, 1))
+            over = right * (v - pltpu.roll(v, FLAT - 1, 1)) + left * (v - pltpu.roll(v, 1, 1))
+            v = centre * v + (down + over)
             found.append(v)
         out_ref[...] = jnp.concatenate(found[1:], axis=0)
         fields.append(jnp.where(kept, jnp.concatenate(found, axis=0), 0.0))
     even, half = products(jnp.concatenate(fields, axis=1))
-    even += even_ref[...]
-    half += half_ref[...]
-    gram = even + half + half.T
+    gram = (own_ref[...] + even) + (half + half.T)
     row = lax.broadcasted_iota(jnp.int32, (B, LON), 0)
     lane = lax.broadcasted_iota(jnp.int32, (B, LON), 1)
     packed = diagonal = jnp.zeros((B, LON), jnp.float32)
@@ -231,15 +227,18 @@
         out_ref[i] = total
 
 
+def join(own_ref, other_ref, out_ref):
+    total = own_ref[...] + other_ref[...]
+    for i in range(out_ref.shape[0]):
+        out_ref[i] = total
+
+
 def unpack(total):
     row = lax.broadcasted_iota(jnp.int32, (B, LON), 0)
     lane = lax.broadcasted_iota(jnp.int32, (B, LON), 1)
     block, place = lane >> 5, lane & (B - 1)
-    turned = jnp.concatenate([total, jnp.zeros((LON - B, LON), jnp.float32)], axis=0).T
-    mirror = jnp.zeros((B, LON), jnp.float32)
-    for k in range(ITERS + 1):
-        part = turned[k * B:(k + 1) * B]
-        mirror = jnp.where(block == k, pltpu.roll(part, k * B, 1) if k else part, mirror)
+    turned = jnp.concatenate([jnp.where(block == k, total, 0.0) for k in range(ITERS + 1)], axis=0).T
+    mirror = (turned[:B] + turned[B:2 * B]) + (turned[2 * B:3 * B] + turned[3 * B:])
     even = jnp.where(place >= row, total, mirror)
     odd = jnp.where(place < row, total, mirror)
     line = jnp.zeros((1, LON), jnp.float32)
@@ -249,25 +248,22 @@
         line = jnp.where((lane[:1] >= target) & (lane[:1] < target + HALF), moved, line)
     odd = jnp.where(place == row, line, odd)
     move = lambda field, k: pltpu.roll(field, (k * B) % LON, 1)
-    even1, even2, odd1, odd2, odd3 = move(even, 1), move(even, -1), move(odd, 1), move(odd, 2), move(odd, 3)
     pick = lambda a, b, c, d: jnp.where(block == 0, a, jnp.where(block == 1, b, jnp.where(block == 2, c, d)))
-    corner = move(odd, -1)
-    return jnp.concatenate(
-        [
-            pick(even, odd1, even1 - SHIFT * odd2, odd2 - SHIFT * (move(even, 2) - SHIFT * odd3)),
-            pick(odd, even, odd1, even1),
-            pick(even2 - SHIFT * odd, odd, even, odd1),
-            pick(corner - SHIFT * (even2 - SHIFT * odd), even2, odd, even),
-        ],
-        axis=0,
-    )
+    even_on, even_back, odd_on, odd_back = move(even, 1), move(even, -1), move(odd, 1), move(odd, -1)
+    rows = [
+        pick(even, odd_on, even_on, move(odd, 2)),
+        pick(odd, even, odd_on, even_on),
+        pick(even_back, odd, even, odd_on),
+        pick(odd_back, even_back, odd, even),
+    ]
+    return even, jnp.concatenate(rows, axis=0)
 
 
 def reciprocal(value):
     return 1.0 / value
 
 
-def factor(gram):
+def factor(first, gram):
     groups = ALL // 8
     lane = lax.broadcasted_iota(jnp.int32, (8, ALL), 1)
     sub = lax.broadcasted_iota(jnp.int32, (8, ALL), 0)
@@ -280,7 +276,7 @@
     diagonal = sum(jnp.where(lane == sub + 8 * g, work[g], 0.0) for g in range(groups))
     guess = full(reciprocal(jnp.sum(diagonal, axis=0, keepdims=True)))
     uppers, inverses = [], []
-    own, after = columns(0, 0), columns(1, 0)
+    own, after = [[full(first[8 * k:8 * k + 8, t:t + 1]) for t in range(8)] for k in range(2)]
     for g in range(groups):
         later, coming = columns(g + 2, g), columns(g + 1, g + 1)
         a = work[g]
@@ -366,10 +362,9 @@
     total = parts_ref[0]
     for i in range(1, parts_ref.shape[0]):
         total += parts_ref[i]
-    inverse, upper = factor(unpack(total * (1.0 / CELLS)))
+    inverse, upper = factor(*unpack(total * (1.0 / CELLS)))
     lane = lax.broadcasted_iota(jnp.int32, (ALL, ALL), 1)
-    own = jnp.where(lane < B, 1.0, jnp.where(lane < ITERS * B, 1.0 + SHIFT, 0.0))
-    image = inverse * own + jnp.where(lane >= B, pltpu.roll(inverse, B, 1), 0.0)
+    image = jnp.where(lane < ITERS * B, inverse, 0.0) + jnp.where(lane >= B, pltpu.roll(inverse, B, 1), 0.0)
     coeffs = lax.dot_general(upper, image, NT, precision=HIGH, preferred_element_type=jnp.float32)
     for k in range(ITERS):
         here, after = slice(k * B, (k + 1) * B), slice((k + 1) * B, (k + 2) * B)
@@ -424,20 +419,20 @@
         core_rows, ((LAT, B + 8, LON), flat, flat), flops=1 << 22, moved=1 << 20
     )(x, h)
     far, near, north, south, own_west, own_east = call(side_columns, (flat, flat, edge, edge, flat, flat))(
-        near, far, part_west, part_east
+        far, near, part_west, part_east
     )
     far = lax.ppermute(far, COL, [(i, (((i + 1) ^ 1) - 1) % 32) for i in range(32)])
     near = lax.ppermute(near, COL, [(i, i ^ 1) for i in range(32)])
     wide = pltpu.VMEM((ROWS, B, LON), jnp.float32)
     thin = pltpu.VMEM((ROWS, 8, LON), jnp.float32)
     square = (ALL, ALL)
-    s, even, half = call(
-        inside, ((LAT, ALL, LON), square, square), [wide, wide, thin, thin, thin], flops=1 << 28, moved=1 << 23
+    s, own = call(
+        inside, ((LAT, ALL, LON), square), [wide, wide, thin, thin, thin], flops=1 << 28, moved=1 << 23
     )(core, north, south)
     rim = (ALL - B, FLAT)
-    gram, west, east = call(border, ((B, LON), rim, rim))(near, far, own_west, own_east, even, half)
-    pair = lax.all_gather(gram, "core")
-    copies = call(spread, ((16, B, LON),))(pair)[0]
+    gram, west, east = call(border, ((B, LON), rim, rim))(far, near, own_west, own_east, own)
+    other = lax.ppermute(gram, ROW, [(i, i ^ 1) for i in range(8)])
+    copies = call(join, ((16, B, LON),))(gram, other)[0]
     parts = lax.all_to_all(copies, ("x", "y"), 0, 0)
     copies = call(spread, ((8, B, LON),))(parts)[0]
     parts = lax.all_to_all(copies, "z", 0, 0)

time: 56.2 us -> 54.6 us (0.972)
  blocking collectives: 38.5 us -> 27.5 us
  starting transfers between devices: 3.7 us -> 12.8 us
    ppermute x1, starting transfers between devices: 2.27 us -> 7.18 us  [body(): near = lax.ppermute(near, COL, [(i, i ^ 1) for i in range(32)])]
    all_gather x1 -> x0, blocking collectives: 4.88 us -> none  [body(): pair = lax.all_gather(gram, 'core')]
    all_to_all x1, blocking collectives: 18.5 us -> 13.9 us  [body(): parts = lax.all_to_all(copies, ('x', 'y'), 0, 0)]
    ppermute x1, starting transfers between devices: 0.09 us -> 2.94 us  [body(): near = lax.ppermute(near, ROW, [(i, i ^ 1) for i in range(8)])]
    all_to_all x1, blocking collectives: 15.1 us -> 13.6 us  [body(): parts = lax.all_to_all(copies, 'z', 0, 0)]
    ppermute x1, starting transfers between devices: 0.67 us -> 1.66 us  [body(): lax.ppermute(far, COL, [(i, ((i + 1 ^ 1) - 1) % 32) for i in range(32)])]
    ppermute x0 -> x1, waiting for transfers between devices: none -> 0.87 us  [body(): other = lax.ppermute(gram, ROW, [(i, i ^ 1) for i in range(8)])]
    ppermute x1, waiting for transfers between devices: 0.85 us -> 0.01 us  [body(): lax.ppermute(far, COL, [(i, ((i + 1 ^ 1) - 1) % 32) for i in range(32)])]
  transfers between devices with their start and end apart: 4 -> 5, of which waited for: 2 -> 3; matrix products, arithmetic and copies ran while one was open for 0% -> 0% of each run, Pallas kernels for 6% -> 6%
where the time goes in v7:
time: 54.6 us; the launch traced here: 54.3 us
  blocking collectives  27.5 us (50%)
  starting transfers between devices  12.8 us (23%)
  Pallas kernels  11.9 us (22%)
  waiting for transfers between devices  1.32 us (2%)
  between operations  0.71 us (1%)
    all_to_all x1, blocking collectives, body(): parts = lax.all_to_all(copies, ('x', 'y'), 0, 0)  13.9 us
    all_to_all x1, blocking collectives, body(): parts = lax.all_to_all(copies, 'z', 0, 0)  13.6 us
    ppermute x1, starting transfers between devices, body(): near = lax.ppermute(near, COL, [(i, i ^ 1) for i in range(32)])  7.18 us
    pallas_call x1, Pallas kernels, body(): call(basis, results, [pltpu.VMEM(shape, jnp.float32) for shape in results...  6.34 us
    ppermute x1, starting transfers between devices, body(): near = lax.ppermute(near, ROW, [(i, i ^ 1) for i in range(8)])  2.94 us
    pallas_call x1, Pallas kernels, body(): call(inside, ((LAT, ALL, LON), square), [wide, wide, thin, thin, thin], f...  2.73 us
    ppermute x1, starting transfers between devices, body(): lax.ppermute(far, COL, [(i, ((i + 1 ^ 1) - 1) % 32) for i in range(32)])  1.66 us
    pallas_call x1, Pallas kernels, body(): call(edge_rows, (edge, edge, (B * LAT, LON), (LAT, LON)), [small, small,...  1.14 us
  transfers between devices with their start and end apart: 5, of which 3 were waited for; matrix products, arithmetic and copies ran while one was open for 0% of the time, Pallas kernels for 6%

profile of v7, /device:TPU:8, one launch (start us, length us, event | category | flops | bytes accessed | tf_op | source)
XLA Modules:
  0.0 54.3 jit_solution(265512486281900065)
XLA Ops:
  0.6 1.1 %shard_map.58 = (f32[3,40,128]{2,1,0:T(8,128)S(1)}, f32[3,40,128]{2,1,0:T(8,128)S(1)}, f32[1024,128]{1,0:T(8,128)S(1)}, f32[32,128]{1,0:T(8,128)S(1)}) custom-call(f32[1024,128]{1,0:T(8,128)} %bitcast.1, s32[32,128]{1,0:T(8,128)} %mask_hbm.1, s32[32,128]{1,0:T(8,128)} %depth_hbm.1), custom_call_target="tpu_custom_call" | custom-call | tf_op jit(solution)/shard_map/pallas_call | solution.py:409
  1.8 0.7 %collective-permute-start = (f32[3,40,128]{2,1,0:T(8,128)S(1)}, f32[3,40,128]{2,1,0:T(8,128)S(1)}, u32[]{:S(2)}, u32[]{:S(2)}) collective-permute-start(f32[3,40,128]{2,1,0:T(8,128)S(1)} %get-tuple-element.21), channel_id=1, source_target_pairs={{32,64},{64,32},{96,128},{128,96},{160,192},{192,160},{33,65},{65,... | collective-permute-start | bytes 184328 | tf_op jit(solution)/shard_map/ppermute | solution.py:415
  2.4 2.9 %collective-permute-start.1 = (f32[3,40,128]{2,1,0:T(8,128)S(1)}, f32[3,40,128]{2,1,0:T(8,128)S(1)}, u32[]{:S(2)}, u32[]{:S(2)}) collective-permute-start(f32[3,40,128]{2,1,0:T(8,128)S(1)} %get-tuple-element.22), channel_id=1, source_target_pairs={{0,32},{32,0},{64,96},{96,64},{128,160},{160,128},{192,224},{224,1... | collective-permute-start | bytes 184328 | tf_op jit(solution)/shard_map/ppermute | solution.py:416
  5.4 0.5 shard_map.59
  5.9 0.0 collective-permute-done.far_ref
  5.9 0.4 collective-permute-done.1.near_ref
  6.3 0.2 shard_map.60
  6.5 1.7 %collective-permute-start.2 = (f32[40,384]{1,0:T(8,128)S(1)}, f32[40,384]{1,0:T(8,128)S(1)}, u32[]{:S(2)}, u32[]{:S(2)}) collective-permute-start(f32[40,384]{1,0:T(8,128)S(1)} %get-tuple-element.27), channel_id=1, source_target_pairs={{0,31},{1,2},{2,1},{3,4},{4,3},{5,6},{6,5},{7,8},{8,7},{9,10},{10,... | collective-permute-start | bytes 184328 | tf_op jit(solution)/shard_map/ppermute | solution.py:424
  8.2 7.2 %collective-permute-start.3 = (f32[40,384]{1,0:T(8,128)S(1)}, f32[40,384]{1,0:T(8,128)S(1)}, u32[]{:S(2)}, u32[]{:S(2)}) collective-permute-start(f32[40,384]{1,0:T(8,128)S(1)} %get-tuple-element.28), channel_id=1, source_target_pairs={{0,1},{1,0},{2,3},{3,2},{4,5},{5,4},{6,7},{7,6},{8,9},{9,8},{10,11... | collective-permute-start | bytes 184328 | tf_op jit(solution)/shard_map/ppermute | solution.py:425
  15.3 2.7 %shard_map.61 = (f32[32,128,128]{2,1,0:T(8,128)S(1)}, f32[128,128]{1,0:T(8,128)S(1)}) custom-call(f32[32,40,128]{2,1,0:T(8,128)S(1)} %get-tuple-element.31.core_ref, f32[3,40,128]{2,1,0:T(8,128)S(1)} %get-tuple-element.32.north_ref, f32[3,40,128]{2,1,0:T(8,128)S(1)} %get-tuple-element.33.south_ref), custom_call_target="tpu_custom_call" | custom-call | flops 268435456 | bytes 8388608 | tf_op jit(solution)/shard_map/pallas_call | solution.py:429
  18.1 0.0 collective-permute-done.2.far_ref
  18.1 0.1 collective-permute-done.3.near_ref
  18.1 1.0 %shard_map.62 = (f32[32,128]{1,0:T(8,128)S(1)}, f32[96,384]{1,0:T(8,128)S(1)}, f32[96,384]{1,0:T(8,128)S(1)}) custom-call(f32[40,384]{1,0:T(8,128)S(1)} %collective-permute-done.2.far_ref, f32[40,384]{1,0:T(8,128)S(1)} %collective-permute-done.3.near_ref, f32[40,384]{1,0:T(8,128)S(1)} %get-tuple-element.29.own_west_ref, ...), custom_call_target="tpu_custom_call" | custom-call | tf_op jit(solution)/shard_map/pallas_call | solution.py:433
  19.1 0.4 collective-permute-start.4
  19.5 0.9 %collective-permute-done.4.other_ref = f32[32,128]{1,0:T(8,128)S(1)} collective-permute-done((f32[32,128]{1,0:T(8,128)S(1)}, f32[32,128]{1,0:T(8,128)S(1)}, u32[]{:S(2)}, u32[]{:S(2)}) %collective-permute-start.4) | collective-permute-done | bytes 16416 | tf_op jit(solution)/shard_map/ppermute | solution.py:434
  20.4 13.9 %all_to_all.10.parts_ref = f32[16,32,128]{2,1,0:T(8,128)S(1)} all-to-all(f32[16,32,128]{2,1,0:T(8,128)S(1)} %shard_map.63), channel_id=1, replica_groups=mesh['x'=4,'core'=2,'z'=8,'y'=4] {'x','y'}, dimensions={0} | all-to-all | bytes 524288 | tf_op jit(solution)/shard_map/all_to_all | solution.py:436
  34.4 13.6 %all_to_all.11.parts_ref = f32[8,32,128]{2,1,0:T(8,128)S(1)} all-to-all(f32[8,32,128]{2,1,0:T(8,128)S(1)} %shard_map.64), channel_id=1, replica_groups=mesh['x'=4,'core'=2,'z'=8,'y'=4] {'z'}, dimensions={0} | all-to-all | bytes 262144 | tf_op jit(solution)/shard_map/all_to_all | solution.py:438
  48.0 6.3 %shard_map.65 = (f32[128,32,128]{2,1,0:T(8,128)}, f32[3,32,32]{2,1,0:T(8,128)}, f32[3,32,32]{2,1,0:T(8,128)}) custom-call(f32[8,32,128]{2,1,0:T(8,128)S(1)} %all_to_all.11.parts_ref, f32[32,128,128]{2,1,0:T(8,128)S(1)} %get-tuple-element.36.s_ref, f32[96,384]{1,0:T(8,128)S(1)} %get-tuple-element.37.west_ref, f32[96,384]{1,0:T(8,128)S(1)} %get-tuple-element.38.east_ref), custom_call_target="tpu_custom_call" | custom-call | tf_op jit(solution)/shard_map/pallas_call | solution.py:441
  (2 shorter events, 0.0 us)
Async XLA Ops:
  1.8 4.1 %collective-permute-start = (f32[3,40,128]{2,1,0:T(8,128)S(1)}, f32[3,40,128]{2,1,0:T(8,128)S(1)}, u32[]{:S(2)}, u32[]{:S(2)}) collective-permute-start(f32[3,40,128]{2,1,0:T(8,128)S(1)} %get-tuple-element.21), channel_id=1, source_target_pairs={{32,64},{64,32},{96,128},{128,96},{160,192},{192,160},{33,65},{65,... | collective-permute-start | bytes 184328 | tf_op jit(solution)/shard_map/ppermute | solution.py:415
  2.4 3.8 %collective-permute-start.1 = (f32[3,40,128]{2,1,0:T(8,128)S(1)}, f32[3,40,128]{2,1,0:T(8,128)S(1)}, u32[]{:S(2)}, u32[]{:S(2)}) collective-permute-start(f32[3,40,128]{2,1,0:T(8,128)S(1)} %get-tuple-element.22), channel_id=1, source_target_pairs={{0,32},{32,0},{64,96},{96,64},{128,160},{160,128},{192,224},{224,1... | collective-permute-start | bytes 184328 | tf_op jit(solution)/shard_map/ppermute | solution.py:416
  6.5 11.6 %collective-permute-start.2 = (f32[40,384]{1,0:T(8,128)S(1)}, f32[40,384]{1,0:T(8,128)S(1)}, u32[]{:S(2)}, u32[]{:S(2)}) collective-permute-start(f32[40,384]{1,0:T(8,128)S(1)} %get-tuple-element.27), channel_id=1, source_target_pairs={{0,31},{1,2},{2,1},{3,4},{4,3},{5,6},{6,5},{7,8},{8,7},{9,10},{10,... | collective-permute-start | bytes 184328 | tf_op jit(solution)/shard_map/ppermute | solution.py:424
  8.2 10.0 %collective-permute-start.3 = (f32[40,384]{1,0:T(8,128)S(1)}, f32[40,384]{1,0:T(8,128)S(1)}, u32[]{:S(2)}, u32[]{:S(2)}) collective-permute-start(f32[40,384]{1,0:T(8,128)S(1)} %get-tuple-element.28), channel_id=1, source_target_pairs={{0,1},{1,0},{2,3},{3,2},{4,5},{5,4},{6,7},{7,6},{8,9},{9,8},{10,11... | collective-permute-start | bytes 184328 | tf_op jit(solution)/shard_map/ppermute | solution.py:425
  19.1 1.3 %collective-permute-start.4 = (f32[32,128]{1,0:T(8,128)S(1)}, f32[32,128]{1,0:T(8,128)S(1)}, u32[]{:S(2)}, u32[]{:S(2)}) collective-permute-start(f32[32,128]{1,0:T(8,128)S(1)} %get-tuple-element.35.own_ref), channel_id=1, source_target_pairs={{0,32},{32,0},{64,96},{96,64},{128,160},{160,128},{192,224},{224,1... | collective-permute-start | bytes 49160 | tf_op jit(solution)/shard_map/ppermute | solution.py:434

commit v8 on v7

--- a/solution.py
+++ b/solution.py
@@ -15,8 +15,7 @@
 LON = 128
 RIM = 3
 ROWS = LAT + 2 * RIM
-SPAN = 3 * RIM
-FLAT = 3 * LON
+STARTS = (0, RIM, LON - 2 * RIM, LON - RIM)
 ALL = (ITERS + 1) * B
 HALF = B // 2
 PIECE = 64
@@ -24,6 +23,7 @@
 HIGH = lax.Precision.HIGHEST
 ROW, COL = ("x", "core"), ("z", "y")
 NT = (((1,), (1,)), ((), ()))
+TN = (((0,), (0,)), ((), ()))
 PARAMS = pltpu.CompilerParams(vmem_limit_bytes=48 * 1024 * 1024)
 
 
@@ -65,47 +65,37 @@
     return jnp.concatenate([row, jnp.broadcast_to(depth, (8, LON))], axis=0)
 
 
-def pack_sides(row, r, west, east):
+def pack_sides(row, r, packed):
     lane = lanes_of(B + 8)
-    for sides, source, target in ((west, 0, SPAN * r + RIM), (east, LON - 2 * RIM, SPAN * r)):
-        moved = pltpu.roll(row, (target - source) % LON, 1)
-        for k in range(target // LON, (target + 2 * RIM - 1) // LON + 1):
-            place = lane + k * LON
-            sides[k] = jnp.where((place >= target) & (place < target + 2 * RIM), moved, sides[k])
-
-
-def chunks(flat):
-    return [flat[:, k * LON:(k + 1) * LON] for k in range(FLAT // LON)]
-
-
-def core_rows(x_ref, h_ref, core_ref, west_ref, east_ref):
-    west, east = chunks(jnp.zeros((B + 8, FLAT), jnp.float32)), chunks(jnp.zeros((B + 8, FLAT), jnp.float32))
+    here = (lane >= RIM * r) & (lane < RIM * r + RIM)
+    return [jnp.where(here, pltpu.roll(row, (RIM * r - start) % LON, 1), p) for p, start in zip(packed, STARTS)]
+
+
+def core_rows(x_ref, h_ref, core_ref, packed_ref):
+    packed = [jnp.zeros((B + 8, LON), jnp.float32)] * len(STARTS)
     for i in range(LAT):
         row = masked_row(i, x_ref, h_ref)
         core_ref[i] = row
-        pack_sides(row, i + RIM, west, east)
-    west_ref[...] = jnp.concatenate(west, axis=1)
-    east_ref[...] = jnp.concatenate(east, axis=1)
-
-
-def side_columns(far_ref, near_ref, part_west_ref, part_east_ref,
-                 far_out, near_out, north_ref, south_ref, west_ref, east_ref):
+        packed = pack_sides(row, i + RIM, packed)
+    for k, value in enumerate(packed):
+        packed_ref[k] = value
+
+
+def side_columns(far_ref, near_ref, part_ref, far_out, near_out, north_ref, south_ref, packed_ref):
     odd = lax.axis_index("core") == 1
-    west, east = chunks(part_west_ref[...]), chunks(part_east_ref[...])
+    packed = [part_ref[k] for k in range(len(STARTS))]
     for i in range(RIM):
         north = jnp.where(odd, near_ref[i], far_ref[i])
         south = jnp.where(odd, far_ref[i], near_ref[i])
         north_ref[i] = north
         south_ref[i] = south
-        pack_sides(north, i, west, east)
-        pack_sides(south, i + RIM + LAT, west, east)
-    west, east = jnp.concatenate(west, axis=1), jnp.concatenate(east, axis=1)
-    west_ref[...] = west
-    east_ref[...] = east
-    to_west, to_east = pltpu.roll(west, RIM, 1), pltpu.roll(east, FLAT - RIM, 1)
+        packed = pack_sides(north, i, packed)
+        packed = pack_sides(south, i + RIM + LAT, packed)
+    for k, value in enumerate(packed):
+        packed_ref[k] = value
     odd = lax.axis_index("y") % 2 == 1
-    near_out[...] = jnp.where(odd, to_west, to_east)
-    far_out[...] = jnp.where(odd, to_east, to_west)
+    near_out[...] = jnp.where(odd, packed[0], packed[3])
+    far_out[...] = jnp.where(odd, packed[3], packed[0])
 
 
 def split(value):
@@ -174,35 +164,57 @@
     own_ref[...] = even + half + half.T
 
 
-def border(far_ref, near_ref, own_west_ref, own_east_ref, own_ref, gram_ref, west_ref, east_ref):
+def border(far_ref, near_ref, packed_ref, own_ref, gram_ref, west_ref, east_ref):
     odd = lax.axis_index("y") % 2 == 1
     near, far = near_ref[...], far_ref[...]
-    lane = lax.broadcasted_iota(jnp.int32, (B + 8, FLAT), 1)
-    line = (lane * 7282) >> 16
-    place = lane - line * SPAN
-    west = jnp.where(place < RIM, jnp.where(odd, near, far), own_west_ref[...])
-    east = jnp.where(place >= 2 * RIM, jnp.where(odd, far, near), own_east_ref[...])
-    joint = place[:8] < SPAN - 1
-    kept = (place[:1] >= RIM) & (place[:1] < 2 * RIM) & (line[:1] >= RIM) & (line[:1] < RIM + LAT)
+    lane = lanes_of(B)
+    line = (lane * 21846) >> 16
+    place = lane - RIM * line
+    first, last = place == 0, place == RIM - 1
+    kept = (line[:1] >= RIM) & (line[:1] < RIM + LAT)
+    move = lambda value, by: pltpu.roll(value, by % LON, 1)
+
+    def rightward(values, i):
+        inner = move(values[i], -1)
+        return jnp.where(last[:inner.shape[0]], move(values[i + 1], RIM - 1), inner) if i < 2 else inner
+
+    def leftward(values, i):
+        inner = move(values[i], 1)
+        return jnp.where(first[:inner.shape[0]], move(values[i - 1], 1 - RIM), inner) if i > 0 else inner
+
     fields = []
-    for start, out_ref in ((west, west_ref), (east, east_ref)):
-        h = start[B:]
-        south = KAPPA * jnp.minimum(h, pltpu.roll(h, FLAT - SPAN, 1))
-        right = jnp.where(joint, KAPPA * jnp.minimum(h, pltpu.roll(h, FLAT - 1, 1)), 0.0)
-        north, left = four(pltpu.roll(south, SPAN, 1)), four(pltpu.roll(right, 1, 1))
-        south, right = four(south), four(right)
-        centre = four(jnp.where(h > 0.0, 0.0, -1.0))
-        v = start[:B]
-        found = [v]
+    for chain, out_ref in (
+        ((jnp.where(odd, near, far), packed_ref[0], packed_ref[1]), west_ref),
+        ((packed_ref[2], packed_ref[3], jnp.where(odd, far, near)), east_ref),
+    ):
+        h = [part[B:] for part in chain]
+        south = [KAPPA * jnp.minimum(h[i], move(h[i], -RIM)) for i in range(3)]
+        right = [KAPPA * jnp.minimum(h[i], rightward(h, i)) for i in range(3)]
+        right[2] = jnp.where(last[:8], 0.0, right[2])
+        left = [leftward(right, i) for i in range(3)]
+        left[0] = jnp.where(first[:8], 0.0, left[0])
+        north = [four(move(value, RIM)) for value in south]
+        south, right, left = [[four(value) for value in values] for values in (south, right, left)]
+        centre = [four(jnp.where(value > 0.0, 0.0, -1.0)) for value in h]
+        v = [part[:B] for part in chain]
+        found = [v[1]]
         for step in range(ITERS):
-            down = south * (v - pltpu.roll(v, FLAT - SPAN, 1)) + north * (v - pltpu.roll(v, SPAN, 1))
-            over = right * (v - pltpu.roll(v, FLAT - 1, 1)) + left * (v - pltpu.roll(v, 1, 1))
-            v = centre * v + (down + over)
-            found.append(v)
+            v = [
+                centre[i] * v[i]
+                + (
+                    (south[i] * (v[i] - move(v[i], -RIM)) + north[i] * (v[i] - move(v[i], RIM)))
+                    + (right[i] * (v[i] - rightward(v, i)) + left[i] * (v[i] - leftward(v, i)))
+                )
+                for i in range(3)
+            ]
+            found.append(v[1])
         out_ref[...] = jnp.concatenate(found[1:], axis=0)
         fields.append(jnp.where(kept, jnp.concatenate(found, axis=0), 0.0))
-    even, half = products(jnp.concatenate(fields, axis=1))
-    gram = (own_ref[...] + even) + (half + half.T)
+    high, middle, low = split(jnp.concatenate(fields, axis=1))
+    both = jnp.concatenate([high, middle], axis=0)
+    both = outer(both, both)
+    large, small = both[:ALL, :ALL], both[:ALL, ALL:] + both[ALL:, :ALL]
+    gram = (own_ref[...] + large) + (small + (both[ALL:, ALL:] + (outer(high, low) + outer(low, high))))
     row = lax.broadcasted_iota(jnp.int32, (B, LON), 0)
     lane = lax.broadcasted_iota(jnp.int32, (B, LON), 1)
     packed = diagonal = jnp.zeros((B, LON), jnp.float32)
@@ -321,8 +333,17 @@
         for t in range(7, 0, -1):
             for s in range(t):
                 c[s] = c[s] - ratio[t, s] * c[t]
-        for k in range(g + 3, groups):
+        panel = 8 * g // B
+        for k in range(g + 3, min((panel + 2) * B // 8, groups)):
             work[k] = jnp.where(block, 0.0, work[k]) - weigh(columns(k, g), c)
+        if (8 * g + 8) % B == 0 and (panel + 2) * B < ALL:
+            top = jnp.concatenate(uppers[-B // 8:], axis=0)
+            wide = lax.broadcasted_iota(jnp.int32, (B, ALL), 1) < (panel + 1) * B
+            rest = jnp.where(wide, jnp.concatenate(inverses[-B // 8:], axis=0), top)
+            change = lax.dot_general(top, rest, TN, precision=HIGH, preferred_element_type=jnp.float32)
+            block = (lane >= panel * B) & (lane < (panel + 1) * B)
+            for k in range((panel + 2) * B // 8, groups):
+                work[k] = jnp.where(block, 0.0, work[k]) - change[8 * k:8 * k + 8]
     return jnp.concatenate(inverses, axis=0), jnp.concatenate(uppers, axis=0)
 
 
@@ -340,13 +361,8 @@
 def whole_row(i, s_ref, west_ref, east_ref):
     lane = lanes_of(ALL - B)
     row = s_ref[i, B:, :]
-    start = SPAN * (i + RIM) + RIM
     for ref, target in ((west_ref, 0), (east_ref, LON - RIM)):
-        k = start // LON
-        side = ref[:, k * LON:(k + 1) * LON]
-        if (start + RIM - 1) // LON > k:
-            side = jnp.where(lane < start - k * LON, ref[:, (k + 1) * LON:(k + 2) * LON], side)
-        side = pltpu.roll(side, (target - start) % LON, 1)
+        side = pltpu.roll(ref[...], (target - RIM * (i + RIM)) % LON, 1)
         row = jnp.where((lane >= target) & (lane < target + RIM), side, row)
     return jnp.concatenate([s_ref[i, :B, :], row], axis=0)
 
@@ -414,13 +430,10 @@
     )(x, sea_mask, depth_levels)
     far = lax.ppermute(far, ROW, [(i, ((i + 1) ^ 1) - 1) for i in range(1, 7)])
     near = lax.ppermute(near, ROW, [(i, i ^ 1) for i in range(8)])
-    flat = (B + 8, FLAT)
-    core, part_west, part_east = call(
-        core_rows, ((LAT, B + 8, LON), flat, flat), flops=1 << 22, moved=1 << 20
-    )(x, h)
-    far, near, north, south, own_west, own_east = call(side_columns, (flat, flat, edge, edge, flat, flat))(
-        far, near, part_west, part_east
-    )
+    flat = (B + 8, LON)
+    packs = (len(STARTS), B + 8, LON)
+    core, part = call(core_rows, ((LAT, B + 8, LON), packs), flops=1 << 22, moved=1 << 20)(x, h)
+    far, near, north, south, packed = call(side_columns, (flat, flat, edge, edge, packs))(far, near, part)
     far = lax.ppermute(far, COL, [(i, (((i + 1) ^ 1) - 1) % 32) for i in range(32)])
     near = lax.ppermute(near, COL, [(i, i ^ 1) for i in range(32)])
     wide = pltpu.VMEM((ROWS, B, LON), jnp.float32)
@@ -429,8 +442,8 @@
     s, own = call(
         inside, ((LAT, ALL, LON), square), [wide, wide, thin, thin, thin], flops=1 << 28, moved=1 << 23
     )(core, north, south)
-    rim = (ALL - B, FLAT)
-    gram, west, east = call(border, ((B, LON), rim, rim))(far, near, own_west, own_east, own)
+    rim = (ALL - B, LON)
+    gram, west, east = call(border, ((B, LON), rim, rim))(far, near, packed, own)
     other = lax.ppermute(gram, ROW, [(i, i ^ 1) for i in range(8)])
     copies = call(join, ((16, B, LON),))(gram, other)[0]
     parts = lax.all_to_all(copies, ("x", "y"), 0, 0)

time: 54.6 us -> 52.7 us (0.965)
  Pallas kernels: 11.9 us -> 10.8 us
    pallas_call x1, Pallas kernels: 6.34 us -> 5.06 us  [body(): call(basis, results, [pltpu.VMEM(shape, jnp.float32) for shape in results...]
  transfers between devices with their start and end apart: 5 -> 5, of which waited for: 3 -> 2; matrix products, arithmetic and copies ran while one was open for 0% -> 0% of each run, Pallas kernels for 6% -> 7%
where the time goes in v8:
time: 52.7 us; the launch traced here: 52.4 us
  blocking collectives  27.1 us (51%)
  starting transfers between devices  12.9 us (24%)
  Pallas kernels  10.8 us (20%)
  waiting for transfers between devices  0.96 us (2%)
  between operations  0.71 us (1%)
    all_to_all x1, blocking collectives, body(): parts = lax.all_to_all(copies, ('x', 'y'), 0, 0)  13.9 us
    all_to_all x1, blocking collectives, body(): parts = lax.all_to_all(copies, 'z', 0, 0)  13.2 us
    ppermute x1, starting transfers between devices, body(): near = lax.ppermute(near, COL, [(i, i ^ 1) for i in range(32)])  7.18 us
    pallas_call x1, Pallas kernels, body(): call(basis, results, [pltpu.VMEM(shape, jnp.float32) for shape in results...  5.06 us
    ppermute x1, starting transfers between devices, body(): near = lax.ppermute(near, ROW, [(i, i ^ 1) for i in range(8)])  2.94 us
    pallas_call x1, Pallas kernels, body(): call(inside, ((LAT, ALL, LON), square), [wide, wide, thin, thin, thin], f...  2.71 us
    ppermute x1, starting transfers between devices, body(): lax.ppermute(far, COL, [(i, ((i + 1 ^ 1) - 1) % 32) for i in range(32)])  1.66 us
    pallas_call x1, Pallas kernels, body(): call(edge_rows, (edge, edge, (B * LAT, LON), (LAT, LON)), [small, small,...  1.14 us
  transfers between devices with their start and end apart: 5, of which 2 were waited for; matrix products, arithmetic and copies ran while one was open for 0% of the time, Pallas kernels for 7%

profile of v8, /device:TPU:8, one launch (start us, length us, event | category | flops | bytes accessed | tf_op | source)
XLA Modules:
  0.0 52.4 jit_solution(10738207657683997034)
XLA Ops:
  0.6 1.1 %shard_map.58 = (f32[3,40,128]{2,1,0:T(8,128)S(1)}, f32[3,40,128]{2,1,0:T(8,128)S(1)}, f32[1024,128]{1,0:T(8,128)S(1)}, f32[32,128]{1,0:T(8,128)S(1)}) custom-call(f32[1024,128]{1,0:T(8,128)} %bitcast.1, s32[32,128]{1,0:T(8,128)} %mask_hbm.1, s32[32,128]{1,0:T(8,128)} %depth_hbm.1), custom_call_target="tpu_custom_call" | custom-call | tf_op jit(solution)/shard_map/pallas_call | solution.py:425
  1.8 0.7 %collective-permute-start = (f32[3,40,128]{2,1,0:T(8,128)S(1)}, f32[3,40,128]{2,1,0:T(8,128)S(1)}, u32[]{:S(2)}, u32[]{:S(2)}) collective-permute-start(f32[3,40,128]{2,1,0:T(8,128)S(1)} %get-tuple-element.19), channel_id=1, source_target_pairs={{32,64},{64,32},{96,128},{128,96},{160,192},{192,160},{33,65},{65,... | collective-permute-start | bytes 184328 | tf_op jit(solution)/shard_map/ppermute | solution.py:431
  2.4 2.9 %collective-permute-start.1 = (f32[3,40,128]{2,1,0:T(8,128)S(1)}, f32[3,40,128]{2,1,0:T(8,128)S(1)}, u32[]{:S(2)}, u32[]{:S(2)}) collective-permute-start(f32[3,40,128]{2,1,0:T(8,128)S(1)} %get-tuple-element.20), channel_id=1, source_target_pairs={{0,32},{32,0},{64,96},{96,64},{128,160},{160,128},{192,224},{224,1... | collective-permute-start | bytes 184328 | tf_op jit(solution)/shard_map/ppermute | solution.py:432
  5.4 0.8 %shard_map.59 = (f32[32,40,128]{2,1,0:T(8,128)S(1)}, f32[4,40,128]{2,1,0:T(8,128)S(1)}) custom-call(f32[1024,128]{1,0:T(8,128)S(1)} %get-tuple-element.21.x_ref, f32[32,128]{1,0:T(8,128)S(1)} %get-tuple-element.22.h_ref), custom_call_target="tpu_custom_call" | custom-call | flops 4194304 | bytes 1048576 | tf_op jit(solution)/shard_map/pallas_call | solution.py:435
  6.2 0.0 collective-permute-done.far_ref
  6.2 0.1 collective-permute-done.1.near_ref
  6.3 0.2 shard_map.60
  6.5 1.7 %collective-permute-start.2 = (f32[40,128]{1,0:T(8,128)S(1)}, f32[40,128]{1,0:T(8,128)S(1)}, u32[]{:S(2)}, u32[]{:S(2)}) collective-permute-start(f32[40,128]{1,0:T(8,128)S(1)} %get-tuple-element.24), channel_id=1, source_target_pairs={{0,31},{1,2},{2,1},{3,4},{4,3},{5,6},{6,5},{7,8},{8,7},{9,10},{10,... | collective-permute-start | bytes 61448 | tf_op jit(solution)/shard_map/ppermute | solution.py:437
  8.1 7.2 %collective-permute-start.3 = (f32[40,128]{1,0:T(8,128)S(1)}, f32[40,128]{1,0:T(8,128)S(1)}, u32[]{:S(2)}, u32[]{:S(2)}) collective-permute-start(f32[40,128]{1,0:T(8,128)S(1)} %get-tuple-element.25), channel_id=1, source_target_pairs={{0,1},{1,0},{2,3},{3,2},{4,5},{5,4},{6,7},{7,6},{8,9},{9,8},{10,11... | collective-permute-start | bytes 61448 | tf_op jit(solution)/shard_map/ppermute | solution.py:438
  15.3 2.7 %shard_map.61 = (f32[32,128,128]{2,1,0:T(8,128)S(1)}, f32[128,128]{1,0:T(8,128)S(1)}) custom-call(f32[32,40,128]{2,1,0:T(8,128)S(1)} %get-tuple-element.27.core_ref, f32[3,40,128]{2,1,0:T(8,128)S(1)} %get-tuple-element.28.north_ref, f32[3,40,128]{2,1,0:T(8,128)S(1)} %get-tuple-element.29.south_ref), custom_call_target="tpu_custom_call" | custom-call | flops 268435456 | bytes 8388608 | tf_op jit(solution)/shard_map/pallas_call | solution.py:442
  18.0 0.0 collective-permute-done.2.far_ref
  18.0 0.0 collective-permute-done.3.near_ref
  18.1 0.8 %shard_map.62 = (f32[32,128]{1,0:T(8,128)S(1)}, f32[96,128]{1,0:T(8,128)S(1)}, f32[96,128]{1,0:T(8,128)S(1)}) custom-call(f32[40,128]{1,0:T(8,128)S(1)} %collective-permute-done.2.far_ref, f32[40,128]{1,0:T(8,128)S(1)} %collective-permute-done.3.near_ref, f32[4,40,128]{2,1,0:T(8,128)S(1)} %get-tuple-element.26.packed_ref, ...), custom_call_target="tpu_custom_call" | custom-call | tf_op jit(solution)/shard_map/pallas_call | solution.py:446
  18.9 0.4 collective-permute-start.4
  19.3 0.8 %collective-permute-done.4.other_ref = f32[32,128]{1,0:T(8,128)S(1)} collective-permute-done((f32[32,128]{1,0:T(8,128)S(1)}, f32[32,128]{1,0:T(8,128)S(1)}, u32[]{:S(2)}, u32[]{:S(2)}) %collective-permute-start.4) | collective-permute-done | bytes 16416 | tf_op jit(solution)/shard_map/ppermute | solution.py:447
  20.2 13.9 %all_to_all.10.parts_ref = f32[16,32,128]{2,1,0:T(8,128)S(1)} all-to-all(f32[16,32,128]{2,1,0:T(8,128)S(1)} %shard_map.63), channel_id=1, replica_groups=mesh['x'=4,'core'=2,'z'=8,'y'=4] {'x','y'}, dimensions={0} | all-to-all | bytes 524288 | tf_op jit(solution)/shard_map/all_to_all | solution.py:449
  34.2 13.2 %all_to_all.11.parts_ref = f32[8,32,128]{2,1,0:T(8,128)S(1)} all-to-all(f32[8,32,128]{2,1,0:T(8,128)S(1)} %shard_map.64), channel_id=1, replica_groups=mesh['x'=4,'core'=2,'z'=8,'y'=4] {'z'}, dimensions={0} | all-to-all | bytes 262144 | tf_op jit(solution)/shard_map/all_to_all | solution.py:451
  47.4 5.1 %shard_map.65 = (f32[128,32,128]{2,1,0:T(8,128)}, f32[3,32,32]{2,1,0:T(8,128)}, f32[3,32,32]{2,1,0:T(8,128)}) custom-call(f32[8,32,128]{2,1,0:T(8,128)S(1)} %all_to_all.11.parts_ref, f32[32,128,128]{2,1,0:T(8,128)S(1)} %get-tuple-element.32.s_ref, f32[96,128]{1,0:T(8,128)S(1)} %get-tuple-element.33.west_ref, f32[96,128]{1,0:T(8,128)S(1)} %get-tuple-element.34.east_ref), custom_call_target="tpu_custom_call" | custom-call | tf_op jit(solution)/shard_map/pallas_call | solution.py:454
  (2 shorter events, 0.0 us)
Async XLA Ops:
  1.8 4.4 %collective-permute-start = (f32[3,40,128]{2,1,0:T(8,128)S(1)}, f32[3,40,128]{2,1,0:T(8,128)S(1)}, u32[]{:S(2)}, u32[]{:S(2)}) collective-permute-start(f32[3,40,128]{2,1,0:T(8,128)S(1)} %get-tuple-element.19), channel_id=1, source_target_pairs={{32,64},{64,32},{96,128},{128,96},{160,192},{192,160},{33,65},{65,... | collective-permute-start | bytes 184328 | tf_op jit(solution)/shard_map/ppermute | solution.py:431
  2.4 3.8 %collective-permute-start.1 = (f32[3,40,128]{2,1,0:T(8,128)S(1)}, f32[3,40,128]{2,1,0:T(8,128)S(1)}, u32[]{:S(2)}, u32[]{:S(2)}) collective-permute-start(f32[3,40,128]{2,1,0:T(8,128)S(1)} %get-tuple-element.20), channel_id=1, source_target_pairs={{0,32},{32,0},{64,96},{96,64},{128,160},{160,128},{192,224},{224,1... | collective-permute-start | bytes 184328 | tf_op jit(solution)/shard_map/ppermute | solution.py:432
  6.5 11.6 %collective-permute-start.2 = (f32[40,128]{1,0:T(8,128)S(1)}, f32[40,128]{1,0:T(8,128)S(1)}, u32[]{:S(2)}, u32[]{:S(2)}) collective-permute-start(f32[40,128]{1,0:T(8,128)S(1)} %get-tuple-element.24), channel_id=1, source_target_pairs={{0,31},{1,2},{2,1},{3,4},{4,3},{5,6},{6,5},{7,8},{8,7},{9,10},{10,... | collective-permute-start | bytes 61448 | tf_op jit(solution)/shard_map/ppermute | solution.py:437
  8.1 9.9 %collective-permute-start.3 = (f32[40,128]{1,0:T(8,128)S(1)}, f32[40,128]{1,0:T(8,128)S(1)}, u32[]{:S(2)}, u32[]{:S(2)}) collective-permute-start(f32[40,128]{1,0:T(8,128)S(1)} %get-tuple-element.25), channel_id=1, source_target_pairs={{0,1},{1,0},{2,3},{3,2},{4,5},{5,4},{6,7},{7,6},{8,9},{9,8},{10,11... | collective-permute-start | bytes 61448 | tf_op jit(solution)/shard_map/ppermute | solution.py:438
  18.9 1.3 %collective-permute-start.4 = (f32[32,128]{1,0:T(8,128)S(1)}, f32[32,128]{1,0:T(8,128)S(1)}, u32[]{:S(2)}, u32[]{:S(2)}) collective-permute-start(f32[32,128]{1,0:T(8,128)S(1)} %get-tuple-element.31.own_ref), channel_id=1, source_target_pairs={{0,32},{32,0},{64,96},{96,64},{128,160},{160,128},{192,224},{224,1... | collective-permute-start | bytes 49160 | tf_op jit(solution)/shard_map/ppermute | solution.py:447

commit v9 on v8

--- a/solution.py
+++ b/solution.py
@@ -302,11 +302,12 @@
                 unit = full(guess[:, 8 * g + t:8 * g + t + 1])
                 near, cross = pivot[t] * unit, line(own[t], t + 1)
                 recip[t + 1] = near * reciprocal(near * line(own[t + 1], t + 1) - cross * (cross * unit))
-            column = jnp.where(sub > t, own[t] * recip[t], 0.0)
+            column = own[t] * recip[t]
             for s in range(t + 1, 8):
                 ratio[s, t] = line(column, s)
                 own[s] = own[s] - column * line(own[t], s)
             if t < 7:
+                column = jnp.where(sub > t, column, 0.0)
                 a = a - column * line(a, t)
                 b = b - column * line(b, t)
                 for ahead in (after, later):
@@ -324,7 +325,10 @@
         c = jnp.where(lane < 8 * g + 8, b, a) * inverted
         c = [line(c, t) for t in range(8)]
         scaled = [after[t] * recip[t] for t in range(8)]
-        own = [coming[u] - weigh(after, [line(scaled[t], u) for t in range(8)]) for u in range(8)]
+        own = []
+        for u in range(8):
+            p = [after[t] * line(scaled[t], u) for t in range(8)]
+            own.append((coming[u] - (((p[0] + p[1]) + (p[2] + p[3])) + (p[4] + p[5]))) - (p[6] + p[7]))
         block = (lane >= 8 * g) & (lane < 8 * g + 8)
         for k, ahead in ((g + 1, after), (g + 2, later)):
             if ahead:

time: 52.7 us -> 52.7 us (level)
  no operation moved by 1% of the time
where the time goes in v9:
time: 52.7 us; the launch traced here: 52.4 us
  blocking collectives  27.1 us (51%)
  starting transfers between devices  12.9 us (24%)
  Pallas kernels  10.7 us (20%)
  waiting for transfers between devices  0.96 us (2%)
  between operations  0.71 us (1%)
    all_to_all x1, blocking collectives, body(): parts = lax.all_to_all(copies, ('x', 'y'), 0, 0)  13.9 us
    all_to_all x1, blocking collectives, body(): parts = lax.all_to_all(copies, 'z', 0, 0)  13.2 us
    ppermute x1, starting transfers between devices, body(): near = lax.ppermute(near, COL, [(i, i ^ 1) for i in range(32)])  7.18 us
    pallas_call x1, Pallas kernels, body(): call(basis, results, [pltpu.VMEM(shape, jnp.float32) for shape in results...  5.04 us
    ppermute x1, starting transfers between devices, body(): near = lax.ppermute(near, ROW, [(i, i ^ 1) for i in range(8)])  2.94 us
    pallas_call x1, Pallas kernels, body(): call(inside, ((LAT, ALL, LON), square), [wide, wide, thin, thin, thin], f...  2.71 us
    ppermute x1, starting transfers between devices, body(): lax.ppermute(far, COL, [(i, ((i + 1 ^ 1) - 1) % 32) for i in range(32)])  1.66 us
    pallas_call x1, Pallas kernels, body(): call(edge_rows, (edge, edge, (B * LAT, LON), (LAT, LON)), [small, small,...  1.14 us
  transfers between devices with their start and end apart: 5, of which 2 were waited for; matrix products, arithmetic and copies ran while one was open for 0% of the time, Pallas kernels for 7%

profile of v9, /device:TPU:8, one launch (start us, length us, event | category | flops | bytes accessed | tf_op | source)
XLA Modules:
  0.0 52.4 jit_solution(18112826797769571556)
XLA Ops:
  0.6 1.1 %shard_map.58 = (f32[3,40,128]{2,1,0:T(8,128)S(1)}, f32[3,40,128]{2,1,0:T(8,128)S(1)}, f32[1024,128]{1,0:T(8,128)S(1)}, f32[32,128]{1,0:T(8,128)S(1)}) custom-call(f32[1024,128]{1,0:T(8,128)} %bitcast.1, s32[32,128]{1,0:T(8,128)} %mask_hbm.1, s32[32,128]{1,0:T(8,128)} %depth_hbm.1), custom_call_target="tpu_custom_call" | custom-call | tf_op jit(solution)/shard_map/pallas_call | solution.py:429
  1.8 0.7 %collective-permute-start = (f32[3,40,128]{2,1,0:T(8,128)S(1)}, f32[3,40,128]{2,1,0:T(8,128)S(1)}, u32[]{:S(2)}, u32[]{:S(2)}) collective-permute-start(f32[3,40,128]{2,1,0:T(8,128)S(1)} %get-tuple-element.19), channel_id=1, source_target_pairs={{32,64},{64,32},{96,128},{128,96},{160,192},{192,160},{33,65},{65,... | collective-permute-start | bytes 184328 | tf_op jit(solution)/shard_map/ppermute | solution.py:435
  2.4 2.9 %collective-permute-start.1 = (f32[3,40,128]{2,1,0:T(8,128)S(1)}, f32[3,40,128]{2,1,0:T(8,128)S(1)}, u32[]{:S(2)}, u32[]{:S(2)}) collective-permute-start(f32[3,40,128]{2,1,0:T(8,128)S(1)} %get-tuple-element.20), channel_id=1, source_target_pairs={{0,32},{32,0},{64,96},{96,64},{128,160},{160,128},{192,224},{224,1... | collective-permute-start | bytes 184328 | tf_op jit(solution)/shard_map/ppermute | solution.py:436
  5.4 0.8 %shard_map.59 = (f32[32,40,128]{2,1,0:T(8,128)S(1)}, f32[4,40,128]{2,1,0:T(8,128)S(1)}) custom-call(f32[1024,128]{1,0:T(8,128)S(1)} %get-tuple-element.21.x_ref, f32[32,128]{1,0:T(8,128)S(1)} %get-tuple-element.22.h_ref), custom_call_target="tpu_custom_call" | custom-call | flops 4194304 | bytes 1048576 | tf_op jit(solution)/shard_map/pallas_call | solution.py:439
  6.2 0.0 collective-permute-done.far_ref
  6.2 0.1 collective-permute-done.1.near_ref
  6.3 0.2 shard_map.60
  6.5 1.7 %collective-permute-start.2 = (f32[40,128]{1,0:T(8,128)S(1)}, f32[40,128]{1,0:T(8,128)S(1)}, u32[]{:S(2)}, u32[]{:S(2)}) collective-permute-start(f32[40,128]{1,0:T(8,128)S(1)} %get-tuple-element.24), channel_id=1, source_target_pairs={{0,31},{1,2},{2,1},{3,4},{4,3},{5,6},{6,5},{7,8},{8,7},{9,10},{10,... | collective-permute-start | bytes 61448 | tf_op jit(solution)/shard_map/ppermute | solution.py:441
  8.1 7.2 %collective-permute-start.3 = (f32[40,128]{1,0:T(8,128)S(1)}, f32[40,128]{1,0:T(8,128)S(1)}, u32[]{:S(2)}, u32[]{:S(2)}) collective-permute-start(f32[40,128]{1,0:T(8,128)S(1)} %get-tuple-element.25), channel_id=1, source_target_pairs={{0,1},{1,0},{2,3},{3,2},{4,5},{5,4},{6,7},{7,6},{8,9},{9,8},{10,11... | collective-permute-start | bytes 61448 | tf_op jit(solution)/shard_map/ppermute | solution.py:442
  15.3 2.7 %shard_map.61 = (f32[32,128,128]{2,1,0:T(8,128)S(1)}, f32[128,128]{1,0:T(8,128)S(1)}) custom-call(f32[32,40,128]{2,1,0:T(8,128)S(1)} %get-tuple-element.27.core_ref, f32[3,40,128]{2,1,0:T(8,128)S(1)} %get-tuple-element.28.north_ref, f32[3,40,128]{2,1,0:T(8,128)S(1)} %get-tuple-element.29.south_ref), custom_call_target="tpu_custom_call" | custom-call | flops 268435456 | bytes 8388608 | tf_op jit(solution)/shard_map/pallas_call | solution.py:446
  18.0 0.0 collective-permute-done.2.far_ref
  18.0 0.0 collective-permute-done.3.near_ref
  18.1 0.8 %shard_map.62 = (f32[32,128]{1,0:T(8,128)S(1)}, f32[96,128]{1,0:T(8,128)S(1)}, f32[96,128]{1,0:T(8,128)S(1)}) custom-call(f32[40,128]{1,0:T(8,128)S(1)} %collective-permute-done.2.far_ref, f32[40,128]{1,0:T(8,128)S(1)} %collective-permute-done.3.near_ref, f32[4,40,128]{2,1,0:T(8,128)S(1)} %get-tuple-element.26.packed_ref, ...), custom_call_target="tpu_custom_call" | custom-call | tf_op jit(solution)/shard_map/pallas_call | solution.py:450
  18.9 0.4 collective-permute-start.4
  19.3 0.8 %collective-permute-done.4.other_ref = f32[32,128]{1,0:T(8,128)S(1)} collective-permute-done((f32[32,128]{1,0:T(8,128)S(1)}, f32[32,128]{1,0:T(8,128)S(1)}, u32[]{:S(2)}, u32[]{:S(2)}) %collective-permute-start.4) | collective-permute-done | bytes 16416 | tf_op jit(solution)/shard_map/ppermute | solution.py:451
  20.2 13.9 %all_to_all.10.parts_ref = f32[16,32,128]{2,1,0:T(8,128)S(1)} all-to-all(f32[16,32,128]{2,1,0:T(8,128)S(1)} %shard_map.63), channel_id=1, replica_groups=mesh['x'=4,'core'=2,'z'=8,'y'=4] {'x','y'}, dimensions={0} | all-to-all | bytes 524288 | tf_op jit(solution)/shard_map/all_to_all | solution.py:453
  34.2 13.2 %all_to_all.11.parts_ref = f32[8,32,128]{2,1,0:T(8,128)S(1)} all-to-all(f32[8,32,128]{2,1,0:T(8,128)S(1)} %shard_map.64), channel_id=1, replica_groups=mesh['x'=4,'core'=2,'z'=8,'y'=4] {'z'}, dimensions={0} | all-to-all | bytes 262144 | tf_op jit(solution)/shard_map/all_to_all | solution.py:455
  47.4 5.0 %shard_map.65 = (f32[128,32,128]{2,1,0:T(8,128)}, f32[3,32,32]{2,1,0:T(8,128)}, f32[3,32,32]{2,1,0:T(8,128)}) custom-call(f32[8,32,128]{2,1,0:T(8,128)S(1)} %all_to_all.11.parts_ref, f32[32,128,128]{2,1,0:T(8,128)S(1)} %get-tuple-element.32.s_ref, f32[96,128]{1,0:T(8,128)S(1)} %get-tuple-element.33.west_ref, f32[96,128]{1,0:T(8,128)S(1)} %get-tuple-element.34.east_ref), custom_call_target="tpu_custom_call" | custom-call | tf_op jit(solution)/shard_map/pallas_call | solution.py:458
  (2 shorter events, 0.0 us)
Async XLA Ops:
  1.8 4.4 %collective-permute-start = (f32[3,40,128]{2,1,0:T(8,128)S(1)}, f32[3,40,128]{2,1,0:T(8,128)S(1)}, u32[]{:S(2)}, u32[]{:S(2)}) collective-permute-start(f32[3,40,128]{2,1,0:T(8,128)S(1)} %get-tuple-element.19), channel_id=1, source_target_pairs={{32,64},{64,32},{96,128},{128,96},{160,192},{192,160},{33,65},{65,... | collective-permute-start | bytes 184328 | tf_op jit(solution)/shard_map/ppermute | solution.py:435
  2.4 3.8 %collective-permute-start.1 = (f32[3,40,128]{2,1,0:T(8,128)S(1)}, f32[3,40,128]{2,1,0:T(8,128)S(1)}, u32[]{:S(2)}, u32[]{:S(2)}) collective-permute-start(f32[3,40,128]{2,1,0:T(8,128)S(1)} %get-tuple-element.20), channel_id=1, source_target_pairs={{0,32},{32,0},{64,96},{96,64},{128,160},{160,128},{192,224},{224,1... | collective-permute-start | bytes 184328 | tf_op jit(solution)/shard_map/ppermute | solution.py:436
  6.5 11.6 %collective-permute-start.2 = (f32[40,128]{1,0:T(8,128)S(1)}, f32[40,128]{1,0:T(8,128)S(1)}, u32[]{:S(2)}, u32[]{:S(2)}) collective-permute-start(f32[40,128]{1,0:T(8,128)S(1)} %get-tuple-element.24), channel_id=1, source_target_pairs={{0,31},{1,2},{2,1},{3,4},{4,3},{5,6},{6,5},{7,8},{8,7},{9,10},{10,... | collective-permute-start | bytes 61448 | tf_op jit(solution)/shard_map/ppermute | solution.py:441
  8.1 9.9 %collective-permute-start.3 = (f32[40,128]{1,0:T(8,128)S(1)}, f32[40,128]{1,0:T(8,128)S(1)}, u32[]{:S(2)}, u32[]{:S(2)}) collective-permute-start(f32[40,128]{1,0:T(8,128)S(1)} %get-tuple-element.25), channel_id=1, source_target_pairs={{0,1},{1,0},{2,3},{3,2},{4,5},{5,4},{6,7},{7,6},{8,9},{9,8},{10,11... | collective-permute-start | bytes 61448 | tf_op jit(solution)/shard_map/ppermute | solution.py:442
  18.9 1.3 %collective-permute-start.4 = (f32[32,128]{1,0:T(8,128)S(1)}, f32[32,128]{1,0:T(8,128)S(1)}, u32[]{:S(2)}, u32[]{:S(2)}) collective-permute-start(f32[32,128]{1,0:T(8,128)S(1)} %get-tuple-element.31.own_ref), channel_id=1, source_target_pairs={{0,32},{32,0},{64,96},{96,64},{128,160},{160,128},{192,224},{224,1... | collective-permute-start | bytes 49160 | tf_op jit(solution)/shard_map/ppermute | solution.py:451

commit v10 on v8

--- a/solution.py
+++ b/solution.py
@@ -191,9 +191,9 @@
         south = [KAPPA * jnp.minimum(h[i], move(h[i], -RIM)) for i in range(3)]
         right = [KAPPA * jnp.minimum(h[i], rightward(h, i)) for i in range(3)]
         right[2] = jnp.where(last[:8], 0.0, right[2])
-        left = [leftward(right, i) for i in range(3)]
+        left = [KAPPA * jnp.minimum(h[i], leftward(h, i)) for i in range(3)]
         left[0] = jnp.where(first[:8], 0.0, left[0])
-        north = [four(move(value, RIM)) for value in south]
+        north = [four(KAPPA * jnp.minimum(value, move(value, RIM))) for value in h]
         south, right, left = [[four(value) for value in values] for values in (south, right, left)]
         centre = [four(jnp.where(value > 0.0, 0.0, -1.0)) for value in h]
         v = [part[:B] for part in chain]
@@ -223,11 +223,11 @@
         after = pltpu.roll(own, LON - B, 1)
         here = (lane >= k * B) & (lane < (k + 1) * B)
         packed = jnp.where(here, jnp.where(lane - k * B >= row, own, after), packed)
-        diagonal = jnp.where(here & (lane - k * B == row), after, diagonal)
+        diagonal = jnp.where(lane - (k + 1) * B == row, own, diagonal)
     line = jnp.sum(diagonal, axis=0, keepdims=True)
     for n, (k, part) in enumerate(HALVES):
         there = (row == B - 1 - n) & (lane >= ITERS * B) & (lane < ITERS * B + HALF)
-        packed = jnp.where(there, pltpu.roll(line, (ITERS * B - k * B - part * HALF) % LON, 1), packed)
+        packed = jnp.where(there, pltpu.roll(line, (ITERS * B - (k + 1) * B - part * HALF) % LON, 1), packed)
     gram_ref[...] = packed
 
 

time: 52.7 us -> 52.6 us (level)
  no operation moved by 1% of the time
where the time goes in v10:
time: 52.6 us; the launch traced here: 52.3 us
  blocking collectives  27.1 us (52%)
  starting transfers between devices  12.9 us (25%)
  Pallas kernels  10.7 us (20%)
  waiting for transfers between devices  0.96 us (2%)
  between operations  0.71 us (1%)
    all_to_all x1, blocking collectives, body(): parts = lax.all_to_all(copies, ('x', 'y'), 0, 0)  13.9 us
    all_to_all x1, blocking collectives, body(): parts = lax.all_to_all(copies, 'z', 0, 0)  13.2 us
    ppermute x1, starting transfers between devices, body(): near = lax.ppermute(near, COL, [(i, i ^ 1) for i in range(32)])  7.18 us
    pallas_call x1, Pallas kernels, body(): call(basis, results, [pltpu.VMEM(shape, jnp.float32) for shape in results...  5.06 us
    ppermute x1, starting transfers between devices, body(): near = lax.ppermute(near, ROW, [(i, i ^ 1) for i in range(8)])  2.94 us
    pallas_call x1, Pallas kernels, body(): call(inside, ((LAT, ALL, LON), square), [wide, wide, thin, thin, thin], f...  2.71 us
    ppermute x1, starting transfers between devices, body(): lax.ppermute(far, COL, [(i, ((i + 1 ^ 1) - 1) % 32) for i in range(32)])  1.66 us
    pallas_call x1, Pallas kernels, body(): call(edge_rows, (edge, edge, (B * LAT, LON), (LAT, LON)), [small, small,...  1.14 us
  transfers between devices with their start and end apart: 5, of which 2 were waited for; matrix products, arithmetic and copies ran while one was open for 0% of the time, Pallas kernels for 7%

profile of v10, /device:TPU:8, one launch (start us, length us, event | category | flops | bytes accessed | tf_op | source)
XLA Modules:
  0.0 52.3 jit_solution(2796658671526663998)
XLA Ops:
  0.6 1.1 %shard_map.58 = (f32[3,40,128]{2,1,0:T(8,128)S(1)}, f32[3,40,128]{2,1,0:T(8,128)S(1)}, f32[1024,128]{1,0:T(8,128)S(1)}, f32[32,128]{1,0:T(8,128)S(1)}) custom-call(f32[1024,128]{1,0:T(8,128)} %bitcast.1, s32[32,128]{1,0:T(8,128)} %mask_hbm.1, s32[32,128]{1,0:T(8,128)} %depth_hbm.1), custom_call_target="tpu_custom_call" | custom-call | tf_op jit(solution)/shard_map/pallas_call | solution.py:425
  1.8 0.7 %collective-permute-start = (f32[3,40,128]{2,1,0:T(8,128)S(1)}, f32[3,40,128]{2,1,0:T(8,128)S(1)}, u32[]{:S(2)}, u32[]{:S(2)}) collective-permute-start(f32[3,40,128]{2,1,0:T(8,128)S(1)} %get-tuple-element.19), channel_id=1, source_target_pairs={{32,64},{64,32},{96,128},{128,96},{160,192},{192,160},{33,65},{65,... | collective-permute-start | bytes 184328 | tf_op jit(solution)/shard_map/ppermute | solution.py:431
  2.4 2.9 %collective-permute-start.1 = (f32[3,40,128]{2,1,0:T(8,128)S(1)}, f32[3,40,128]{2,1,0:T(8,128)S(1)}, u32[]{:S(2)}, u32[]{:S(2)}) collective-permute-start(f32[3,40,128]{2,1,0:T(8,128)S(1)} %get-tuple-element.20), channel_id=1, source_target_pairs={{0,32},{32,0},{64,96},{96,64},{128,160},{160,128},{192,224},{224,1... | collective-permute-start | bytes 184328 | tf_op jit(solution)/shard_map/ppermute | solution.py:432
  5.4 0.8 %shard_map.59 = (f32[32,40,128]{2,1,0:T(8,128)S(1)}, f32[4,40,128]{2,1,0:T(8,128)S(1)}) custom-call(f32[1024,128]{1,0:T(8,128)S(1)} %get-tuple-element.21.x_ref, f32[32,128]{1,0:T(8,128)S(1)} %get-tuple-element.22.h_ref), custom_call_target="tpu_custom_call" | custom-call | flops 4194304 | bytes 1048576 | tf_op jit(solution)/shard_map/pallas_call | solution.py:435
  6.2 0.0 collective-permute-done.far_ref
  6.2 0.1 collective-permute-done.1.near_ref
  6.3 0.2 shard_map.60
  6.5 1.7 %collective-permute-start.2 = (f32[40,128]{1,0:T(8,128)S(1)}, f32[40,128]{1,0:T(8,128)S(1)}, u32[]{:S(2)}, u32[]{:S(2)}) collective-permute-start(f32[40,128]{1,0:T(8,128)S(1)} %get-tuple-element.24), channel_id=1, source_target_pairs={{0,31},{1,2},{2,1},{3,4},{4,3},{5,6},{6,5},{7,8},{8,7},{9,10},{10,... | collective-permute-start | bytes 61448 | tf_op jit(solution)/shard_map/ppermute | solution.py:437
  8.1 7.2 %collective-permute-start.3 = (f32[40,128]{1,0:T(8,128)S(1)}, f32[40,128]{1,0:T(8,128)S(1)}, u32[]{:S(2)}, u32[]{:S(2)}) collective-permute-start(f32[40,128]{1,0:T(8,128)S(1)} %get-tuple-element.25), channel_id=1, source_target_pairs={{0,1},{1,0},{2,3},{3,2},{4,5},{5,4},{6,7},{7,6},{8,9},{9,8},{10,11... | collective-permute-start | bytes 61448 | tf_op jit(solution)/shard_map/ppermute | solution.py:438
  15.3 2.7 %shard_map.61 = (f32[32,128,128]{2,1,0:T(8,128)S(1)}, f32[128,128]{1,0:T(8,128)S(1)}) custom-call(f32[32,40,128]{2,1,0:T(8,128)S(1)} %get-tuple-element.27.core_ref, f32[3,40,128]{2,1,0:T(8,128)S(1)} %get-tuple-element.28.north_ref, f32[3,40,128]{2,1,0:T(8,128)S(1)} %get-tuple-element.29.south_ref), custom_call_target="tpu_custom_call" | custom-call | flops 268435456 | bytes 8388608 | tf_op jit(solution)/shard_map/pallas_call | solution.py:442
  18.0 0.0 collective-permute-done.2.far_ref
  18.0 0.0 collective-permute-done.3.near_ref
  18.1 0.8 %shard_map.62 = (f32[32,128]{1,0:T(8,128)S(1)}, f32[96,128]{1,0:T(8,128)S(1)}, f32[96,128]{1,0:T(8,128)S(1)}) custom-call(f32[40,128]{1,0:T(8,128)S(1)} %collective-permute-done.2.far_ref, f32[40,128]{1,0:T(8,128)S(1)} %collective-permute-done.3.near_ref, f32[4,40,128]{2,1,0:T(8,128)S(1)} %get-tuple-element.26.packed_ref, ...), custom_call_target="tpu_custom_call" | custom-call | tf_op jit(solution)/shard_map/pallas_call | solution.py:446
  18.8 0.4 collective-permute-start.4
  19.3 0.8 %collective-permute-done.4.other_ref = f32[32,128]{1,0:T(8,128)S(1)} collective-permute-done((f32[32,128]{1,0:T(8,128)S(1)}, f32[32,128]{1,0:T(8,128)S(1)}, u32[]{:S(2)}, u32[]{:S(2)}) %collective-permute-start.4) | collective-permute-done | bytes 16416 | tf_op jit(solution)/shard_map/ppermute | solution.py:447
  20.1 13.9 %all_to_all.10.parts_ref = f32[16,32,128]{2,1,0:T(8,128)S(1)} all-to-all(f32[16,32,128]{2,1,0:T(8,128)S(1)} %shard_map.63), channel_id=1, replica_groups=mesh['x'=4,'core'=2,'z'=8,'y'=4] {'x','y'}, dimensions={0} | all-to-all | bytes 524288 | tf_op jit(solution)/shard_map/all_to_all | solution.py:449
  34.1 13.2 %all_to_all.11.parts_ref = f32[8,32,128]{2,1,0:T(8,128)S(1)} all-to-all(f32[8,32,128]{2,1,0:T(8,128)S(1)} %shard_map.64), channel_id=1, replica_groups=mesh['x'=4,'core'=2,'z'=8,'y'=4] {'z'}, dimensions={0} | all-to-all | bytes 262144 | tf_op jit(solution)/shard_map/all_to_all | solution.py:451
  47.3 5.1 %shard_map.65 = (f32[128,32,128]{2,1,0:T(8,128)}, f32[3,32,32]{2,1,0:T(8,128)}, f32[3,32,32]{2,1,0:T(8,128)}) custom-call(f32[8,32,128]{2,1,0:T(8,128)S(1)} %all_to_all.11.parts_ref, f32[32,128,128]{2,1,0:T(8,128)S(1)} %get-tuple-element.32.s_ref, f32[96,128]{1,0:T(8,128)S(1)} %get-tuple-element.33.west_ref, f32[96,128]{1,0:T(8,128)S(1)} %get-tuple-element.34.east_ref), custom_call_target="tpu_custom_call" | custom-call | tf_op jit(solution)/shard_map/pallas_call | solution.py:454
  (2 shorter events, 0.0 us)
Async XLA Ops:
  1.8 4.4 %collective-permute-start = (f32[3,40,128]{2,1,0:T(8,128)S(1)}, f32[3,40,128]{2,1,0:T(8,128)S(1)}, u32[]{:S(2)}, u32[]{:S(2)}) collective-permute-start(f32[3,40,128]{2,1,0:T(8,128)S(1)} %get-tuple-element.19), channel_id=1, source_target_pairs={{32,64},{64,32},{96,128},{128,96},{160,192},{192,160},{33,65},{65,... | collective-permute-start | bytes 184328 | tf_op jit(solution)/shard_map/ppermute | solution.py:431
  2.4 3.8 %collective-permute-start.1 = (f32[3,40,128]{2,1,0:T(8,128)S(1)}, f32[3,40,128]{2,1,0:T(8,128)S(1)}, u32[]{:S(2)}, u32[]{:S(2)}) collective-permute-start(f32[3,40,128]{2,1,0:T(8,128)S(1)} %get-tuple-element.20), channel_id=1, source_target_pairs={{0,32},{32,0},{64,96},{96,64},{128,160},{160,128},{192,224},{224,1... | collective-permute-start | bytes 184328 | tf_op jit(solution)/shard_map/ppermute | solution.py:432
  6.5 11.6 %collective-permute-start.2 = (f32[40,128]{1,0:T(8,128)S(1)}, f32[40,128]{1,0:T(8,128)S(1)}, u32[]{:S(2)}, u32[]{:S(2)}) collective-permute-start(f32[40,128]{1,0:T(8,128)S(1)} %get-tuple-element.24), channel_id=1, source_target_pairs={{0,31},{1,2},{2,1},{3,4},{4,3},{5,6},{6,5},{7,8},{8,7},{9,10},{10,... | collective-permute-start | bytes 61448 | tf_op jit(solution)/shard_map/ppermute | solution.py:437
  8.1 9.9 %collective-permute-start.3 = (f32[40,128]{1,0:T(8,128)S(1)}, f32[40,128]{1,0:T(8,128)S(1)}, u32[]{:S(2)}, u32[]{:S(2)}) collective-permute-start(f32[40,128]{1,0:T(8,128)S(1)} %get-tuple-element.25), channel_id=1, source_target_pairs={{0,1},{1,0},{2,3},{3,2},{4,5},{5,4},{6,7},{7,6},{8,9},{9,8},{10,11... | collective-permute-start | bytes 61448 | tf_op jit(solution)/shard_map/ppermute | solution.py:438
  18.8 1.3 %collective-permute-start.4 = (f32[32,128]{1,0:T(8,128)S(1)}, f32[32,128]{1,0:T(8,128)S(1)}, u32[]{:S(2)}, u32[]{:S(2)}) collective-permute-start(f32[32,128]{1,0:T(8,128)S(1)} %get-tuple-element.31.own_ref), channel_id=1, source_target_pairs={{0,32},{32,0},{64,96},{96,64},{128,160},{160,128},{192,224},{224,1... | collective-permute-start | bytes 49160 | tf_op jit(solution)/shard_map/ppermute | solution.py:447

commit v11 on v10

--- a/solution.py
+++ b/solution.py
@@ -222,12 +222,12 @@
         own = gram[k * B:(k + 1) * B]
         after = pltpu.roll(own, LON - B, 1)
         here = (lane >= k * B) & (lane < (k + 1) * B)
-        packed = jnp.where(here, jnp.where(lane - k * B >= row, own, after), packed)
+        packed = jnp.where(here, jnp.where(lane - k * B <= row, own, after), packed)
         diagonal = jnp.where(lane - (k + 1) * B == row, own, diagonal)
     line = jnp.sum(diagonal, axis=0, keepdims=True)
     for n, (k, part) in enumerate(HALVES):
-        there = (row == B - 1 - n) & (lane >= ITERS * B) & (lane < ITERS * B + HALF)
-        packed = jnp.where(there, pltpu.roll(line, (ITERS * B - (k + 1) * B - part * HALF) % LON, 1), packed)
+        there = (row == n) & (lane >= ITERS * B + HALF)
+        packed = jnp.where(there, pltpu.roll(line, (ITERS * B + HALF - (k + 1) * B - part * HALF) % LON, 1), packed)
     gram_ref[...] = packed
 
 
@@ -251,12 +251,12 @@
     block, place = lane >> 5, lane & (B - 1)
     turned = jnp.concatenate([jnp.where(block == k, total, 0.0) for k in range(ITERS + 1)], axis=0).T
     mirror = (turned[:B] + turned[B:2 * B]) + (turned[2 * B:3 * B] + turned[3 * B:])
-    even = jnp.where(place >= row, total, mirror)
-    odd = jnp.where(place < row, total, mirror)
+    even = jnp.where(place <= row, total, mirror)
+    odd = jnp.where(place > row, total, mirror)
     line = jnp.zeros((1, LON), jnp.float32)
     for n, (k, part) in enumerate(HALVES):
         target = k * B + part * HALF
-        moved = pltpu.roll(total[B - 1 - n:B - n], (target - ITERS * B) % LON, 1)
+        moved = pltpu.roll(total[n:n + 1], (target - ITERS * B - HALF) % LON, 1)
         line = jnp.where((lane[:1] >= target) & (lane[:1] < target + HALF), moved, line)
     odd = jnp.where(place == row, line, odd)
     move = lambda field, k: pltpu.roll(field, (k * B) % LON, 1)
@@ -268,7 +268,7 @@
         pick(even_back, odd, even, odd_on),
         pick(odd_back, even_back, odd, even),
     ]
-    return even, jnp.concatenate(rows, axis=0)
+    return total, jnp.concatenate(rows, axis=0)
 
 
 def reciprocal(value):

time: 52.6 us -> 52.6 us (level)
  no operation moved by 1% of the time
where the time goes in v11:
time: 52.6 us; the launch traced here: 52.4 us
  blocking collectives  27.1 us (52%)
  starting transfers between devices  12.9 us (25%)
  Pallas kernels  10.7 us (20%)
  waiting for transfers between devices  0.96 us (2%)
  between operations  0.71 us (1%)
    all_to_all x1, blocking collectives, body(): parts = lax.all_to_all(copies, ('x', 'y'), 0, 0)  13.9 us
    all_to_all x1, blocking collectives, body(): parts = lax.all_to_all(copies, 'z', 0, 0)  13.2 us
    ppermute x1, starting transfers between devices, body(): near = lax.ppermute(near, COL, [(i, i ^ 1) for i in range(32)])  7.18 us
    pallas_call x1, Pallas kernels, body(): call(basis, results, [pltpu.VMEM(shape, jnp.float32) for shape in results...  5.07 us
    ppermute x1, starting transfers between devices, body(): near = lax.ppermute(near, ROW, [(i, i ^ 1) for i in range(8)])  2.94 us
    pallas_call x1, Pallas kernels, body(): call(inside, ((LAT, ALL, LON), square), [wide, wide, thin, thin, thin], f...  2.71 us
    ppermute x1, starting transfers between devices, body(): lax.ppermute(far, COL, [(i, ((i + 1 ^ 1) - 1) % 32) for i in range(32)])  1.66 us
    pallas_call x1, Pallas kernels, body(): call(edge_rows, (edge, edge, (B * LAT, LON), (LAT, LON)), [small, small,...  1.14 us
  transfers between devices with their start and end apart: 5, of which 2 were waited for; matrix products, arithmetic and copies ran while one was open for 0% of the time, Pallas kernels for 7%

profile of v11, /device:TPU:8, one launch (start us, length us, event | category | flops | bytes accessed | tf_op | source)
XLA Modules:
  0.0 52.4 jit_solution(15850480109197252034)
XLA Ops:
  0.6 1.1 %shard_map.58 = (f32[3,40,128]{2,1,0:T(8,128)S(1)}, f32[3,40,128]{2,1,0:T(8,128)S(1)}, f32[1024,128]{1,0:T(8,128)S(1)}, f32[32,128]{1,0:T(8,128)S(1)}) custom-call(f32[1024,128]{1,0:T(8,128)} %bitcast.1, s32[32,128]{1,0:T(8,128)} %mask_hbm.1, s32[32,128]{1,0:T(8,128)} %depth_hbm.1), custom_call_target="tpu_custom_call" | custom-call | tf_op jit(solution)/shard_map/pallas_call | solution.py:425
  1.8 0.7 %collective-permute-start = (f32[3,40,128]{2,1,0:T(8,128)S(1)}, f32[3,40,128]{2,1,0:T(8,128)S(1)}, u32[]{:S(2)}, u32[]{:S(2)}) collective-permute-start(f32[3,40,128]{2,1,0:T(8,128)S(1)} %get-tuple-element.19), channel_id=1, source_target_pairs={{32,64},{64,32},{96,128},{128,96},{160,192},{192,160},{33,65},{65,... | collective-permute-start | bytes 184328 | tf_op jit(solution)/shard_map/ppermute | solution.py:431
  2.4 2.9 %collective-permute-start.1 = (f32[3,40,128]{2,1,0:T(8,128)S(1)}, f32[3,40,128]{2,1,0:T(8,128)S(1)}, u32[]{:S(2)}, u32[]{:S(2)}) collective-permute-start(f32[3,40,128]{2,1,0:T(8,128)S(1)} %get-tuple-element.20), channel_id=1, source_target_pairs={{0,32},{32,0},{64,96},{96,64},{128,160},{160,128},{192,224},{224,1... | collective-permute-start | bytes 184328 | tf_op jit(solution)/shard_map/ppermute | solution.py:432
  5.4 0.8 %shard_map.59 = (f32[32,40,128]{2,1,0:T(8,128)S(1)}, f32[4,40,128]{2,1,0:T(8,128)S(1)}) custom-call(f32[1024,128]{1,0:T(8,128)S(1)} %get-tuple-element.21.x_ref, f32[32,128]{1,0:T(8,128)S(1)} %get-tuple-element.22.h_ref), custom_call_target="tpu_custom_call" | custom-call | flops 4194304 | bytes 1048576 | tf_op jit(solution)/shard_map/pallas_call | solution.py:435
  6.2 0.0 collective-permute-done.far_ref
  6.2 0.1 collective-permute-done.1.near_ref
  6.3 0.2 shard_map.60
  6.5 1.7 %collective-permute-start.2 = (f32[40,128]{1,0:T(8,128)S(1)}, f32[40,128]{1,0:T(8,128)S(1)}, u32[]{:S(2)}, u32[]{:S(2)}) collective-permute-start(f32[40,128]{1,0:T(8,128)S(1)} %get-tuple-element.24), channel_id=1, source_target_pairs={{0,31},{1,2},{2,1},{3,4},{4,3},{5,6},{6,5},{7,8},{8,7},{9,10},{10,... | collective-permute-start | bytes 61448 | tf_op jit(solution)/shard_map/ppermute | solution.py:437
  8.1 7.2 %collective-permute-start.3 = (f32[40,128]{1,0:T(8,128)S(1)}, f32[40,128]{1,0:T(8,128)S(1)}, u32[]{:S(2)}, u32[]{:S(2)}) collective-permute-start(f32[40,128]{1,0:T(8,128)S(1)} %get-tuple-element.25), channel_id=1, source_target_pairs={{0,1},{1,0},{2,3},{3,2},{4,5},{5,4},{6,7},{7,6},{8,9},{9,8},{10,11... | collective-permute-start | bytes 61448 | tf_op jit(solution)/shard_map/ppermute | solution.py:438
  15.3 2.7 %shard_map.61 = (f32[32,128,128]{2,1,0:T(8,128)S(1)}, f32[128,128]{1,0:T(8,128)S(1)}) custom-call(f32[32,40,128]{2,1,0:T(8,128)S(1)} %get-tuple-element.27.core_ref, f32[3,40,128]{2,1,0:T(8,128)S(1)} %get-tuple-element.28.north_ref, f32[3,40,128]{2,1,0:T(8,128)S(1)} %get-tuple-element.29.south_ref), custom_call_target="tpu_custom_call" | custom-call | flops 268435456 | bytes 8388608 | tf_op jit(solution)/shard_map/pallas_call | solution.py:442
  18.0 0.0 collective-permute-done.2.far_ref
  18.0 0.0 collective-permute-done.3.near_ref
  18.1 0.8 %shard_map.62 = (f32[32,128]{1,0:T(8,128)S(1)}, f32[96,128]{1,0:T(8,128)S(1)}, f32[96,128]{1,0:T(8,128)S(1)}) custom-call(f32[40,128]{1,0:T(8,128)S(1)} %collective-permute-done.2.far_ref, f32[40,128]{1,0:T(8,128)S(1)} %collective-permute-done.3.near_ref, f32[4,40,128]{2,1,0:T(8,128)S(1)} %get-tuple-element.26.packed_ref, ...), custom_call_target="tpu_custom_call" | custom-call | tf_op jit(solution)/shard_map/pallas_call | solution.py:446
  18.8 0.4 collective-permute-start.4
  19.3 0.8 %collective-permute-done.4.other_ref = f32[32,128]{1,0:T(8,128)S(1)} collective-permute-done((f32[32,128]{1,0:T(8,128)S(1)}, f32[32,128]{1,0:T(8,128)S(1)}, u32[]{:S(2)}, u32[]{:S(2)}) %collective-permute-start.4) | collective-permute-done | bytes 16416 | tf_op jit(solution)/shard_map/ppermute | solution.py:447
  20.1 13.9 %all_to_all.10.parts_ref = f32[16,32,128]{2,1,0:T(8,128)S(1)} all-to-all(f32[16,32,128]{2,1,0:T(8,128)S(1)} %shard_map.63), channel_id=1, replica_groups=mesh['x'=4,'core'=2,'z'=8,'y'=4] {'x','y'}, dimensions={0} | all-to-all | bytes 524288 | tf_op jit(solution)/shard_map/all_to_all | solution.py:449
  34.1 13.2 %all_to_all.11.parts_ref = f32[8,32,128]{2,1,0:T(8,128)S(1)} all-to-all(f32[8,32,128]{2,1,0:T(8,128)S(1)} %shard_map.64), channel_id=1, replica_groups=mesh['x'=4,'core'=2,'z'=8,'y'=4] {'z'}, dimensions={0} | all-to-all | bytes 262144 | tf_op jit(solution)/shard_map/all_to_all | solution.py:451
  47.3 5.1 %shard_map.65 = (f32[128,32,128]{2,1,0:T(8,128)}, f32[3,32,32]{2,1,0:T(8,128)}, f32[3,32,32]{2,1,0:T(8,128)}) custom-call(f32[8,32,128]{2,1,0:T(8,128)S(1)} %all_to_all.11.parts_ref, f32[32,128,128]{2,1,0:T(8,128)S(1)} %get-tuple-element.32.s_ref, f32[96,128]{1,0:T(8,128)S(1)} %get-tuple-element.33.west_ref, f32[96,128]{1,0:T(8,128)S(1)} %get-tuple-element.34.east_ref), custom_call_target="tpu_custom_call" | custom-call | tf_op jit(solution)/shard_map/pallas_call | solution.py:454
  (2 shorter events, 0.0 us)
Async XLA Ops:
  1.8 4.4 %collective-permute-start = (f32[3,40,128]{2,1,0:T(8,128)S(1)}, f32[3,40,128]{2,1,0:T(8,128)S(1)}, u32[]{:S(2)}, u32[]{:S(2)}) collective-permute-start(f32[3,40,128]{2,1,0:T(8,128)S(1)} %get-tuple-element.19), channel_id=1, source_target_pairs={{32,64},{64,32},{96,128},{128,96},{160,192},{192,160},{33,65},{65,... | collective-permute-start | bytes 184328 | tf_op jit(solution)/shard_map/ppermute | solution.py:431
  2.4 3.8 %collective-permute-start.1 = (f32[3,40,128]{2,1,0:T(8,128)S(1)}, f32[3,40,128]{2,1,0:T(8,128)S(1)}, u32[]{:S(2)}, u32[]{:S(2)}) collective-permute-start(f32[3,40,128]{2,1,0:T(8,128)S(1)} %get-tuple-element.20), channel_id=1, source_target_pairs={{0,32},{32,0},{64,96},{96,64},{128,160},{160,128},{192,224},{224,1... | collective-permute-start | bytes 184328 | tf_op jit(solution)/shard_map/ppermute | solution.py:432
  6.5 11.6 %collective-permute-start.2 = (f32[40,128]{1,0:T(8,128)S(1)}, f32[40,128]{1,0:T(8,128)S(1)}, u32[]{:S(2)}, u32[]{:S(2)}) collective-permute-start(f32[40,128]{1,0:T(8,128)S(1)} %get-tuple-element.24), channel_id=1, source_target_pairs={{0,31},{1,2},{2,1},{3,4},{4,3},{5,6},{6,5},{7,8},{8,7},{9,10},{10,... | collective-permute-start | bytes 61448 | tf_op jit(solution)/shard_map/ppermute | solution.py:437
  8.1 9.9 %collective-permute-start.3 = (f32[40,128]{1,0:T(8,128)S(1)}, f32[40,128]{1,0:T(8,128)S(1)}, u32[]{:S(2)}, u32[]{:S(2)}) collective-permute-start(f32[40,128]{1,0:T(8,128)S(1)} %get-tuple-element.25), channel_id=1, source_target_pairs={{0,1},{1,0},{2,3},{3,2},{4,5},{5,4},{6,7},{7,6},{8,9},{9,8},{10,11... | collective-permute-start | bytes 61448 | tf_op jit(solution)/shard_map/ppermute | solution.py:438
  18.8 1.3 %collective-permute-start.4 = (f32[32,128]{1,0:T(8,128)S(1)}, f32[32,128]{1,0:T(8,128)S(1)}, u32[]{:S(2)}, u32[]{:S(2)}) collective-permute-start(f32[32,128]{1,0:T(8,128)S(1)} %get-tuple-element.31.own_ref), channel_id=1, source_target_pairs={{0,32},{32,0},{64,96},{96,64},{128,160},{160,128},{192,224},{224,1... | collective-permute-start | bytes 49160 | tf_op jit(solution)/shard_map/ppermute | solution.py:447

commit v12 on v11

--- a/solution.py
+++ b/solution.py
@@ -302,11 +302,12 @@
                 unit = full(guess[:, 8 * g + t:8 * g + t + 1])
                 near, cross = pivot[t] * unit, line(own[t], t + 1)
                 recip[t + 1] = near * reciprocal(near * line(own[t + 1], t + 1) - cross * (cross * unit))
-            column = jnp.where(sub > t, own[t] * recip[t], 0.0)
+            column = own[t] * recip[t]
             for s in range(t + 1, 8):
                 ratio[s, t] = line(column, s)
                 own[s] = own[s] - column * line(own[t], s)
             if t < 7:
+                column = jnp.where(sub > t, column, 0.0)
                 a = a - column * line(a, t)
                 b = b - column * line(b, t)
                 for ahead in (after, later):

time: 52.6 us -> 52.6 us (level)
  no operation moved by 1% of the time
where the time goes in v12:
time: 52.6 us; the launch traced here: 52.4 us
  blocking collectives  27.1 us (52%)
  starting transfers between devices  12.9 us (25%)
  Pallas kernels  10.7 us (20%)
  waiting for transfers between devices  0.96 us (2%)
  between operations  0.71 us (1%)
    all_to_all x1, blocking collectives, body(): parts = lax.all_to_all(copies, ('x', 'y'), 0, 0)  13.9 us
    all_to_all x1, blocking collectives, body(): parts = lax.all_to_all(copies, 'z', 0, 0)  13.2 us
    ppermute x1, starting transfers between devices, body(): near = lax.ppermute(near, COL, [(i, i ^ 1) for i in range(32)])  7.18 us
    pallas_call x1, Pallas kernels, body(): call(basis, results, [pltpu.VMEM(shape, jnp.float32) for shape in results...  5.08 us
    ppermute x1, starting transfers between devices, body(): near = lax.ppermute(near, ROW, [(i, i ^ 1) for i in range(8)])  2.94 us
    pallas_call x1, Pallas kernels, body(): call(inside, ((LAT, ALL, LON), square), [wide, wide, thin, thin, thin], f...  2.71 us
    ppermute x1, starting transfers between devices, body(): lax.ppermute(far, COL, [(i, ((i + 1 ^ 1) - 1) % 32) for i in range(32)])  1.66 us
    pallas_call x1, Pallas kernels, body(): call(edge_rows, (edge, edge, (B * LAT, LON), (LAT, LON)), [small, small,...  1.14 us
  transfers between devices with their start and end apart: 5, of which 2 were waited for; matrix products, arithmetic and copies ran while one was open for 0% of the time, Pallas kernels for 7%

profile of v12, /device:TPU:8, one launch (start us, length us, event | category | flops | bytes accessed | tf_op | source)
XLA Modules:
  0.0 52.4 jit_solution(1930636406436178556)
XLA Ops:
  0.6 1.1 %shard_map.58 = (f32[3,40,128]{2,1,0:T(8,128)S(1)}, f32[3,40,128]{2,1,0:T(8,128)S(1)}, f32[1024,128]{1,0:T(8,128)S(1)}, f32[32,128]{1,0:T(8,128)S(1)}) custom-call(f32[1024,128]{1,0:T(8,128)} %bitcast.1, s32[32,128]{1,0:T(8,128)} %mask_hbm.1, s32[32,128]{1,0:T(8,128)} %depth_hbm.1), custom_call_target="tpu_custom_call" | custom-call | tf_op jit(solution)/shard_map/pallas_call | solution.py:426
  1.8 0.7 %collective-permute-start = (f32[3,40,128]{2,1,0:T(8,128)S(1)}, f32[3,40,128]{2,1,0:T(8,128)S(1)}, u32[]{:S(2)}, u32[]{:S(2)}) collective-permute-start(f32[3,40,128]{2,1,0:T(8,128)S(1)} %get-tuple-element.19), channel_id=1, source_target_pairs={{32,64},{64,32},{96,128},{128,96},{160,192},{192,160},{33,65},{65,... | collective-permute-start | bytes 184328 | tf_op jit(solution)/shard_map/ppermute | solution.py:432
  2.4 2.9 %collective-permute-start.1 = (f32[3,40,128]{2,1,0:T(8,128)S(1)}, f32[3,40,128]{2,1,0:T(8,128)S(1)}, u32[]{:S(2)}, u32[]{:S(2)}) collective-permute-start(f32[3,40,128]{2,1,0:T(8,128)S(1)} %get-tuple-element.20), channel_id=1, source_target_pairs={{0,32},{32,0},{64,96},{96,64},{128,160},{160,128},{192,224},{224,1... | collective-permute-start | bytes 184328 | tf_op jit(solution)/shard_map/ppermute | solution.py:433
  5.4 0.8 %shard_map.59 = (f32[32,40,128]{2,1,0:T(8,128)S(1)}, f32[4,40,128]{2,1,0:T(8,128)S(1)}) custom-call(f32[1024,128]{1,0:T(8,128)S(1)} %get-tuple-element.21.x_ref, f32[32,128]{1,0:T(8,128)S(1)} %get-tuple-element.22.h_ref), custom_call_target="tpu_custom_call" | custom-call | flops 4194304 | bytes 1048576 | tf_op jit(solution)/shard_map/pallas_call | solution.py:436
  6.2 0.0 collective-permute-done.far_ref
  6.2 0.1 collective-permute-done.1.near_ref
  6.3 0.2 shard_map.60
  6.5 1.7 %collective-permute-start.2 = (f32[40,128]{1,0:T(8,128)S(1)}, f32[40,128]{1,0:T(8,128)S(1)}, u32[]{:S(2)}, u32[]{:S(2)}) collective-permute-start(f32[40,128]{1,0:T(8,128)S(1)} %get-tuple-element.24), channel_id=1, source_target_pairs={{0,31},{1,2},{2,1},{3,4},{4,3},{5,6},{6,5},{7,8},{8,7},{9,10},{10,... | collective-permute-start | bytes 61448 | tf_op jit(solution)/shard_map/ppermute | solution.py:438
  8.1 7.2 %collective-permute-start.3 = (f32[40,128]{1,0:T(8,128)S(1)}, f32[40,128]{1,0:T(8,128)S(1)}, u32[]{:S(2)}, u32[]{:S(2)}) collective-permute-start(f32[40,128]{1,0:T(8,128)S(1)} %get-tuple-element.25), channel_id=1, source_target_pairs={{0,1},{1,0},{2,3},{3,2},{4,5},{5,4},{6,7},{7,6},{8,9},{9,8},{10,11... | collective-permute-start | bytes 61448 | tf_op jit(solution)/shard_map/ppermute | solution.py:439
  15.3 2.7 %shard_map.61 = (f32[32,128,128]{2,1,0:T(8,128)S(1)}, f32[128,128]{1,0:T(8,128)S(1)}) custom-call(f32[32,40,128]{2,1,0:T(8,128)S(1)} %get-tuple-element.27.core_ref, f32[3,40,128]{2,1,0:T(8,128)S(1)} %get-tuple-element.28.north_ref, f32[3,40,128]{2,1,0:T(8,128)S(1)} %get-tuple-element.29.south_ref), custom_call_target="tpu_custom_call" | custom-call | flops 268435456 | bytes 8388608 | tf_op jit(solution)/shard_map/pallas_call | solution.py:443
  18.0 0.0 collective-permute-done.2.far_ref
  18.0 0.0 collective-permute-done.3.near_ref
  18.1 0.8 %shard_map.62 = (f32[32,128]{1,0:T(8,128)S(1)}, f32[96,128]{1,0:T(8,128)S(1)}, f32[96,128]{1,0:T(8,128)S(1)}) custom-call(f32[40,128]{1,0:T(8,128)S(1)} %collective-permute-done.2.far_ref, f32[40,128]{1,0:T(8,128)S(1)} %collective-permute-done.3.near_ref, f32[4,40,128]{2,1,0:T(8,128)S(1)} %get-tuple-element.26.packed_ref, ...), custom_call_target="tpu_custom_call" | custom-call | tf_op jit(solution)/shard_map/pallas_call | solution.py:447
  18.8 0.4 collective-permute-start.4
  19.3 0.8 %collective-permute-done.4.other_ref = f32[32,128]{1,0:T(8,128)S(1)} collective-permute-done((f32[32,128]{1,0:T(8,128)S(1)}, f32[32,128]{1,0:T(8,128)S(1)}, u32[]{:S(2)}, u32[]{:S(2)}) %collective-permute-start.4) | collective-permute-done | bytes 16416 | tf_op jit(solution)/shard_map/ppermute | solution.py:448
  20.1 13.9 %all_to_all.10.parts_ref = f32[16,32,128]{2,1,0:T(8,128)S(1)} all-to-all(f32[16,32,128]{2,1,0:T(8,128)S(1)} %shard_map.63), channel_id=1, replica_groups=mesh['x'=4,'core'=2,'z'=8,'y'=4] {'x','y'}, dimensions={0} | all-to-all | bytes 524288 | tf_op jit(solution)/shard_map/all_to_all | solution.py:450
  34.1 13.2 %all_to_all.11.parts_ref = f32[8,32,128]{2,1,0:T(8,128)S(1)} all-to-all(f32[8,32,128]{2,1,0:T(8,128)S(1)} %shard_map.64), channel_id=1, replica_groups=mesh['x'=4,'core'=2,'z'=8,'y'=4] {'z'}, dimensions={0} | all-to-all | bytes 262144 | tf_op jit(solution)/shard_map/all_to_all | solution.py:452
  47.3 5.1 %shard_map.65 = (f32[128,32,128]{2,1,0:T(8,128)}, f32[3,32,32]{2,1,0:T(8,128)}, f32[3,32,32]{2,1,0:T(8,128)}) custom-call(f32[8,32,128]{2,1,0:T(8,128)S(1)} %all_to_all.11.parts_ref, f32[32,128,128]{2,1,0:T(8,128)S(1)} %get-tuple-element.32.s_ref, f32[96,128]{1,0:T(8,128)S(1)} %get-tuple-element.33.west_ref, f32[96,128]{1,0:T(8,128)S(1)} %get-tuple-element.34.east_ref), custom_call_target="tpu_custom_call" | custom-call | tf_op jit(solution)/shard_map/pallas_call | solution.py:455
  (2 shorter events, 0.0 us)
Async XLA Ops:
  1.8 4.4 %collective-permute-start = (f32[3,40,128]{2,1,0:T(8,128)S(1)}, f32[3,40,128]{2,1,0:T(8,128)S(1)}, u32[]{:S(2)}, u32[]{:S(2)}) collective-permute-start(f32[3,40,128]{2,1,0:T(8,128)S(1)} %get-tuple-element.19), channel_id=1, source_target_pairs={{32,64},{64,32},{96,128},{128,96},{160,192},{192,160},{33,65},{65,... | collective-permute-start | bytes 184328 | tf_op jit(solution)/shard_map/ppermute | solution.py:432
  2.4 3.8 %collective-permute-start.1 = (f32[3,40,128]{2,1,0:T(8,128)S(1)}, f32[3,40,128]{2,1,0:T(8,128)S(1)}, u32[]{:S(2)}, u32[]{:S(2)}) collective-permute-start(f32[3,40,128]{2,1,0:T(8,128)S(1)} %get-tuple-element.20), channel_id=1, source_target_pairs={{0,32},{32,0},{64,96},{96,64},{128,160},{160,128},{192,224},{224,1... | collective-permute-start | bytes 184328 | tf_op jit(solution)/shard_map/ppermute | solution.py:433
  6.5 11.6 %collective-permute-start.2 = (f32[40,128]{1,0:T(8,128)S(1)}, f32[40,128]{1,0:T(8,128)S(1)}, u32[]{:S(2)}, u32[]{:S(2)}) collective-permute-start(f32[40,128]{1,0:T(8,128)S(1)} %get-tuple-element.24), channel_id=1, source_target_pairs={{0,31},{1,2},{2,1},{3,4},{4,3},{5,6},{6,5},{7,8},{8,7},{9,10},{10,... | collective-permute-start | bytes 61448 | tf_op jit(solution)/shard_map/ppermute | solution.py:438
  8.1 9.9 %collective-permute-start.3 = (f32[40,128]{1,0:T(8,128)S(1)}, f32[40,128]{1,0:T(8,128)S(1)}, u32[]{:S(2)}, u32[]{:S(2)}) collective-permute-start(f32[40,128]{1,0:T(8,128)S(1)} %get-tuple-element.25), channel_id=1, source_target_pairs={{0,1},{1,0},{2,3},{3,2},{4,5},{5,4},{6,7},{7,6},{8,9},{9,8},{10,11... | collective-permute-start | bytes 61448 | tf_op jit(solution)/shard_map/ppermute | solution.py:439
  18.8 1.3 %collective-permute-start.4 = (f32[32,128]{1,0:T(8,128)S(1)}, f32[32,128]{1,0:T(8,128)S(1)}, u32[]{:S(2)}, u32[]{:S(2)}) collective-permute-start(f32[32,128]{1,0:T(8,128)S(1)} %get-tuple-element.31.own_ref), channel_id=1, source_target_pairs={{0,32},{32,0},{64,96},{96,64},{128,160},{160,128},{192,224},{224,1... | collective-permute-start | bytes 49160 | tf_op jit(solution)/shard_map/ppermute | solution.py:448
